TPU v7x, 512 devices: a whole 4x8x8 slice. The times are simulated.
512 devices in a mesh: space: 64 (over x, y, z_hi), dp: 8 (over z_lo, core).
Axes of the slice: x: 4, y: 8, z: 8 (z_hi: 2, z_lo: 4; z = z_hi * 4 + z_lo), core: 2. Of those that a mesh axis runs over, the one named last changes fastest.
Arguments:
- volume: bfloat16 [8, 128, 16, 256], P('dp', 'space'), may hold values from -6 to 6
- weight: bfloat16 [1728, 128], replicated, may hold values from -0.15625 to 0.15625
- cotangent: bfloat16 [8, 128, 16, 512], P('dp', 'space'), may hold values from -6 to 6
- left_stat: float32 [1728, 1728], P('dp'), may hold values from -27648 to 27648, as said below
- right_stat: float32 [128, 128], replicated, may hold values from -27648 to 27648, as said below
Outputs:
- output: bfloat16 [8, 128, 16, 512], P('dp', 'space')
- input_grad: bfloat16 [8, 128, 16, 256], P('dp', 'space')
- gradient: float32 [1728, 128], replicated
- direction: float32 [1728, 128], P('dp')
Inputs may be any that keep to these rules, and one draw needn't show every extreme that they name: `left_stat`: symmetric positive definite. `right_stat`: symmetric positive definite.
All inputs are finite; a program needn't handle non-finite values.
Results may differ from a plain program's by a relative error of at most 0.0049.
Values may be sent and summed in bfloat16 or wider, within the bound.
No kernel may reach another device: no remote copies, remote signals or barrier semaphores. Data moves between devices by JAX's collectives and lax.ppermute only.
A program may use at most 64 MiB of HBM per device.

v0:
```python
import math

import jax
import jax.numpy as jnp
from jax import lax
from jax.sharding import PartitionSpec as P

POWER = 4


DECAY = 0.9
EXACT_MODE = lax.Precision.HIGHEST


def extended(cells, sides, width):
    for axis, dim in sides:
        count = lax.axis_size(axis)
        head = lax.slice_in_dim(cells, 0, width, axis=dim)
        tail = lax.slice_in_dim(cells, cells.shape[dim] - width, cells.shape[dim], axis=dim)
        cells = jnp.concatenate(
            [
                lax.ppermute(tail, axis, [(i, (i + 1) % count) for i in range(count)]),
                cells,
                lax.ppermute(head, axis, [((i + 1) % count, i) for i in range(count)]),
            ],
            axis=dim,
        )
    return cells


def offset_list():
    return [(a, b, c) for a in (-1, 0, 1) for b in (-1, 0, 1) for c in (-1, 0, 1)]


def root_coefficients():
    terms_list = [(1, 5.0), (5, -5.0), (6, 4.0)]
    coeffs = [0.0] * 7
    for degree, factor in terms_list:
        for j in range(degree + 1):
            coeffs[j] += factor * math.comb(degree, j) * 1.25 ** (degree - j) * (-0.25) ** j / 4.0
    return coeffs


def top_scale(matrix):
    dimension = matrix.shape[0]
    vector = jnp.full((dimension,), 1.0 / math.sqrt(dimension), jnp.float32)
    length = jnp.float32(1.0)
    for repeat in range(POWER):
        product = jnp.dot(matrix, vector, precision=EXACT_MODE)
        length = jnp.sqrt(jnp.sum(product * product))
        vector = product / length
    return length


def small_root(matrix):
    largest = top_scale(matrix)
    unit_matrix = matrix / largest
    coeffs = root_coefficients()
    identity = jnp.eye(matrix.shape[0], dtype=jnp.float32)
    summed = coeffs[0] * identity + coeffs[1] * unit_matrix
    current = unit_matrix
    for degree in range(2, 7):
        current = jnp.dot(current, unit_matrix, precision=EXACT_MODE)
        summed = summed + coeffs[degree] * current
    return summed * largest ** (-0.25)


def gather_patches(padded, depth, channels, sign):
    leading = padded.shape[0]
    height = padded.shape[2]
    across = padded.shape[3] // channels
    pieces = []
    for a, b, c in offset_list():
        plane_block = lax.slice_in_dim(padded, 1 + sign * a, 1 + sign * a + depth, axis=1)
        plane_block = plane_block.reshape(leading, depth, height, across, channels)
        plane_block = jnp.roll(plane_block, (-sign * b, -sign * c), axis=(2, 3))
        pieces.append(plane_block)
    return jnp.concatenate(pieces, axis=4).reshape(-1, 27 * channels)


def per_device(volume, weight, cotangent, left_stat, right_stat):
    channels_in = weight.shape[0] // 27
    channels_out = weight.shape[1]
    leading, depth, height, wide = volume.shape
    across = wide // channels_in
    padded = extended(volume, (("space", 1),), 1)
    patches = gather_patches(padded, depth, channels_in, 1)
    preact = jnp.dot(patches, weight, preferred_element_type=jnp.float32)
    sigmoid_val = jax.nn.sigmoid(preact)
    output = (
        (preact * sigmoid_val)
        .astype(jnp.bfloat16)
        .reshape(leading, depth, height, across * channels_out)
    )
    upstream = cotangent.reshape(-1, channels_out).astype(jnp.float32)
    pre_grad = (upstream * sigmoid_val * (1.0 + preact * (1.0 - sigmoid_val))).astype(jnp.bfloat16)
    local_grad = lax.dot_general(
        patches, pre_grad, (((0,), (0,)), ((), ())), preferred_element_type=jnp.float32
    )
    summed_grad = lax.psum(local_grad, ("space", "dp"))
    voxels = leading * lax.axis_size("dp") * depth * lax.axis_size("space") * height * across
    gradient = summed_grad / math.sqrt(voxels)
    grad_grid = pre_grad.reshape(leading, depth, height, across * channels_out)
    grad_padded = extended(grad_grid, (("space", 1),), 1)
    back_patches = gather_patches(grad_padded, depth, channels_out, -1)
    flipped = (
        weight.reshape(27, channels_in, channels_out)
        .transpose(0, 2, 1)
        .reshape(27 * channels_out, channels_in)
    )
    input_grad = jnp.dot(back_patches, flipped, preferred_element_type=jnp.float32)
    input_grad = input_grad.astype(jnp.bfloat16).reshape(
        leading, depth, height, across * channels_in
    )
    row_count = left_stat.shape[0]
    fan_total = gradient.shape[0]
    first_row = lax.axis_index("dp") * row_count
    grad_rows = lax.dynamic_slice_in_dim(gradient, first_row, row_count, 0)
    left_rows = DECAY * left_stat + lax.dot_general(
        grad_rows, gradient, (((1,), (1,)), ((), ())), precision=EXACT_MODE
    )
    vector = jnp.full((fan_total,), 1.0 / math.sqrt(fan_total), jnp.float32)
    length = jnp.float32(1.0)
    for repeat in range(POWER):
        product = lax.all_gather(
            jnp.dot(left_rows, vector, precision=EXACT_MODE), "dp", axis=0, tiled=True
        )
        length = jnp.sqrt(jnp.sum(product * product))
        vector = product / length
    unit_rows = (left_rows / length).astype(jnp.bfloat16)
    unit_full = lax.all_gather(unit_rows, "dp", axis=0, tiled=True)
    right_full = DECAY * right_stat + lax.dot_general(
        gradient, gradient, (((0,), (0,)), ((), ())), precision=EXACT_MODE
    )
    right_root = small_root(right_full)
    carried = jnp.dot(gradient, right_root, precision=EXACT_MODE)
    coeffs = root_coefficients()
    slabs = lax.axis_size("space")
    slab_rows = (fan_total + slabs - 1) // slabs
    slab_start = lax.axis_index("space") * slab_rows
    slab_unit = lax.dynamic_slice_in_dim(unit_full, slab_start, slab_rows, 0)
    held_rows = slab_unit.shape[0]
    row_ids = lax.broadcasted_iota(jnp.int32, (held_rows, fan_total), 0) + slab_start
    col_ids = lax.broadcasted_iota(jnp.int32, (held_rows, fan_total), 1)
    identity = (row_ids == col_ids).astype(jnp.float32)
    summed = coeffs[0] * identity + coeffs[1] * slab_unit.astype(jnp.float32)
    current = slab_unit
    for degree in range(2, 7):
        current = jnp.dot(current, unit_full, preferred_element_type=jnp.float32).astype(
            jnp.bfloat16
        )
        summed = summed + coeffs[degree] * current.astype(jnp.float32)
    slab_update = jnp.dot(summed * length ** (-0.25), carried, precision=EXACT_MODE)
    joined = lax.all_gather(slab_update, "space", axis=0, tiled=True)
    update_rows = lax.dynamic_slice_in_dim(joined, first_row, row_count, 0)
    update_norm = lax.psum(jnp.sum(update_rows * update_rows), "dp")
    grad_norm = jnp.sqrt(jnp.sum(gradient * gradient))
    direction = update_rows * grad_norm / (jnp.sqrt(update_norm) + 1e-06)
    return (output, input_grad, gradient, direction)


def solution(mesh):
    placed = (P("dp", "space", None, None), P(), P("dp", "space", None, None), P("dp", None), P())
    return jax.shard_map(
        per_device,
        mesh=mesh,
        in_specs=placed,
        out_specs=(P("dp", "space", None, None), P("dp", "space", None, None), P(), P("dp", None)),
        check_vma=False,
    )
```

profile of v0, /device:TPU:1, one launch (start us, length us, event | category | flops | bytes accessed | tf_op | source)
XLA Modules:
  0.0 728.1 jit_solution(14247892414987078626)
XLA Ops:
  7.2 0.8 fusion.105
  8.0 16.6 %collective-permute-start.1 = (bf16[1,1,16,256]{3,2,1,0:T(8,128)(2,1)S(1)}, bf16[1,1,16,256]{3,2,1,0:T(8,128)(2,1)S(1)}, u32[]{:S(2)}, u32[]{:S(2)}) collective-permute-start(bf16[1,1,16,256]{3,2,1,0:T(8,128)(2,1)S(1)} %get-tuple-element.110), channel_id=1, source_target_pairs={{8,0},{16,8},{24,16},{32,24},{40,32},{48,40},{56,48},{64,56},{72,6... | collective-permute-start | bytes 24584 | tf_op jit(solution)/shard_map/ppermute | solution.py:24
  24.6 1.9 collective-permute-start
  26.5 0.8 reshape.144
  28.0 0.8 concatenate.346
  28.9 0.8 reshape.153
  30.0 1.3 dynamic-slice
  31.9 5.2 collective-permute-done
  39.0 0.5 concatenate.373
  40.1 1.2 fusion.106
  41.3 1.9 collective-permute-start.3
  43.2 11.5 %collective-permute-start.2 = (bf16[1,1,16,512]{3,2,1,0:T(8,128)(2,1)S(1)}, bf16[1,1,16,512]{3,2,1,0:T(8,128)(2,1)S(1)}, u32[]{:S(2)}, u32[]{:S(2)}) collective-permute-start(bf16[1,1,16,512]{3,2,1,0:T(8,128)(2,1)S(1)} %get-tuple-element.27), channel_id=1, source_target_pairs={{8,0},{16,8},{24,16},{32,24},{40,32},{48,40},{56,48},{64,56},{72,6... | collective-permute-start | bytes 49160 | tf_op jit(solution)/shard_map/ppermute | solution.py:24
  55.0 265.3 %all-reduce.6.cloned.1.call-done = f32[1728,128]{1,0:T(8,128)} async-done(((f32[1728,128]{1,0:T(8,128)}), f32[1728,128]{1,0:T(8,128)}) %all-reduce.6.cloned.1.call-update) | async-done | bytes 884752 | tf_op jit(solution)/shard_map/psum | solution.py:100
  320.3 2.0 multiply_reduce_fusion
  322.3 3.1 convolution_add_fusion
  325.4 1.3 fusion.60
  327.0 13.6 %all-reduce = f32[1728]{0:T(1024)S(1)} all-reduce(f32[1728]{0:T(1024)S(1)} %dynamic-update-slice), channel_id=1, replica_groups=mesh['space'=64,'dp'=8] {'dp'}, use_global_device_ids=true, to_apply=%add | all-reduce | flops 1728 | bytes 13824
  340.6 0.6 multiply_reduce_fusion.5
  342.0 1.3 fusion.107
  343.5 16.7 %all-reduce.1 = f32[1728]{0:T(1024)S(1)} all-reduce(f32[1728]{0:T(1024)S(1)} %dynamic-update-slice.1), channel_id=1, replica_groups=mesh['space'=64,'dp'=8] {'dp'}, use_global_device_ids=true, to_apply=%add.1 | all-reduce | flops 1728 | bytes 13824
  360.2 0.6 multiply_reduce_fusion.4
  361.5 1.3 fusion.108
  363.1 14.0 %all-reduce.2 = f32[1728]{0:T(1024)S(1)} all-reduce(f32[1728]{0:T(1024)S(1)} %dynamic-update-slice.2), channel_id=1, replica_groups=mesh['space'=64,'dp'=8] {'dp'}, use_global_device_ids=true, to_apply=%add.2 | all-reduce | flops 1728 | bytes 13824
  377.1 0.6 multiply_reduce_fusion.3
  378.4 1.3 fusion.109
  380.0 14.0 %all-reduce.3 = f32[1728]{0:T(1024)S(1)} all-reduce(f32[1728]{0:T(1024)S(1)} %dynamic-update-slice.3), channel_id=1, replica_groups=mesh['space'=64,'dp'=8] {'dp'}, use_global_device_ids=true, to_apply=%add.3 | all-reduce | flops 1728 | bytes 13824
  393.9 0.6 multiply_reduce_fusion.2
  395.2 1.0 divide_convert_fusion
  396.5 0.6 reshape.146
  399.7 0.7 reshape.152
  400.5 1.6 convolution_add_fusion.1
  402.2 0.9 multiply_reduce_fusion.8
  403.8 0.9 multiply_reduce_fusion.7
  405.4 0.9 multiply_reduce_fusion.6
  407.0 0.9 fusion.7
  409.7 0.8 fusion.110
  410.6 54.7 %all-gather.3.cloned.1.call-done = bf16[1728,1728]{1,0:T(8,128)(2,1)} async-done(((bf16[216,1728]{1,0:T(8,128)(2,1)}), bf16[1728,1728]{1,0:T(8,128)(2,1)}) %all-gather.3.cloned.1.call-update) | async-done | bytes 5971984 | tf_op jit(solution)/shard_map/all_gather | solution.py:131
  465.3 4.0 convolution_convert_fusion.4
  469.3 0.6 copy-done
  469.9 1.0 convolution_convert_fusion.3
  470.9 1.1 convolution_convert_fusion.2
  472.0 1.1 convolution_convert_fusion.1
  473.1 1.1 fusion.3
  474.2 0.6 convolution_bitcast_fusion
  474.8 201.9 %all-gather = f32[64,27,128]{2,1,0:T(8,128)S(1)} all-gather(f32[1,27,128]{2,1,0:T(8,128)S(1)} %convolution_bitcast_fusion), channel_id=1, replica_groups=mesh['space'=64,'dp'=8] {'space'}, dimensions={0}, use_global_device_ids=true | all-gather | bytes 898560 | tf_op jit(solution)/shard_map/all_gather | solution.py:154
  676.7 0.6 multiply_reduce_fusion.1
  678.0 41.8 %psum.15 = f32[]{:T(128)} all-reduce(f32[]{:T(128)} %multiply_reduce_fusion.1), channel_id=1, replica_groups=mesh['space'=64,'dp'=8] {'dp'}, use_global_device_ids=true, to_apply=%region_11.12 | all-reduce | flops 1 | bytes 8 | tf_op jit(solution)/shard_map/psum | solution.py:156
  720.6 0.7 multiply_divide_fusion
  (164 shorter events, 8.0 us)
Async XLA Ops:
  7.2 30.0 %copy-start.3 = (bf16[1,2,16,256]{3,2,1,0:T(8,128)(2,1)S(1)}, bf16[1,2,16,256]{3,2,1,0:T(8,128)(2,1)}, u32[]{:S(2)}) copy-start(bf16[1,2,16,256]{3,2,1,0:T(8,128)(2,1)} %param.5) | copy-start | bytes 49156
  7.2 22.5 %copy-start.2 = (bf16[1728,128]{1,0:T(8,128)(2,1)S(1)}, bf16[1728,128]{1,0:T(8,128)(2,1)}, u32[]{:S(2)}) copy-start(bf16[1728,128]{1,0:T(8,128)(2,1)} %param.6) | copy-start | bytes 1327108
  7.2 313.1 %all-reduce.6.cloned.1.call-start = ((), (), s32[]{:S(2)}) async-start(), calls=%async_computation | async-start | bytes 1769472 | tf_op jit(solution)/shard_map/psum | solution.py:100
  8.0 23.9 %collective-permute-start.1 = (bf16[1,1,16,256]{3,2,1,0:T(8,128)(2,1)S(1)}, bf16[1,1,16,256]{3,2,1,0:T(8,128)(2,1)S(1)}, u32[]{:S(2)}, u32[]{:S(2)}) collective-permute-start(bf16[1,1,16,256]{3,2,1,0:T(8,128)(2,1)S(1)} %get-tuple-element.110), channel_id=1, source_target_pairs={{8,0},{16,8},{24,16},{32,24},{40,32},{48,40},{56,48},{64,56},{72,6... | collective-permute-start | bytes 24584 | tf_op jit(solution)/shard_map/ppermute | solution.py:24
  24.6 12.6 %collective-permute-start = (bf16[1,1,16,256]{3,2,1,0:T(8,128)(2,1)S(1)}, bf16[1,1,16,256]{3,2,1,0:T(8,128)(2,1)S(1)}, u32[]{:S(2)}, u32[]{:S(2)}) collective-permute-start(bf16[1,1,16,256]{3,2,1,0:T(8,128)(2,1)S(1)} %get-tuple-element.111), channel_id=1, source_target_pairs={{0,8},{8,16},{16,24},{24,32},{32,40},{40,48},{48,56},{56,64},{64,7... | collective-permute-start | bytes 24584 | tf_op jit(solution)/shard_map/ppermute | solution.py:22
  41.3 355.8 %collective-permute-start.3 = (bf16[1,1,16,512]{3,2,1,0:T(8,128)(2,1)S(1)}, bf16[1,1,16,512]{3,2,1,0:T(8,128)(2,1)S(1)}, u32[]{:S(2)}, u32[]{:S(2)}) collective-permute-start(bf16[1,1,16,512]{3,2,1,0:T(8,128)(2,1)S(1)} %get-tuple-element.26), channel_id=1, source_target_pairs={{0,8},{8,16},{16,24},{24,32},{32,40},{40,48},{48,56},{56,64},{64,7... | collective-permute-start | bytes 49160 | tf_op jit(solution)/shard_map/ppermute | solution.py:22
  43.2 353.9 %collective-permute-start.2 = (bf16[1,1,16,512]{3,2,1,0:T(8,128)(2,1)S(1)}, bf16[1,1,16,512]{3,2,1,0:T(8,128)(2,1)S(1)}, u32[]{:S(2)}, u32[]{:S(2)}) collective-permute-start(bf16[1,1,16,512]{3,2,1,0:T(8,128)(2,1)S(1)} %get-tuple-element.27), channel_id=1, source_target_pairs={{8,0},{16,8},{24,16},{32,24},{40,32},{48,40},{56,48},{64,56},{72,6... | collective-permute-start | bytes 49160 | tf_op jit(solution)/shard_map/ppermute | solution.py:24
  54.8 410.5 %all-gather.3.cloned.1.call-start = ((), (), s32[]{:S(2)}) async-start(), calls=%async_computation.1 | async-start | bytes 6967296 | tf_op jit(solution)/shard_map/all_gather | solution.py:131
  322.3 87.4 %copy-start.1 = (f32[1728,128]{1,0:T(8,128)}, f32[1728,128]{1,0:T(8,128)S(1)}, u32[]{:S(2)}) copy-start(f32[1728,128]{1,0:T(8,128)S(1)} %get-tuple-element.5) | copy-start | bytes 2654212
  398.5 2.0 copy-start.4
  465.3 4.6 copy-start
Sparse Core Ops, SparseCore 0:
  54.9 265.3 all-reduce.5
  396.4 68.8 all-gather.2
where the time goes:
time: 729 us; the launch traced here: 728 us
  waiting for transfers between devices  325 us (45%)
  blocking collectives  302 us (41%)
  starting transfers between devices  32 us (4%)
  matrix products  26.2 us (4%)
  between operations  22.9 us (3%)
  other arithmetic  9.91 us (1%)
  local copies, waits for them, and re-layouts  9.76 us (1%)
    psum x1, waiting for transfers between devices, per_device(): summed_grad = lax.psum(local_grad, ('space', 'dp'))  265 us
    all_gather x1, blocking collectives, per_device(): joined = lax.all_gather(slab_update, 'space', axis=0, tiled=True)  202 us
    unnamed x4, blocking collectives  58.3 us
    all_gather x1, waiting for transfers between devices, per_device(): unit_full = lax.all_gather(unit_rows, 'dp', axis=0, tiled=True)  54.7 us
    psum x1, blocking collectives, per_device(): update_norm = lax.psum(jnp.sum(update_rows * update_rows), 'dp')  41.8 us
    ppermute x2, starting transfers between devices, extended(): lax.ppermute(head, axis, [((i + 1) % count, i) for i in range(count)])  28 us
  transfers between devices with their start and end apart: 6, of which 3 were waited for; matrix products, arithmetic and copies ran while one was open for 4% of the time, Pallas kernels for 0%

commit v1 on v0

v1 whole, which is shorter than its diff:
```python
import math

import jax
import jax.numpy as jnp
from jax import lax
from jax.sharding import PartitionSpec as P

POWER = 4
DEGREE = 6


DECAY = 0.9
EXACT_MODE = lax.Precision.HIGHEST
EVERY = ("space", "dp")


def offset_list():
    return [(a, b, c) for a in (-1, 0, 1) for b in (-1, 0, 1) for c in (-1, 0, 1)]


def root_coefficients():
    terms_list = [(1, 5.0), (5, -5.0), (6, 4.0)]
    coeffs = [0.0] * 7
    for degree, factor in terms_list:
        for j in range(degree + 1):
            coeffs[j] += factor * math.comb(degree, j) * 1.25 ** (degree - j) * (-0.25) ** j / 4.0
    return coeffs


def top_scale(matrix):
    dimension = matrix.shape[0]
    vector = jnp.full((dimension,), 1.0 / math.sqrt(dimension), jnp.float32)
    length = jnp.float32(1.0)
    for repeat in range(POWER):
        product = jnp.dot(matrix, vector, precision=EXACT_MODE)
        length = jnp.sqrt(jnp.sum(product * product))
        vector = product / length
    return length


def small_root(matrix):
    largest = top_scale(matrix)
    unit_matrix = matrix / largest
    coeffs = root_coefficients()
    identity = jnp.eye(matrix.shape[0], dtype=jnp.float32)
    summed = coeffs[0] * identity + coeffs[1] * unit_matrix
    current = unit_matrix
    for degree in range(2, 7):
        current = jnp.dot(current, unit_matrix, precision=EXACT_MODE)
        summed = summed + coeffs[degree] * current
    return summed * largest ** (-0.25)


def gather_patches(padded, depth, channels, sign):
    leading = padded.shape[0]
    height = padded.shape[2]
    across = padded.shape[3] // channels
    pieces = []
    for a, b, c in offset_list():
        plane_block = lax.slice_in_dim(padded, 1 + sign * a, 1 + sign * a + depth, axis=1)
        plane_block = plane_block.reshape(leading, depth, height, across, channels)
        plane_block = jnp.roll(plane_block, (-sign * b, -sign * c), axis=(2, 3))
        pieces.append(plane_block)
    return jnp.concatenate(pieces, axis=4).reshape(-1, 27 * channels)


def with_neighbours(volume, cotangent):
    count = lax.axis_size("space")
    onward = [(i, (i + 1) % count) for i in range(count)]
    back = [((i + 1) % count, i) for i in range(count)]
    wide = cotangent.shape[3]
    packed = volume.reshape(1, 1, -1, wide)
    before = lax.ppermute(jnp.concatenate([packed, cotangent[:, 1:]], axis=2), "space", onward)
    after = lax.ppermute(jnp.concatenate([packed, cotangent[:, :1]], axis=2), "space", back)
    held = packed.shape[2]
    volumes = [before[:, :, :held].reshape(volume.shape), volume, after[:, :, :held].reshape(volume.shape)]
    cotangents = [before[:, :, held:], cotangent, after[:, :, held:]]
    return jnp.concatenate(volumes, axis=1), jnp.concatenate(cotangents, axis=1)


def summed_everywhere(local):
    devices = lax.axis_size(EVERY)
    rows, width = local.shape
    piece = 4 * ((rows + 4 * devices - 1) // (4 * devices))
    sent = jnp.pad(local.astype(jnp.bfloat16), ((0, piece * devices - rows), (0, 0)))
    terms = lax.all_to_all(sent.reshape(devices, piece, width), EVERY, 0, 0)
    total = jnp.sum(terms.astype(jnp.float32), axis=0).astype(jnp.bfloat16)
    spread = jnp.broadcast_to(total[None], (devices, piece, width))
    joined = lax.all_to_all(spread, EVERY, 0, 0)
    return joined.reshape(devices * piece, width)[:rows]


def per_device(volume, weight, cotangent, left_stat, right_stat):
    channels_in = weight.shape[0] // 27
    channels_out = weight.shape[1]
    leading, depth, height, wide = volume.shape
    across = wide // channels_in
    left_all = lax.all_gather(left_stat.astype(jnp.bfloat16), "dp", axis=0, tiled=True)
    volumes, cotangents = with_neighbours(volume, cotangent)
    patches = gather_patches(volumes, depth + 2, channels_in, 1)
    preact = jnp.dot(patches, weight, preferred_element_type=jnp.float32)
    sigmoid_val = jax.nn.sigmoid(preact)
    cells = (leading, depth + 2, height, across * channels_out)
    output = (preact * sigmoid_val).astype(jnp.bfloat16).reshape(cells)[:, 1:-1]
    upstream = cotangents.reshape(-1, channels_out).astype(jnp.float32)
    pre_grad = (upstream * sigmoid_val * (1.0 + preact * (1.0 - sigmoid_val))).astype(jnp.bfloat16)
    grad_padded = pre_grad.reshape(cells)
    plane = height * across
    local_grad = lax.dot_general(
        patches[plane:-plane],
        pre_grad[plane:-plane],
        (((0,), (0,)), ((), ())),
        preferred_element_type=jnp.float32,
    )
    voxels = leading * lax.axis_size("dp") * depth * lax.axis_size("space") * height * across
    rounded = summed_everywhere(local_grad / math.sqrt(voxels))
    gradient = rounded.astype(jnp.float32)
    back_patches = gather_patches(grad_padded, depth, channels_out, -1)
    flipped = (
        weight.reshape(27, channels_in, channels_out)
        .transpose(0, 2, 1)
        .reshape(27 * channels_out, channels_in)
    )
    input_grad = jnp.dot(back_patches, flipped, preferred_element_type=jnp.float32)
    input_grad = input_grad.astype(jnp.bfloat16).reshape(
        leading, depth, height, across * channels_in
    )
    row_count = left_stat.shape[0]
    fan_total = gradient.shape[0]
    first_row = lax.axis_index("dp") * row_count
    right_full = DECAY * right_stat + lax.dot_general(
        rounded, rounded, (((0,), (0,)), ((), ())), preferred_element_type=jnp.float32
    )
    right_root = small_root(right_full)
    carried = jnp.dot(gradient, right_root, precision=EXACT_MODE)
    left_full = DECAY * left_all.astype(jnp.float32) + lax.dot_general(
        rounded, rounded, (((1,), (1,)), ((), ())), preferred_element_type=jnp.float32
    )
    row_ids = lax.broadcasted_iota(jnp.int32, (fan_total, fan_total), 0)
    col_ids = lax.broadcasted_iota(jnp.int32, (fan_total, fan_total), 1)
    trace = jnp.sum(jnp.where(row_ids == col_ids, left_full, 0.0))
    scaled = (left_full / trace).astype(jnp.bfloat16)
    start = jnp.full((fan_total, 128), 1.0 / math.sqrt(fan_total), jnp.float32)
    block = jnp.concatenate([carried, start], axis=1)
    powers, lengths = [carried], []
    for degree in range(1, DEGREE + 1):
        block = jnp.dot(scaled, block.astype(jnp.bfloat16), preferred_element_type=jnp.float32)
        powers.append(block[:, :channels_out])
        lengths.append(jnp.sqrt(jnp.sum(block[:, channels_out] * block[:, channels_out])))
    share = lengths[POWER - 1] / lengths[POWER - 2]
    coeffs = root_coefficients()
    update = coeffs[0] * powers[0]
    factor = jnp.float32(1.0)
    for degree in range(1, DEGREE + 1):
        factor = factor / share
        update = update + (coeffs[degree] * factor) * powers[degree]
    update = update * (share * trace) ** (-0.25)
    update_norm = jnp.sqrt(jnp.sum(update * update))
    grad_norm = jnp.sqrt(jnp.sum(gradient * gradient))
    update_rows = lax.dynamic_slice_in_dim(update, first_row, row_count, 0)
    direction = update_rows * grad_norm / (update_norm + 1e-06)
    return (output, input_grad, gradient, direction)


def solution(mesh):
    placed = (P("dp", "space", None, None), P(), P("dp", "space", None, None), P("dp", None), P())
    return jax.shard_map(
        per_device,
        mesh=mesh,
        in_specs=placed,
        out_specs=(P("dp", "space", None, None), P("dp", "space", None, None), P(), P("dp", None)),
        check_vma=False,
    )
```

time: 729 us -> 191 us (0.26)
  blocking collectives: 302 us -> 0 us
  waiting for transfers between devices: 325 us -> 29 us
  other arithmetic: 9.91 us -> 32.7 us
  local copies, waits for them, and re-layouts: 9.76 us -> 29 us
  starting transfers between devices: 32 us -> 42.7 us
  matrix products: 26.2 us -> 34.6 us
    psum x1 -> x0, waiting for transfers between devices: 265 us -> none  [per_device(): summed_grad = lax.psum(local_grad, ('space', 'dp'))]
    all_gather x1 -> x0, blocking collectives: 202 us -> none  [per_device(): joined = lax.all_gather(slab_update, 'space', axis=0, tiled=True)]
    unnamed x4 -> x0, blocking collectives: 58.3 us -> none
    all_gather x1, waiting for transfers between devices: 54.7 us -> 0.01 us  [per_device(): lax.all_gather(left_stat.astype(jnp.bfloat16), 'dp', axis=0, tiled=True)]
    psum x1 -> x0, blocking collectives: 41.8 us -> none  [per_device(): update_norm = lax.psum(jnp.sum(update_rows * update_rows), 'dp')]
    all_to_all x0 -> x2, waiting for transfers between devices: none -> 29 us  [the longest x1 20.3 us: summed_everywhere(): joined = lax.all_to_all(spread, EVERY, 0, 0)]
    all_to_all x0 -> x2, starting transfers between devices: none -> 24.2 us  [the longest x1 13.4 us: summed_everywhere(): terms = lax.all_to_all(sent.reshape(devices, piece, width), EVERY, 0, 0)]
    concatenate x60, other arithmetic: 3.16 us -> 17.6 us  [gather_patches(): plane_block = jnp.roll(plane_block, (-sign * b, -sign * c), axis=(2, 3))]
  transfers between devices with their start and end apart: 6 -> 5, of which waited for: 3 -> 2; matrix products, arithmetic and copies ran while one was open for 4% -> 30% of each run, Pallas kernels for 0% -> 0%
where the time goes in v1:
time: 191 us; the launch traced here: 190 us
  starting transfers between devices  42.7 us (22%)
  matrix products  34.6 us (18%)
  other arithmetic  32.7 us (17%)
  local copies, waits for them, and re-layouts  29 us (15%)
  waiting for transfers between devices  29 us (15%)
  between operations  21.7 us (11%)
    all_to_all x1, waiting for transfers between devices, summed_everywhere(): joined = lax.all_to_all(spread, EVERY, 0, 0)  20.3 us
    concatenate x60, other arithmetic, gather_patches(): plane_block = jnp.roll(plane_block, (-sign * b, -sign * c), axis=(2, 3))  17.6 us
    dot_general x6, matrix products, per_device(): jnp.dot(scaled, block.astype(jnp.bfloat16), preferred_element_type=jnp.fl...  17.3 us
    concatenate x9, local copies, waits for them, and re-layouts, gather_patches(): return jnp.concatenate(pieces, axis=4).reshape(-1, 27 * channels)  14.6 us
    all_to_all x1, starting transfers between devices, summed_everywhere(): terms = lax.all_to_all(sent.reshape(devices, piece, width), EVERY, 0, 0)  13.4 us
    ppermute x1, starting transfers between devices, with_neighbours(): lax.ppermute(jnp.concatenate([packed, cotangent[:, 1:]], axis=2), 'space'...  11.5 us
    all_to_all x1, starting transfers between devices, summed_everywhere(): joined = lax.all_to_all(spread, EVERY, 0, 0)  10.7 us
    dot_general x1, matrix products, per_device(): lax.dot_general(rounded, rounded, (((1,), (1,)), ((), ())), preferred_ele...  8.67 us
  transfers between devices with their start and end apart: 5, of which 2 were waited for; matrix products, arithmetic and copies ran while one was open for 30% of the time, Pallas kernels for 0%

profile of v1, /device:TPU:1, one launch (start us, length us, event | category | flops | bytes accessed | tf_op | source)
XLA Modules:
  0.0 189.7 jit_solution(6279248984849966653)
XLA Ops:
  8.7 11.5 %collective-permute-start = (bf16[1,1,32,512]{3,2,1,0:T(8,128)(2,1)S(1)}, bf16[1,1,32,512]{3,2,1,0:T(8,128)(2,1)S(1)}, u32[]{:S(2)}, u32[]{:S(2)}) collective-permute-start(bf16[1,1,32,512]{3,2,1,0:T(8,128)(2,1)S(1)} %get-tuple-element.117), channel_id=1, source_target_pairs={{0,8},{8,16},{16,24},{24,32},{32,40},{40,48},{48,56},{56,64},{64,7... | collective-permute-start | bytes 98312 | tf_op jit(solution)/shard_map/ppermute | solution.py:73
  20.2 7.0 %collective-permute-start.1 = (bf16[1,1,32,512]{3,2,1,0:T(8,128)(2,1)S(1)}, bf16[1,1,32,512]{3,2,1,0:T(8,128)(2,1)S(1)}, u32[]{:S(2)}, u32[]{:S(2)}) collective-permute-start(bf16[1,1,32,512]{3,2,1,0:T(8,128)(2,1)S(1)} %get-tuple-element.116), channel_id=1, source_target_pairs={{8,0},{16,8},{24,16},{32,24},{40,32},{48,40},{56,48},{64,56},{72,6... | collective-permute-start | bytes 98312 | tf_op jit(solution)/shard_map/ppermute | solution.py:74
  27.2 2.4 %convert_element_type.61 = bf16[216,1728]{1,0:T(8,128)(2,1)} convert(f32[216,1728]{1,0:T(8,128)} %param.8) | non-fusion elementwise | flops 373248 | bytes 2239488 | tf_op jit(solution)/shard_map/convert_element_type | solution.py:98
  29.6 0.8 concatenate.345
  30.5 1.4 copy.12
  36.2 0.8 pad_maximum_fusion.4
  40.2 3.9 %concatenate.404 = bf16[256,1728]{1,0:T(8,128)(2,1)S(1)} concatenate(bf16[256,64]{1,0:T(8,128)(2,1)S(1)} %bitcast.154, bf16[256,64]{1,0:T(8,128)(2,1)S(1)} %bitcast.166, bf16[256,64]{1,0:T(8,128)(2,1)S(1)} %bitcast.155, bf16[256,64]{1,0:T(8,128)(2,1)S(1)} %bitcast.148, bf16[256,64]{1,0:T(8,128)(2,1)} %concatenate.356, bf16[256,64]{1,0:T(8,128)(2,1)S(1)} %bitcast.149, ...), dimensions={1} | concatenate | bytes 1769472 | tf_op jit(solution)/shard_map/concatenate | solution.py:64
  44.1 1.0 fusion.122
  45.2 1.6 multiply_convert_fusion
  52.2 7.0 %concatenate.458 = bf16[1,4,16,4,1728]{4,3,2,1,0:T(4,128)(2,1)S(1)} concatenate(bf16[1,4,16,4,64]{4,3,2,1,0:T(4,128)(2,1)S(1)} %pad_maximum_fusion.6, bf16[1,4,16,4,64]{4,3,2,1,0:T(4,128)(2,1)S(1)} %get-tuple-element.130, bf16[1,4,16,4,64]{4,3,2,1,0:T(4,128)(2,1)S(1)} %pad_maximum_fusion.7, bf16[1,4,16,4,64]{4,3,2,1,0:T(4,128)(2,1)S(1)} %get-tuple-element.136, ...), dimensions={4} | concatenate | bytes 1769472 | tf_op jit(solution)/shard_map/concatenate | solution.py:64
  59.7 1.1 fusion.2
  60.8 0.8 pad.6
  61.6 13.4 %all-to-all-start = ((bf16[512,4,128]{2,1,0:T(4,128)(2,1)}), bf16[512,4,128]{2,1,0:T(4,128)(2,1)S(1)}, u32[]{:S(2)}, u32[]{:S(2)}) async-start(bf16[512,4,128]{2,1,0:T(4,128)(2,1)} %bitcast.50), calls=%async_computation | async-start | bytes 1048576 | tf_op jit(solution)/shard_map/all_to_all | solution.py:86
  75.1 0.8 fusion.70
  75.9 0.8 concatenate.431
  77.6 0.9 fusion.51
  78.5 0.8 pad_maximum_fusion.36
  79.3 0.8 constant_dynamic-update-slice_fusion.29
  81.1 0.8 fusion.49
  81.9 0.8 pad_maximum_fusion.40
  82.7 0.8 pad_maximum_fusion.41
  83.5 0.8 fusion.47
  84.3 0.8 pad_maximum_fusion.42
  85.6 0.8 fusion.43
  86.6 0.9 reshape.178
  88.3 8.6 %all-to-all-done = bf16[512,4,128]{2,1,0:T(4,128)(2,1)S(1)} async-done(((bf16[512,4,128]{2,1,0:T(4,128)(2,1)}), bf16[512,4,128]{2,1,0:T(4,128)(2,1)S(1)}, u32[]{:S(2)}, u32[]{:S(2)}) %all-to-all-start) | async-done | bytes 524320 | tf_op jit(solution)/shard_map/all_to_all | solution.py:86
  97.5 0.9 broadcast_in_dim.14
  98.4 10.7 %all-to-all-start.1 = ((bf16[512,4,128]{2,1,0:T(4,128)(2,1)}), bf16[512,4,128]{2,1,0:T(4,128)(2,1)S(1)}, u32[]{:S(2)}, u32[]{:S(2)}) async-start(bf16[512,4,128]{2,1,0:T(4,128)(2,1)} %broadcast_in_dim.14), calls=%async_computation.1 | async-start | bytes 1048576 | tf_op jit(solution)/shard_map/all_to_all | solution.py:89
  110.7 20.3 %all-to-all-done.1 = bf16[512,4,128]{2,1,0:T(4,128)(2,1)S(1)} async-done(((bf16[512,4,128]{2,1,0:T(4,128)(2,1)}), bf16[512,4,128]{2,1,0:T(4,128)(2,1)S(1)}, u32[]{:S(2)}, u32[]{:S(2)}) %all-to-all-start.1) | async-done | bytes 524320 | tf_op jit(solution)/shard_map/all_to_all | solution.py:89
  131.2 1.0 convert_element_type.60
  132.5 0.8 multiply_reduce_fusion.4
  134.0 0.8 multiply_reduce_fusion.3
  135.5 0.8 multiply_reduce_fusion.2
  137.0 0.8 fusion.24
  138.5 0.8 multiply_reduce_fusion.1
  141.2 1.4 fusion.121
  142.6 8.7 %select_reduce_fusion = (f32[]{:T(128)}, f32[1728,1728]{1,0:T(8,128)}) fusion(bf16[1728,128]{1,0:T(8,128)(2,1)S(1)} %bitcast.145, bf16[1728,1728]{1,0:T(8,128)(2,1)} %all-gather.2.cloned.1.call-done), kind=kOutput, calls=%fused_computation.1 | convolution fusion | flops 782327808 | bytes 18358276 | tf_op jit(solution)/shard_map/dot_general | solution.py:136
  151.3 6.1 %divide_convert_fusion = bf16[1728,1728]{1,0:T(8,128)(2,1)S(1)} fusion(f32[1728,1728]{1,0:T(8,128)} %get-tuple-element.119, f32[]{:T(128)} %get-tuple-element.118), kind=kLoop, calls=%fused_computation | loop fusion | flops 5971968 | bytes 17915908 | tf_op jit(solution)/shard_map/convert_element_type | solution.py:142
  157.4 1.8 fusion.22
  159.3 1.3 copy-done.4
  160.6 1.8 fusion.20
  162.4 1.2 copy-done.5
  163.6 1.8 fusion.18
  165.5 1.8 fusion.16
  167.3 1.1 fusion.12
  168.4 0.8 fusion.13
  169.2 3.1 %fusion.14 = f32[1728,256]{1,0:T(8,128)} fusion(bf16[1728,1728]{1,0:T(8,128)(2,1)S(1)} %divide_convert_fusion, f32[1728,256]{1,0:T(8,128)S(1)} %fusion.16), kind=kOutput, calls=%fused_computation.35 | convolution fusion | flops 1529266176 | bytes 9510912 | tf_op jit(solution)/shard_map/dot_general | solution.py:147
  174.5 6.9 %multiply_reduce_fusion = (f32[]{:T(128)}, f32[1728,128]{1,0:T(8,128)S(1)}) fusion(f32[]{:T(128)S(6)} %pow.7, bf16[1728,1728]{1,0:T(8,128)(2,1)} %copy-done, f32[1728,256]{1,0:T(8,128)} %fusion.14, f32[]{:T(128)S(6)} %mul.224, f32[]{:T(128)S(6)} %mul.221, f32[1728,256]{1,0:T(8,128)} %copy-done.2, f32[]{:T(128)S(6)} %mul.218, f32[1728,256]{1,0:T(8,128)} %copy-done.1, ...), kind=kOutput, calls=%fused_computation.33 | convolution fusion | flops 768172032 | bytes 13049888 | tf_op jit(solution)/shard_map/dot_general | solution.py:147
  (204 shorter events, 22.0 us)
Async XLA Ops:
  7.2 26.2 %copy-start.16 = (bf16[1,2,16,256]{3,2,1,0:T(8,128)(2,1)S(1)}, bf16[1,2,16,256]{3,2,1,0:T(8,128)(2,1)}, u32[]{:S(2)}) copy-start(bf16[1,2,16,256]{3,2,1,0:T(8,128)(2,1)} %param.5) | copy-start | bytes 49156
  7.2 135.5 %all-gather.2.cloned.1.call-start = ((), (), s32[]{:S(2)}) async-start(), calls=%async_computation.2 | async-start | bytes 6967296 | tf_op jit(solution)/shard_map/all_gather | solution.py:98
  8.7 23.1 %collective-permute-start = (bf16[1,1,32,512]{3,2,1,0:T(8,128)(2,1)S(1)}, bf16[1,1,32,512]{3,2,1,0:T(8,128)(2,1)S(1)}, u32[]{:S(2)}, u32[]{:S(2)}) collective-permute-start(bf16[1,1,32,512]{3,2,1,0:T(8,128)(2,1)S(1)} %get-tuple-element.117), channel_id=1, source_target_pairs={{0,8},{8,16},{16,24},{24,32},{32,40},{40,48},{48,56},{56,64},{64,7... | collective-permute-start | bytes 98312 | tf_op jit(solution)/shard_map/ppermute | solution.py:73
  20.2 12.6 %collective-permute-start.1 = (bf16[1,1,32,512]{3,2,1,0:T(8,128)(2,1)S(1)}, bf16[1,1,32,512]{3,2,1,0:T(8,128)(2,1)S(1)}, u32[]{:S(2)}, u32[]{:S(2)}) collective-permute-start(bf16[1,1,32,512]{3,2,1,0:T(8,128)(2,1)S(1)} %get-tuple-element.116), channel_id=1, source_target_pairs={{8,0},{16,8},{24,16},{32,24},{40,32},{48,40},{56,48},{64,56},{72,6... | collective-permute-start | bytes 98312 | tf_op jit(solution)/shard_map/ppermute | solution.py:74
  30.5 13.7 %copy-start.3 = (bf16[1728,128]{1,0:T(8,128)(2,1)S(1)}, bf16[1728,128]{1,0:T(8,128)(2,1)}, u32[]{:S(2)}) copy-start(bf16[1728,128]{1,0:T(8,128)(2,1)} %param.6) | copy-start | bytes 1327108
  32.1 13.1 %copy-start.20 = (bf16[1,2,16,512]{3,2,1,0:T(8,128)(2,1)S(1)}, bf16[1,2,16,512]{3,2,1,0:T(8,128)(2,1)}, u32[]{:S(2)}) copy-start(bf16[1,2,16,512]{3,2,1,0:T(8,128)(2,1)} %param.7) | copy-start | bytes 98308
  34.7 15.5 %copy-start.6 = (bf16[1,4,16,4,64]{4,3,2,1,0:T(4,128)(2,1)}, bf16[1,4,16,4,64]{4,3,2,1,0:T(4,128)(2,1)S(1)}, u32[]{:S(2)}) copy-start(bf16[1,4,16,4,64]{4,3,2,1,0:T(4,128)(2,1)S(1)} %get-tuple-element.138) | copy-start | bytes 98308
  34.7 10.5 %copy-start.21 = (bf16[1,1,16,512]{3,2,1,0:T(8,128)(2,1)S(1)}, bf16[1,1,16,512]{3,2,1,0:T(8,128)(2,1)}, u32[]{:S(2)}) copy-start(bf16[1,1,16,512]{3,2,1,0:T(8,128)(2,1)} %get-tuple-element.107) | copy-start | bytes 49156
  46.8 4.7 %copy-start.12 = (bf16[256,128]{1,0:T(8,128)(2,1)}, bf16[256,128]{1,0:T(8,128)(2,1)S(1)}, u32[]{:S(2)}) copy-start(bf16[256,128]{1,0:T(8,128)(2,1)S(1)} %get-tuple-element.4) | copy-start | bytes 196612
  46.9 4.6 %copy-start.15 = (bf16[1,2,16,512]{3,2,1,0:T(8,128)(2,1)}, bf16[1,2,16,512]{3,2,1,0:T(8,128)(2,1)S(1)}, u32[]{:S(2)}) copy-start(bf16[1,2,16,512]{3,2,1,0:T(8,128)(2,1)S(1)} %get-tuple-element.7) | copy-start | bytes 98308
  46.9 12.4 %copy-start.13 = (bf16[1,2,16,512]{3,2,1,0:T(8,128)(2,1)}, bf16[1,2,16,512]{3,2,1,0:T(8,128)(2,1)S(1)}, u32[]{:S(2)}) copy-start(bf16[1,2,16,512]{3,2,1,0:T(8,128)(2,1)S(1)} %get-tuple-element.6) | copy-start | bytes 98308
  47.0 12.3 %copy-start.27 = (bf16[1,2,1,4,128]{4,3,2,1,0:T(4,128)(2,1)}, bf16[1,2,1,4,128]{4,3,2,1,0:T(4,128)(2,1)S(1)}, u32[]{:S(2)}) copy-start(bf16[1,2,1,4,128]{4,3,2,1,0:T(4,128)(2,1)S(1)} %get-tuple-element.95) | copy-start | bytes 6148
  47.0 12.3 %copy-start.28 = (bf16[1,2,1,4,128]{4,3,2,1,0:T(4,128)(2,1)}, bf16[1,2,1,4,128]{4,3,2,1,0:T(4,128)(2,1)S(1)}, u32[]{:S(2)}) copy-start(bf16[1,2,1,4,128]{4,3,2,1,0:T(4,128)(2,1)S(1)} %get-tuple-element.96) | copy-start | bytes 6148
  47.0 4.5 %copy-start.9 = (bf16[1,2,15,4,128]{4,3,2,1,0:T(4,128)(2,1)}, bf16[1,2,15,4,128]{4,3,2,1,0:T(4,128)(2,1)S(1)}, u32[]{:S(2)}) copy-start(bf16[1,2,15,4,128]{4,3,2,1,0:T(4,128)(2,1)S(1)} %get-tuple-element.93) | copy-start | bytes 92164
  47.0 4.5 %copy-start.11 = (bf16[1,2,15,4,128]{4,3,2,1,0:T(4,128)(2,1)}, bf16[1,2,15,4,128]{4,3,2,1,0:T(4,128)(2,1)S(1)}, u32[]{:S(2)}) copy-start(bf16[1,2,15,4,128]{4,3,2,1,0:T(4,128)(2,1)S(1)} %get-tuple-element.94) | copy-start | bytes 92164
  50.8 0.7 copy-start.26
  50.9 8.3 %copy-start.7 = (bf16[1,2,15,4,128]{4,3,2,1,0:T(4,128)(2,1)}, bf16[1,2,15,4,128]{4,3,2,1,0:T(4,128)(2,1)S(1)}, u32[]{:S(2)}) copy-start(bf16[1,2,15,4,128]{4,3,2,1,0:T(4,128)(2,1)S(1)} %get-tuple-element.78) | copy-start | bytes 92164
  59.2 21.8 %copy-start.19 = (bf16[128,128]{1,0:T(8,128)(2,1)S(1)}, bf16[128,128]{1,0:T(8,128)(2,1)}, u32[]{:S(2)}) copy-start(bf16[128,128]{1,0:T(8,128)(2,1)} %concatenate.414) | copy-start | bytes 98308
  59.2 21.9 %copy-start.10 = (bf16[1,2,15,4,128]{4,3,2,1,0:T(4,128)(2,1)S(1)}, bf16[1,2,15,4,128]{4,3,2,1,0:T(4,128)(2,1)}, u32[]{:S(2)}) copy-start(bf16[1,2,15,4,128]{4,3,2,1,0:T(4,128)(2,1)} %copy-done.9) | copy-start | bytes 92164
  59.2 23.4 %copy-start.18 = (bf16[1,2,16,4,128]{4,3,2,1,0:T(4,128)(2,1)S(1)}, bf16[1,2,16,4,128]{4,3,2,1,0:T(4,128)(2,1)}, u32[]{:S(2)}) copy-start(bf16[1,2,16,4,128]{4,3,2,1,0:T(4,128)(2,1)} %pad_maximum_fusion.25) | copy-start | bytes 98308
  59.2 25.8 %copy-start.17 = (bf16[1,2,16,4,128]{4,3,2,1,0:T(4,128)(2,1)S(1)}, bf16[1,2,16,4,128]{4,3,2,1,0:T(4,128)(2,1)}, u32[]{:S(2)}) copy-start(bf16[1,2,16,4,128]{4,3,2,1,0:T(4,128)(2,1)} %pad_maximum_fusion.26) | copy-start | bytes 98308
  59.2 24.2 %copy-start.8 = (bf16[1,2,15,4,128]{4,3,2,1,0:T(4,128)(2,1)S(1)}, bf16[1,2,15,4,128]{4,3,2,1,0:T(4,128)(2,1)}, u32[]{:S(2)}) copy-start(bf16[1,2,15,4,128]{4,3,2,1,0:T(4,128)(2,1)} %copy-done.7) | copy-start | bytes 92164
  59.3 18.2 %copy-start.22 = (bf16[1,2,1,4,128]{4,3,2,1,0:T(4,128)(2,1)}, bf16[1,2,1,4,128]{4,3,2,1,0:T(4,128)(2,1)S(1)}, u32[]{:S(2)}) copy-start(bf16[1,2,1,4,128]{4,3,2,1,0:T(4,128)(2,1)S(1)} %get-tuple-element.63) | copy-start | bytes 6148
  59.3 18.2 %copy-start.25 = (bf16[1,2,1,4,128]{4,3,2,1,0:T(4,128)(2,1)}, bf16[1,2,1,4,128]{4,3,2,1,0:T(4,128)(2,1)S(1)}, u32[]{:S(2)}) copy-start(bf16[1,2,1,4,128]{4,3,2,1,0:T(4,128)(2,1)S(1)} %get-tuple-element.64) | copy-start | bytes 6148
  59.3 27.2 %copy-start.14 = (bf16[1,2,16,512]{3,2,1,0:T(8,128)(2,1)S(1)}, bf16[1,2,16,512]{3,2,1,0:T(8,128)(2,1)}, u32[]{:S(2)}) copy-start(bf16[1,2,16,512]{3,2,1,0:T(8,128)(2,1)} %copy-done.13) | copy-start | bytes 98308
  59.5 25.9 %copy-start.24 = (bf16[1,2,1,4,128]{4,3,2,1,0:T(4,128)(2,1)S(1)}, bf16[1,2,1,4,128]{4,3,2,1,0:T(4,128)(2,1)}, u32[]{:S(2)}) copy-start(bf16[1,2,1,4,128]{4,3,2,1,0:T(4,128)(2,1)} %get-tuple-element.79) | copy-start | bytes 6148
  61.6 70.5 %copy-start.29 = (f32[128,128]{1,0:T(8,128)S(1)}, f32[128,128]{1,0:T(8,128)}, u32[]{:S(2)}) copy-start(f32[128,128]{1,0:T(8,128)} %param.9) | copy-start | bytes 196612
  61.6 35.3 %all-to-all-start = ((bf16[512,4,128]{2,1,0:T(4,128)(2,1)}), bf16[512,4,128]{2,1,0:T(4,128)(2,1)S(1)}, u32[]{:S(2)}, u32[]{:S(2)}) async-start(bf16[512,4,128]{2,1,0:T(4,128)(2,1)} %bitcast.50), calls=%async_computation | async-start | bytes 1048576 | tf_op jit(solution)/shard_map/all_to_all | solution.py:86
  77.6 31.5 %copy-start.23 = (bf16[1,2,1,4,128]{4,3,2,1,0:T(4,128)(2,1)S(1)}, bf16[1,2,1,4,128]{4,3,2,1,0:T(4,128)(2,1)}, u32[]{:S(2)}) copy-start(bf16[1,2,1,4,128]{4,3,2,1,0:T(4,128)(2,1)} %copy-done.22) | copy-start | bytes 6148
  98.4 32.6 %all-to-all-start.1 = ((bf16[512,4,128]{2,1,0:T(4,128)(2,1)}), bf16[512,4,128]{2,1,0:T(4,128)(2,1)S(1)}, u32[]{:S(2)}, u32[]{:S(2)}) async-start(bf16[512,4,128]{2,1,0:T(4,128)(2,1)} %broadcast_in_dim.14), calls=%async_computation.1 | async-start | bytes 1048576 | tf_op jit(solution)/shard_map/all_to_all | solution.py:89
  157.4 11.8 %copy-start = (bf16[1728,1728]{1,0:T(8,128)(2,1)}, bf16[1728,1728]{1,0:T(8,128)(2,1)S(1)}, u32[]{:S(2)}) copy-start(bf16[1728,1728]{1,0:T(8,128)(2,1)S(1)} %divide_convert_fusion) | copy-start | bytes 17915908
  159.3 1.3 copy-start.4
  162.4 1.2 copy-start.5
  165.5 1.8 copy-start.1
  167.3 1.9 %copy-start.2 = (f32[1728,256]{1,0:T(8,128)}, f32[1728,256]{1,0:T(8,128)S(1)}, u32[]{:S(2)}) copy-start(f32[1728,256]{1,0:T(8,128)S(1)} %fusion.16) | copy-start | bytes 5308420
Sparse Core Ops, SparseCore 0:
  29.8 93.7 all-gather.1

commit v2 on v1

v2 whole, which is shorter than its diff:
```python
import functools
import math

import jax
import jax.numpy as jnp
from jax import lax
from jax.experimental import pallas as pl
from jax.experimental.pallas import tpu as pltpu
from jax.sharding import PartitionSpec as P

POWER = 4
DEGREE = 6
DECAY = 0.9
EVERY = ("space", "dp")
VMEM = pl.BlockSpec(memory_space=pltpu.VMEM)
SMEM = pl.BlockSpec(memory_space=pltpu.SMEM)
BIG = pltpu.CompilerParams(vmem_limit_bytes=48 * 1024 * 1024)
ROWS_AT_ONCE = 432
CHUNKS = 4


def offset_list():
    return [(a, b, c) for a in (-1, 0, 1) for b in (-1, 0, 1) for c in (-1, 0, 1)]


def root_coefficients():
    terms_list = [(1, 5.0), (5, -5.0), (6, 4.0)]
    coeffs = [0.0] * 7
    for degree, factor in terms_list:
        for j in range(degree + 1):
            coeffs[j] += factor * math.comb(degree, j) * 1.25 ** (degree - j) * (-0.25) ** j / 4.0
    return coeffs


def rolled_rows(cells, shift):
    if shift == 0:
        return cells
    if shift > 0:
        return jnp.concatenate([cells[:, shift:], cells[:, :shift]], axis=1)
    height = cells.shape[1]
    return jnp.concatenate([cells[:, height + shift :], cells[:, : height + shift]], axis=1)


def conv_kernel(scale, before, volume, after, cotangent, weight, out, sent, pre_grad, patches):
    height = volume.shape[2]
    wide = volume.shape[3]
    lanes = weight.shape[1]
    half = lanes // 2
    across = wide // half
    depth = volume.shape[1]
    held = depth + 2
    rows = held * height
    cells = jnp.concatenate([before[0, :2], volume[0], after[0, :2]], axis=0).astype(jnp.float32)
    low = lax.broadcasted_iota(jnp.int32, (1, 1, lanes), 2) < half
    low_flat = lax.broadcasted_iota(jnp.int32, (1, lanes), 1) < half
    doubled = {}
    for pair in range(across // 2):
        both = cells[:, :, pair * lanes : (pair + 1) * lanes]
        turned = jnp.concatenate([both[:, :, half:], both[:, :, :half]], axis=2)
        for side, one in enumerate((jnp.where(low, both, turned), jnp.where(low, turned, both))):
            for b in (-1, 0, 1):
                moved = rolled_rows(one, b).astype(jnp.bfloat16)
                doubled[2 * pair + side, b] = moved.reshape((held + 2) * height, lanes)

    def piece(offset):
        a, b, c = offset
        first = (1 + a) * height
        return [doubled[(x + c) % across, b][first : first + rows] for x in range(across)]

    taps = [piece(o) for o in offset_list()]
    taps.append([jnp.zeros((rows, lanes), jnp.bfloat16)] * across)
    for j in range(len(taps) // 2):
        for x in range(across):
            patches[x * rows : (x + 1) * rows, j * lanes : (j + 1) * lanes] = jnp.where(
                low_flat, taps[2 * j][x], taps[2 * j + 1][x]
            )
    preact = jnp.dot(patches[...], weight[...], preferred_element_type=jnp.float32)
    sigmoid_val = jax.nn.sigmoid(preact)
    output = (preact * sigmoid_val).astype(jnp.bfloat16)
    inner = []
    upstream = []
    for x in range(across):
        span = slice(x * lanes, (x + 1) * lanes)
        place = (x % (across // 2)) * lanes
        side = 2 + x // (across // 2)
        upstream.append(before[0, side, :, place : place + lanes])
        upstream.extend(cotangent[0, p, :, span] for p in range(depth))
        upstream.append(after[0, side, :, place : place + lanes])
        for p in range(depth):
            first = x * rows + (1 + p) * height
            out[0, p, :, span] = output[first : first + height]
    upstream = jnp.concatenate(upstream, axis=0).astype(jnp.float32)
    slope = sigmoid_val * (1.0 + preact * (1.0 - sigmoid_val))
    grads = (upstream * slope).astype(jnp.bfloat16)
    pre_grad[...] = grads
    own = [slice(x * rows + height, x * rows + rows - height) for x in range(across)]
    own_patches = jnp.concatenate([patches[s, :] for s in own], axis=0)
    own_grads = jnp.concatenate([grads[s] for s in own], axis=0)
    local = lax.dot_general(
        own_patches, own_grads, (((0,), (0,)), ((), ())), preferred_element_type=jnp.float32
    )
    fan = patches.shape[1]
    sent[:fan, :] = (local * scale).astype(jnp.bfloat16)
    sent[fan:, :] = jnp.zeros((sent.shape[0] - fan, lanes), jnp.bfloat16)


def back_kernel(pre_grad, flipped, out, patches):
    height, depth = out.shape[2], out.shape[1]
    lanes = pre_grad.shape[1]
    across = out.shape[3] // (lanes // 2)
    rows = pre_grad.shape[0] // across
    held = rows // height
    own = depth * height
    grads = pre_grad[...].astype(jnp.float32).reshape(across, held, height, lanes)
    moved = {}
    for x in range(across):
        for b in (-1, 0, 1):
            moved[x, b] = rolled_rows(grads[x], -b).astype(jnp.bfloat16).reshape(rows, lanes)
    for k, (a, b, c) in enumerate(offset_list()):
        first = (1 - a) * height
        for x in range(across):
            patches[x * own : (x + 1) * own, k * lanes : (k + 1) * lanes] = moved[
                (x - c) % across, b
            ][first : first + own]
    result = jnp.dot(patches[...], flipped[...], preferred_element_type=jnp.float32)
    low = lax.broadcasted_iota(jnp.int32, (1, lanes), 1) < lanes // 2
    for pair in range(across // 2):
        left = result[2 * pair * own : (2 * pair + 1) * own]
        right = result[(2 * pair + 1) * own : (2 * pair + 2) * own]
        both = jnp.where(low, left, right).astype(jnp.bfloat16)
        for p in range(depth):
            out[0, p, :, pair * lanes : (pair + 1) * lanes] = both[p * height : (p + 1) * height]


def whole_sum(values):
    return jnp.sum(jnp.sum(values, axis=0, keepdims=True), axis=1, keepdims=True)


def diagonal_sum(block):
    row_ids = lax.broadcasted_iota(jnp.int32, block.shape, 0)
    col_ids = lax.broadcasted_iota(jnp.int32, block.shape, 1)
    return whole_sum(jnp.where(row_ids == col_ids, block, 0.0))


def sharp_dot(left, right):
    return jnp.dot(
        left, right, precision=lax.Precision.HIGHEST, preferred_element_type=jnp.float32
    )


def right_root_of(full, coeffs):
    size = full.shape[0]
    trace = diagonal_sum(full)
    scaled = full / trace
    vector = jnp.full((1, size), 1.0 / math.sqrt(size), jnp.float32)
    lengths = []
    for step in range(POWER):
        vector = jnp.sum(scaled * vector, axis=1 - step % 2, keepdims=True)
        lengths.append(jnp.sqrt(whole_sum(vector * vector)))
    largest = trace * lengths[POWER - 1] / lengths[POWER - 2]
    unit = full / largest
    row_ids = lax.broadcasted_iota(jnp.int32, full.shape, 0)
    col_ids = lax.broadcasted_iota(jnp.int32, full.shape, 1)
    identity = (row_ids == col_ids).astype(jnp.float32)
    square = sharp_dot(unit, unit)
    cube = sharp_dot(square, unit)
    low = coeffs[0] * identity + coeffs[1] * unit + coeffs[2] * square + coeffs[3] * cube
    high = coeffs[4] * unit + coeffs[5] * square + coeffs[6] * cube
    return (low + sharp_dot(cube, high)) * lax.rsqrt(jnp.sqrt(largest))


def refresh_kernel(first, joined, left_far, right_stat, gradient, direction, left, block, powers, sems):
    fan, width = gradient.shape
    part = fan // CHUNKS
    copies = []
    for k in range(CHUNKS):
        rows = pl.ds(k * part, part)
        copies.append(pltpu.make_async_copy(left_far.at[rows], left.at[rows], sems.at[k]))
        copies[-1].start()
    coeffs = root_coefficients()
    rounded = joined[:fan, :]
    wide_grad = rounded.astype(jnp.float32)
    gradient[...] = wide_grad
    grad_square = whole_sum(wide_grad * wide_grad)
    right_full = DECAY * right_stat[...] + lax.dot_general(
        rounded, rounded, (((0,), (0,)), ((), ())), preferred_element_type=jnp.float32
    )
    root = right_root_of(right_full, coeffs)
    root_high = root.astype(jnp.bfloat16)
    root_low = (root - root_high.astype(jnp.float32)).astype(jnp.bfloat16)
    parts = jnp.dot(
        rounded,
        jnp.concatenate([root_high, root_low], axis=1),
        preferred_element_type=jnp.float32,
    )
    carried = parts[:, :width] + parts[:, width:]
    powers[0] = carried
    block[0, :, :width] = carried.astype(jnp.bfloat16)
    block[0, :, width:] = jnp.full((fan, width), 1.0 / math.sqrt(fan), jnp.bfloat16)
    for copy in copies:
        copy.wait()
    trace = grad_square
    for start in range(0, fan, width):
        size = min(width, fan - start)
        trace = trace + DECAY * diagonal_sum(
            left[start : start + size, start : start + size].astype(jnp.float32)
        )
    inverse = 1.0 / trace

    def add_gradient(k, _):
        rows = pl.ds(pl.multiple_of(k * 144, 144), 144)
        outer = lax.dot_general(
            joined[rows, :], rounded, (((1,), (1,)), ((), ())), preferred_element_type=jnp.float32
        )
        left[rows, :] = (DECAY * left[rows, :].astype(jnp.float32) + outer).astype(jnp.bfloat16)
        return 0

    lax.fori_loop(0, fan // 144, add_gradient, 0)
    squares = {}
    for degree in range(1, DEGREE + 1):
        held = block[(degree - 1) % 2]

        def multiply(k, square, held=held, degree=degree):
            rows = pl.ds(pl.multiple_of(k * ROWS_AT_ONCE, ROWS_AT_ONCE), ROWS_AT_ONCE)
            product = inverse * jnp.dot(left[rows, :], held, preferred_element_type=jnp.float32)
            powers[degree, rows, :] = product[:, :width]
            if degree < DEGREE:
                block[degree % 2, rows, :] = product.astype(jnp.bfloat16)
            if degree in (POWER - 1, POWER):
                column = product[:, width:]
                square = square + jnp.sum(column * column, axis=0, keepdims=True)
            return square

        squares[degree] = lax.fori_loop(
            0, fan // ROWS_AT_ONCE, multiply, jnp.zeros((1, width), jnp.float32)
        )
    share = jnp.sqrt(squares[POWER][:, :1]) / jnp.sqrt(squares[POWER - 1][:, :1])
    update = coeffs[0] * powers[0]
    factor = 1.0 / share
    scale = factor
    for degree in range(1, DEGREE + 1):
        update = update + (coeffs[degree] * scale) * powers[degree]
        scale = scale * factor
    update = update * lax.rsqrt(jnp.sqrt(share * trace))
    powers[0] = update
    update_norm = jnp.sqrt(whole_sum(update * update))
    ratio = jnp.sqrt(grad_square) / (update_norm + 1e-06)
    size = direction.shape[0]
    direction[...] = powers[0, pl.ds(pl.multiple_of(first[0], 8), size), :] * ratio


def convolved(before, volume, after, cotangent, weight, scale, spread_rows):
    leading, depth, height, wide = volume.shape
    lanes = weight.shape[1]
    cells = wide // (lanes // 2) * (depth + 2) * height
    return pl.pallas_call(
        functools.partial(conv_kernel, scale),
        out_shape=(
            jax.ShapeDtypeStruct(cotangent.shape, jnp.bfloat16),
            jax.ShapeDtypeStruct((spread_rows, lanes), jnp.bfloat16),
            jax.ShapeDtypeStruct((cells, lanes), jnp.bfloat16),
        ),
        in_specs=[VMEM] * 5,
        out_specs=(VMEM,) * 3,
        scratch_shapes=[pltpu.VMEM((cells, weight.shape[0]), jnp.bfloat16)],
        compiler_params=BIG,
        name="conv",
    )(before, volume, after, cotangent, weight)


def convolved_back(pre_grad, flipped, volume):
    leading, depth, height, wide = volume.shape
    lanes = pre_grad.shape[1]
    own = wide // (lanes // 2) * depth * height
    return pl.pallas_call(
        back_kernel,
        out_shape=jax.ShapeDtypeStruct(volume.shape, jnp.bfloat16),
        in_specs=[VMEM] * 2,
        out_specs=VMEM,
        scratch_shapes=[pltpu.VMEM((own, flipped.shape[0]), jnp.bfloat16)],
        compiler_params=BIG,
        cost_estimate=pl.CostEstimate(
            flops=2 * own * flipped.size, bytes_accessed=2 * own * flipped.shape[0], transcendentals=0
        ),
        name="conv_back",
    )(pre_grad, flipped)


def refreshed(first_row, joined, left_all, right_stat, fan, row_count):
    width = right_stat.shape[0]
    return pl.pallas_call(
        refresh_kernel,
        out_shape=(
            jax.ShapeDtypeStruct((fan, width), jnp.float32),
            jax.ShapeDtypeStruct((row_count, width), jnp.float32),
        ),
        in_specs=[SMEM, VMEM, pl.BlockSpec(memory_space=pl.ANY), VMEM],
        out_specs=(VMEM, VMEM),
        scratch_shapes=[
            pltpu.VMEM((fan, fan), jnp.bfloat16),
            pltpu.VMEM((2, fan, 2 * width), jnp.bfloat16),
            pltpu.VMEM((DEGREE + 1, fan, width), jnp.float32),
            pltpu.SemaphoreType.DMA((CHUNKS,)),
        ],
        compiler_params=BIG,
        name="refresh",
    )(first_row, joined, left_all, right_stat)


def per_device(volume, weight, cotangent, left_stat, right_stat):
    fan, lanes = weight.shape
    leading, depth, height, wide = volume.shape
    devices = lax.axis_size(EVERY)
    slabs = lax.axis_size("space")
    left_all = lax.all_gather(left_stat.astype(jnp.bfloat16), "dp", axis=0, tiled=True)
    onward = [(i, (i + 1) % slabs) for i in range(slabs)]
    back = [((i + 1) % slabs, i) for i in range(slabs)]

    def with_plane(plane):
        return jnp.concatenate([volume, plane[..., :wide], plane[..., wide:]], axis=1)

    before = lax.ppermute(with_plane(cotangent[:, -1:]), "space", onward)
    after = lax.ppermute(with_plane(cotangent[:, :1]), "space", back)
    channels = fan // 27
    flipped = weight.reshape(27, channels, lanes).transpose(0, 2, 1).reshape(27 * lanes, channels)
    flipped = jnp.concatenate([flipped, flipped], axis=1)
    padded_fan = (fan + lanes - 1) // lanes * lanes
    padded = jnp.pad(weight, ((0, padded_fan - fan), (0, 0)))
    piece = 4 * ((fan + 4 * devices - 1) // (4 * devices))
    cells = slabs * lax.axis_size("dp") * leading * depth * height * (wide // channels)
    output, sent, pre_grad = convolved(
        before, volume, after, cotangent, padded, 1.0 / math.sqrt(cells), piece * devices
    )
    terms = lax.all_to_all(sent.reshape(devices, piece, lanes), EVERY, 0, 0)
    total = jnp.sum(terms.astype(jnp.float32), axis=0).astype(jnp.bfloat16)
    joined = lax.all_to_all(jnp.broadcast_to(total[None], terms.shape), EVERY, 0, 0)
    input_grad = convolved_back(pre_grad, flipped, volume)
    row_count = left_stat.shape[0]
    first_row = (lax.axis_index("dp") * row_count).astype(jnp.int32).reshape(1)
    gradient, direction = refreshed(
        first_row, joined.reshape(devices * piece, lanes), left_all, right_stat, fan, row_count
    )
    return output, input_grad, gradient, direction


def solution(mesh):
    placed = (P("dp", "space", None, None), P(), P("dp", "space", None, None), P("dp", None), P())
    return jax.shard_map(
        per_device,
        mesh=mesh,
        in_specs=placed,
        out_specs=(P("dp", "space", None, None), P("dp", "space", None, None), P(), P("dp", None)),
        check_vma=False,
    )
```

time: 191 us -> 145 us (0.76)
  blocking collectives: 0 us -> 38.6 us
  matrix products: 34.6 us -> 0 us
  other arithmetic: 32.7 us -> 3.45 us
  local copies, waits for them, and re-layouts: 29 us -> 1.45 us
  Pallas kernels: 0 us -> 25.3 us
  starting transfers between devices: 42.7 us -> 28 us
  between operations: 21.7 us -> 14.2 us
  waiting for transfers between devices: 29 us -> 31.4 us
    all_to_all x0 -> x1, blocking collectives: none -> 38.6 us  [per_device(): terms = lax.all_to_all(sent.reshape(devices, piece, lanes), EVERY, 0, 0)]
    dot_general x21 -> x0, matrix products: 34.6 us -> none  [the longest x6 17.3 us: per_device(): jnp.dot(scaled, block.astype(jnp.bfloat16), preferred_element_type=jnp.fl...]
    pallas_call x0 -> x3, Pallas kernels: none -> 25.3 us  [the longest x1 23.1 us: refreshed(): pl.pallas_call(refresh_kernel, out_shape=(jax.ShapeDtypeStruct((fan, widt...]
    concatenate x62 -> x2, other arithmetic: 17.6 us -> 0.5 us  [the longest x1 0.49 us: per_device(): flipped = jnp.concatenate([flipped, flipped], axis=1)]
    concatenate x13 -> x0, local copies, waits for them, and re-layouts: 15.6 us -> none  [the longest x9 14.6 us: gather_patches(): return jnp.concatenate(pieces, axis=4).reshape(-1, 27 * channels)]
    all_to_all x2 -> x1, starting transfers between devices: 24.2 us -> 9.52 us  [per_device(): lax.all_to_all(jnp.broadcast_to(total[None], terms.shape), EVERY, 0, 0)]
    all_gather x1, waiting for transfers between devices: 0.01 us -> 9.72 us  [per_device(): lax.all_gather(left_stat.astype(jnp.bfloat16), 'dp', axis=0, tiled=True)]
    all_to_all x2 -> x1, waiting for transfers between devices: 29 us -> 19.9 us  [per_device(): lax.all_to_all(jnp.broadcast_to(total[None], terms.shape), EVERY, 0, 0)]
  transfers between devices with their start and end apart: 5 -> 4, of which waited for: 2 -> 3; matrix products, arithmetic and copies ran while one was open for 30% -> 2% of each run, Pallas kernels for 0% -> 2%
where the time goes in v2:
time: 145 us; the launch traced here: 142 us
  blocking collectives  38.6 us (27%)
  waiting for transfers between devices  31.4 us (22%)
  starting transfers between devices  28 us (19%)
  Pallas kernels  25.3 us (17%)
  between operations  14.2 us (10%)
  other arithmetic  3.45 us (2%)
  local copies, waits for them, and re-layouts  1.45 us (1%)
    all_to_all x1, blocking collectives, per_device(): terms = lax.all_to_all(sent.reshape(devices, piece, lanes), EVERY, 0, 0)  38.6 us
    pallas_call x1, Pallas kernels, refreshed(): pl.pallas_call(refresh_kernel, out_shape=(jax.ShapeDtypeStruct((fan, widt...  23.1 us
    all_to_all x1, waiting for transfers between devices, per_device(): lax.all_to_all(jnp.broadcast_to(total[None], terms.shape), EVERY, 0, 0)  19.9 us
    ppermute x1, starting transfers between devices, per_device(): before = lax.ppermute(with_plane(cotangent[:, -1:]), 'space', onward)  11.5 us
    all_gather x1, waiting for transfers between devices, per_device(): lax.all_gather(left_stat.astype(jnp.bfloat16), 'dp', axis=0, tiled=True)  9.72 us
    all_to_all x1, starting transfers between devices, per_device(): lax.all_to_all(jnp.broadcast_to(total[None], terms.shape), EVERY, 0, 0)  9.52 us
    ppermute x1, starting transfers between devices, per_device(): after = lax.ppermute(with_plane(cotangent[:, :1]), 'space', back)  7.02 us
  transfers between devices with their start and end apart: 4, of which 3 were waited for; matrix products, arithmetic and copies ran while one was open for 2% of the time, Pallas kernels for 2%

profile of v2, /device:TPU:1, one launch (start us, length us, event | category | flops | bytes accessed | tf_op | source)
XLA Modules:
  0.0 142.4 jit_solution(4474731404767283578)
XLA Ops:
  7.2 0.0 copy-start
  7.2 0.0 copy-start.2
  7.2 0.0 copy-start.3
  7.2 0.0 all-gather.2.cloned.1.call-start
  7.2 2.4 %convert_element_type.4 = bf16[216,1728]{1,0:T(8,128)(2,1)} convert(f32[216,1728]{1,0:T(8,128)} %param.8) | non-fusion elementwise | flops 373248 | bytes 2239488 | tf_op jit(solution)/shard_map/convert_element_type | solution.py:315
  9.6 0.0 all-gather.2.cloned.1.call-update
  9.7 0.0 copy-done
  9.7 0.0 copy-done.2
  9.7 11.5 %collective-permute-start = (bf16[1,4,16,256]{3,2,1,0:T(8,128)(2,1)S(1)}, bf16[1,4,16,256]{3,2,1,0:T(8,128)(2,1)S(1)}, u32[]{:S(2)}, u32[]{:S(2)}) collective-permute-start(bf16[1,4,16,256]{3,2,1,0:T(8,128)(2,1)S(1)} %get-tuple-element.19), channel_id=1, source_target_pairs={{0,8},{8,16},{16,24},{24,32},{32,40},{40,48},{48,56},{56,64},{64,7... | collective-permute-start | bytes 98312 | tf_op jit(solution)/shard_map/ppermute | solution.py:322
  21.2 7.0 %collective-permute-start.1 = (bf16[1,4,16,256]{3,2,1,0:T(8,128)(2,1)S(1)}, bf16[1,4,16,256]{3,2,1,0:T(8,128)(2,1)S(1)}, u32[]{:S(2)}, u32[]{:S(2)}) collective-permute-start(bf16[1,4,16,256]{3,2,1,0:T(8,128)(2,1)S(1)} %get-tuple-element.18), channel_id=1, source_target_pairs={{8,0},{16,8},{24,16},{32,24},{40,32},{48,40},{56,48},{64,56},{72,6... | collective-permute-start | bytes 98312 | tf_op jit(solution)/shard_map/ppermute | solution.py:323
  28.2 0.0 copy-done.3
  28.3 0.0 collective-permute-done.before
  28.3 1.8 %collective-permute-done.1.after = bf16[1,4,16,256]{3,2,1,0:T(8,128)(2,1)S(1)} collective-permute-done((bf16[1,4,16,256]{3,2,1,0:T(8,128)(2,1)S(1)}, bf16[1,4,16,256]{3,2,1,0:T(8,128)(2,1)S(1)}, u32[]{:S(2)}, u32[]{:S(2)}) %collective-permute-start.1) | collective-permute-done | bytes 32800 | tf_op jit(solution)/shard_map/ppermute | solution.py:323
  30.1 1.2 conv.1
  31.2 38.6 %all_to_all.10 = bf16[512,4,128]{2,1,0:T(4,128)(2,1)S(1)} all-to-all(bf16[512,4,128]{2,1,0:T(4,128)(2,1)S(1)} %bitcast.8), channel_id=1, replica_groups=mesh['space'=64,'dp'=8] {'space','dp'}, dimensions={0} | all-to-all | bytes 1048576 | tf_op jit(solution)/shard_map/all_to_all | solution.py:334
  69.8 0.6 reduce_sum.12
  70.4 1.0 broadcast_in_dim.2
  71.3 9.5 %all-to-all-start.1 = ((bf16[512,4,128]{2,1,0:T(4,128)(2,1)}), bf16[512,4,128]{2,1,0:T(4,128)(2,1)S(1)}, u32[]{:S(2)}, u32[]{:S(2)}) async-start(bf16[512,4,128]{2,1,0:T(4,128)(2,1)} %broadcast_in_dim.2), calls=%async_computation.1 | async-start | bytes 1048576 | tf_op jit(solution)/shard_map/all_to_all | solution.py:336
  80.9 0.0 copy-start.1
  80.9 0.4 copy.9
  81.3 0.5 pad_maximum_fusion.flipped
  81.8 1.0 conv_back.1
  82.9 19.9 %all-to-all-done.1 = bf16[512,4,128]{2,1,0:T(4,128)(2,1)S(1)} async-done(((bf16[512,4,128]{2,1,0:T(4,128)(2,1)}), bf16[512,4,128]{2,1,0:T(4,128)(2,1)S(1)}, u32[]{:S(2)}, u32[]{:S(2)}) %all-to-all-start.1) | async-done | bytes 524320 | tf_op jit(solution)/shard_map/all_to_all | solution.py:336
  102.7 9.7 %all-gather.2.cloned.1.call-done.left_far = bf16[1728,1728]{1,0:T(8,128)(2,1)} async-done(((bf16[216,1728]{1,0:T(8,128)(2,1)}), bf16[1728,1728]{1,0:T(8,128)(2,1)}) %all-gather.2.cloned.1.call-update) | async-done | bytes 5971984 | tf_op jit(solution)/shard_map/all_gather | solution.py:315
  112.4 0.0 copy-done.1
  112.4 23.1 %refresh.1 = (f32[1728,128]{1,0:T(8,128)}, f32[216,128]{1,0:T(8,128)}) custom-call(s32[1]{0:T(128)} %bitcast.3.first, bf16[2048,128]{1,0:T(8,128)(2,1)S(1)} %bitcast.7, bf16[1728,1728]{1,0:T(8,128)(2,1)} %all-gather.2.cloned.1.call-done.left_far, f32[128,128]{1,0:T(8,128)S(1)} %copy-done.1), custom_call_target="tpu_custom_call" | custom-call | tf_op jit(solution)/shard_map/refresh/pallas_call | solution.py:291
  (3 shorter events, 0.0 us)
Async XLA Ops:
  7.2 2.5 %copy-start = (bf16[1,2,16,512]{3,2,1,0:T(8,128)(2,1)S(1)}, bf16[1,2,16,512]{3,2,1,0:T(8,128)(2,1)}, u32[]{:S(2)}) copy-start(bf16[1,2,16,512]{3,2,1,0:T(8,128)(2,1)} %cotangent.1) | copy-start | bytes 98308
  7.2 2.5 %copy-start.2 = (bf16[1,2,16,256]{3,2,1,0:T(8,128)(2,1)S(1)}, bf16[1,2,16,256]{3,2,1,0:T(8,128)(2,1)}, u32[]{:S(2)}) copy-start(bf16[1,2,16,256]{3,2,1,0:T(8,128)(2,1)} %volume.1) | copy-start | bytes 49156
  7.2 21.0 %copy-start.3 = (bf16[1728,128]{1,0:T(8,128)(2,1)S(1)}, bf16[1728,128]{1,0:T(8,128)(2,1)}, u32[]{:S(2)}) copy-start(bf16[1728,128]{1,0:T(8,128)(2,1)} %param.6) | copy-start | bytes 1327108
  7.2 105.2 %all-gather.2.cloned.1.call-start = ((), (), s32[]{:S(2)}) async-start(), calls=%async_computation.2 | async-start | bytes 6967296 | tf_op jit(solution)/shard_map/all_gather | solution.py:315
  9.7 18.6 %collective-permute-start = (bf16[1,4,16,256]{3,2,1,0:T(8,128)(2,1)S(1)}, bf16[1,4,16,256]{3,2,1,0:T(8,128)(2,1)S(1)}, u32[]{:S(2)}, u32[]{:S(2)}) collective-permute-start(bf16[1,4,16,256]{3,2,1,0:T(8,128)(2,1)S(1)} %get-tuple-element.19), channel_id=1, source_target_pairs={{0,8},{8,16},{16,24},{24,32},{32,40},{40,48},{48,56},{56,64},{64,7... | collective-permute-start | bytes 98312 | tf_op jit(solution)/shard_map/ppermute | solution.py:322
  21.2 8.9 %collective-permute-start.1 = (bf16[1,4,16,256]{3,2,1,0:T(8,128)(2,1)S(1)}, bf16[1,4,16,256]{3,2,1,0:T(8,128)(2,1)S(1)}, u32[]{:S(2)}, u32[]{:S(2)}) collective-permute-start(bf16[1,4,16,256]{3,2,1,0:T(8,128)(2,1)S(1)} %get-tuple-element.18), channel_id=1, source_target_pairs={{8,0},{16,8},{24,16},{32,24},{40,32},{48,40},{56,48},{64,56},{72,6... | collective-permute-start | bytes 98312 | tf_op jit(solution)/shard_map/ppermute | solution.py:323
  71.3 31.4 %all-to-all-start.1 = ((bf16[512,4,128]{2,1,0:T(4,128)(2,1)}), bf16[512,4,128]{2,1,0:T(4,128)(2,1)S(1)}, u32[]{:S(2)}, u32[]{:S(2)}) async-start(bf16[512,4,128]{2,1,0:T(4,128)(2,1)} %broadcast_in_dim.2), calls=%async_computation.1 | async-start | bytes 1048576 | tf_op jit(solution)/shard_map/all_to_all | solution.py:336
  80.9 31.6 %copy-start.1 = (f32[128,128]{1,0:T(8,128)S(1)}, f32[128,128]{1,0:T(8,128)}, u32[]{:S(2)}) copy-start(f32[128,128]{1,0:T(8,128)} %right_stat.1) | copy-start | bytes 196612
Sparse Core Ops, SparseCore 0:
  10.7 101.7 all-gather.1

commit v3 on v2

--- a/solution.py
+++ b/solution.py
@@ -6,17 +6,15 @@
 from jax import lax
 from jax.experimental import pallas as pl
 from jax.experimental.pallas import tpu as pltpu
+from jax.sharding import Mesh
 from jax.sharding import PartitionSpec as P
 
 POWER = 4
 DEGREE = 6
 DECAY = 0.9
-EVERY = ("space", "dp")
 VMEM = pl.BlockSpec(memory_space=pltpu.VMEM)
 SMEM = pl.BlockSpec(memory_space=pltpu.SMEM)
 BIG = pltpu.CompilerParams(vmem_limit_bytes=48 * 1024 * 1024)
-ROWS_AT_ONCE = 432
-CHUNKS = 4
 
 
 def offset_list():
@@ -41,7 +39,9 @@
     return jnp.concatenate([cells[:, height + shift :], cells[:, : height + shift]], axis=1)
 
 
-def conv_kernel(scale, before, volume, after, cotangent, weight, out, sent, pre_grad, patches):
+def conv_kernel(
+    scale, place, before, volume, after, cotangent, weight, out, keep, give, pre_grad, patches
+):
     height = volume.shape[2]
     wide = volume.shape[3]
     lanes = weight.shape[1]
@@ -81,11 +81,11 @@
     upstream = []
     for x in range(across):
         span = slice(x * lanes, (x + 1) * lanes)
-        place = (x % (across // 2)) * lanes
+        begin = (x % (across // 2)) * lanes
         side = 2 + x // (across // 2)
-        upstream.append(before[0, side, :, place : place + lanes])
+        upstream.append(before[0, side, :, begin : begin + lanes])
         upstream.extend(cotangent[0, p, :, span] for p in range(depth))
-        upstream.append(after[0, side, :, place : place + lanes])
+        upstream.append(after[0, side, :, begin : begin + lanes])
         for p in range(depth):
             first = x * rows + (1 + p) * height
             out[0, p, :, span] = output[first : first + height]
@@ -99,9 +99,13 @@
     local = lax.dot_general(
         own_patches, own_grads, (((0,), (0,)), ((), ())), preferred_element_type=jnp.float32
     )
-    fan = patches.shape[1]
-    sent[:fan, :] = (local * scale).astype(jnp.bfloat16)
-    sent[fan:, :] = jnp.zeros((sent.shape[0] - fan, lanes), jnp.bfloat16)
+    local = local * scale
+    part = keep.shape[0]
+    rest = jnp.zeros((2 * part - local.shape[0], lanes), jnp.float32)
+    head, tail = local[:part], jnp.concatenate([local[part:], rest], axis=0)
+    leading = place[0] == 0
+    keep[...] = jnp.where(leading, head, tail)
+    give[...] = jnp.where(leading, tail, head).astype(jnp.bfloat16)
 
 
 def back_kernel(pre_grad, flipped, out, patches):
@@ -169,72 +173,78 @@
     return (low + sharp_dot(cube, high)) * lax.rsqrt(jnp.sqrt(largest))
 
 
-def refresh_kernel(first, joined, left_far, right_stat, gradient, direction, left, block, powers, sems):
+def pack_kernel(rows, packed):
+    count, fan = rows.shape
+    spare = packed.shape[0] - count
+    gap = jnp.zeros((count, spare), jnp.float32)
+    pieces = []
+    for start in range(0, fan, count):
+        pieces.extend([rows[:, start : start + count], gap])
+    wide = jnp.concatenate(pieces, axis=1)
+    tall = jnp.concatenate([wide, jnp.zeros((spare, wide.shape[1]), jnp.float32)], axis=0)
+    packed[...] = tall.astype(jnp.bfloat16)
+
+
+def refresh_kernel(
+    place, mine, theirs, left_mine, left_theirs, right_stat, gradient, direction,
+    left, spaced, tall_ref, block, powers, window,
+):
     fan, width = gradient.shape
-    part = fan // CHUNKS
-    copies = []
-    for k in range(CHUNKS):
-        rows = pl.ds(k * part, part)
-        copies.append(pltpu.make_async_copy(left_far.at[rows], left.at[rows], sems.at[k]))
-        copies[-1].start()
+    count = direction.shape[0]
+    blocks = fan // count
+    step = left.shape[0] // blocks
+    core = place[0]
     coeffs = root_coefficients()
-    rounded = joined[:fan, :]
-    wide_grad = rounded.astype(jnp.float32)
-    gradient[...] = wide_grad
-    grad_square = whole_sum(wide_grad * wide_grad)
-    right_full = DECAY * right_stat[...] + lax.dot_general(
-        rounded, rounded, (((0,), (0,)), ((), ())), preferred_element_type=jnp.float32
-    )
+    own, other = mine[...].astype(jnp.float32), theirs[...].astype(jnp.float32)
+    half = own.shape[0]
+    gradient[:half, :] = jnp.where(core == 0, own, other)
+    gradient[half:, :] = jnp.where(core == 0, other, own)[: fan - half]
+    grad_square = whole_sum(gradient[...] * gradient[...])
+    for k in range(blocks):
+        spaced[k * step : k * step + count, :] = gradient[k * count : (k + 1) * count, :]
+        spaced[k * step + count : (k + 1) * step, :] = jnp.zeros((step - count, width), jnp.float32)
+    tall = spaced[...].astype(jnp.bfloat16)
+    tall_ref[...] = tall
+    flat = jnp.transpose(spaced[...]).astype(jnp.bfloat16)
+    for source, side in ((left_mine, core), (left_theirs, 1 - core)):
+
+        def add_gradient(chip, _, source=source, side=side):
+            rows = pl.ds(pl.multiple_of((2 * chip + side) * step, step), step)
+            outer = jnp.dot(tall_ref[rows, :], flat, preferred_element_type=jnp.float32)
+            held = source[pl.ds(pl.multiple_of(chip * step, step), step), :].astype(jnp.float32)
+            left[rows, :] = (DECAY * held + outer).astype(jnp.bfloat16)
+            return 0
+
+        lax.fori_loop(0, blocks // 2, add_gradient, 0)
+    trace = jnp.zeros((1, 1), jnp.float32)
+    for start in range(0, left.shape[0], width):
+        square = left[start : start + width, start : start + width]
+        trace = trace + diagonal_sum(square.astype(jnp.float32))
+    inverse = 1.0 / trace
+    right_full = DECAY * right_stat[...] + jnp.dot(flat, tall, preferred_element_type=jnp.float32)
     root = right_root_of(right_full, coeffs)
     root_high = root.astype(jnp.bfloat16)
     root_low = (root - root_high.astype(jnp.float32)).astype(jnp.bfloat16)
     parts = jnp.dot(
-        rounded,
-        jnp.concatenate([root_high, root_low], axis=1),
-        preferred_element_type=jnp.float32,
-    )
-    carried = parts[:, :width] + parts[:, width:]
+        jnp.concatenate([root_high, root_low], axis=0), flat, preferred_element_type=jnp.float32
+    )
+    carried = parts[:width] + parts[width:]
     powers[0] = carried
-    block[0, :, :width] = carried.astype(jnp.bfloat16)
-    block[0, :, width:] = jnp.full((fan, width), 1.0 / math.sqrt(fan), jnp.bfloat16)
-    for copy in copies:
-        copy.wait()
-    trace = grad_square
-    for start in range(0, fan, width):
-        size = min(width, fan - start)
-        trace = trace + DECAY * diagonal_sum(
-            left[start : start + size, start : start + size].astype(jnp.float32)
-        )
-    inverse = 1.0 / trace
-
-    def add_gradient(k, _):
-        rows = pl.ds(pl.multiple_of(k * 144, 144), 144)
-        outer = lax.dot_general(
-            joined[rows, :], rounded, (((1,), (1,)), ((), ())), preferred_element_type=jnp.float32
-        )
-        left[rows, :] = (DECAY * left[rows, :].astype(jnp.float32) + outer).astype(jnp.bfloat16)
-        return 0
-
-    lax.fori_loop(0, fan // 144, add_gradient, 0)
+    vectors = block.shape[1] - width
+    first_row = lax.broadcasted_iota(jnp.int32, (vectors, left.shape[0]), 0) == 0
+    block[0, :width, :] = carried.astype(jnp.bfloat16)
+    block[0, width:, :] = jnp.where(first_row, 1.0 / math.sqrt(fan), 0.0).astype(jnp.bfloat16)
     squares = {}
     for degree in range(1, DEGREE + 1):
-        held = block[(degree - 1) % 2]
-
-        def multiply(k, square, held=held, degree=degree):
-            rows = pl.ds(pl.multiple_of(k * ROWS_AT_ONCE, ROWS_AT_ONCE), ROWS_AT_ONCE)
-            product = inverse * jnp.dot(left[rows, :], held, preferred_element_type=jnp.float32)
-            powers[degree, rows, :] = product[:, :width]
-            if degree < DEGREE:
-                block[degree % 2, rows, :] = product.astype(jnp.bfloat16)
-            if degree in (POWER - 1, POWER):
-                column = product[:, width:]
-                square = square + jnp.sum(column * column, axis=0, keepdims=True)
-            return square
-
-        squares[degree] = lax.fori_loop(
-            0, fan // ROWS_AT_ONCE, multiply, jnp.zeros((1, width), jnp.float32)
+        product = inverse * jnp.dot(
+            block[(degree - 1) % 2], left[...], preferred_element_type=jnp.float32
         )
-    share = jnp.sqrt(squares[POWER][:, :1]) / jnp.sqrt(squares[POWER - 1][:, :1])
+        powers[degree] = product[:width]
+        if degree < DEGREE:
+            block[degree % 2] = product.astype(jnp.bfloat16)
+        if degree in (POWER - 1, POWER):
+            squares[degree] = whole_sum(product[width:] * product[width:])
+    share = jnp.sqrt(squares[POWER]) / jnp.sqrt(squares[POWER - 1])
     update = coeffs[0] * powers[0]
     factor = 1.0 / share
     scale = factor
@@ -245,11 +255,14 @@
     powers[0] = update
     update_norm = jnp.sqrt(whole_sum(update * update))
     ratio = jnp.sqrt(grad_square) / (update_norm + 1e-06)
-    size = direction.shape[0]
-    direction[...] = powers[0, pl.ds(pl.multiple_of(first[0], 8), size), :] * ratio
-
-
-def convolved(before, volume, after, cotangent, weight, scale, spread_rows):
+    span = window.shape[0]
+    first = place[1] * step
+    base = jnp.minimum(first // width * width, left.shape[0] - span)
+    window[...] = jnp.transpose(powers[0, :, pl.ds(pl.multiple_of(base, width), span)])
+    direction[...] = window[pl.ds(pl.multiple_of(first - base, 8), count), :] * ratio
+
+
+def convolved(place, before, volume, after, cotangent, weight, scale, part):
     leading, depth, height, wide = volume.shape
     lanes = weight.shape[1]
     cells = wide // (lanes // 2) * (depth + 2) * height
@@ -257,15 +270,16 @@
         functools.partial(conv_kernel, scale),
         out_shape=(
             jax.ShapeDtypeStruct(cotangent.shape, jnp.bfloat16),
-            jax.ShapeDtypeStruct((spread_rows, lanes), jnp.bfloat16),
+            jax.ShapeDtypeStruct((part, lanes), jnp.float32),
+            jax.ShapeDtypeStruct((part, lanes), jnp.bfloat16),
             jax.ShapeDtypeStruct((cells, lanes), jnp.bfloat16),
         ),
-        in_specs=[VMEM] * 5,
-        out_specs=(VMEM,) * 3,
+        in_specs=[SMEM] + [VMEM] * 5,
+        out_specs=(VMEM,) * 4,
         scratch_shapes=[pltpu.VMEM((cells, weight.shape[0]), jnp.bfloat16)],
         compiler_params=BIG,
         name="conv",
-    )(before, volume, after, cotangent, weight)
+    )(place, before, volume, after, cotangent, weight)
 
 
 def convolved_back(pre_grad, flipped, volume):
@@ -286,33 +300,70 @@
     )(pre_grad, flipped)
 
 
-def refreshed(first_row, joined, left_all, right_stat, fan, row_count):
+def add_kernel(keep, got, passing, sent, passed):
+    sent[...] = (keep[...] + got[...].astype(jnp.float32)).astype(jnp.bfloat16)
+
+
+def added(keep, got, passing):
+    far = pl.BlockSpec(memory_space=pl.ANY)
+    return pl.pallas_call(
+        add_kernel,
+        out_shape=(
+            jax.ShapeDtypeStruct(got.shape, jnp.bfloat16),
+            jax.ShapeDtypeStruct(passing.shape, passing.dtype),
+        ),
+        in_specs=[VMEM, VMEM, far],
+        out_specs=(VMEM, far),
+        input_output_aliases={2: 1},
+        name="add",
+    )(keep, got, passing)
+
+
+def packed_rows(rows):
+    count, fan = rows.shape
+    step = (count + 31) // 32 * 32
+    return pl.pallas_call(
+        pack_kernel,
+        out_shape=jax.ShapeDtypeStruct((step, fan // count * step), jnp.bfloat16),
+        in_specs=[VMEM],
+        out_specs=VMEM,
+        compiler_params=BIG,
+        name="pack",
+    )(rows)
+
+
+def refreshed(place, mine, theirs, left_mine, left_theirs, right_stat, fan, count):
     width = right_stat.shape[0]
+    size = left_mine.shape[1]
     return pl.pallas_call(
         refresh_kernel,
         out_shape=(
             jax.ShapeDtypeStruct((fan, width), jnp.float32),
-            jax.ShapeDtypeStruct((row_count, width), jnp.float32),
+            jax.ShapeDtypeStruct((count, width), jnp.float32),
         ),
-        in_specs=[SMEM, VMEM, pl.BlockSpec(memory_space=pl.ANY), VMEM],
+        in_specs=[SMEM] + [VMEM] * 5,
         out_specs=(VMEM, VMEM),
         scratch_shapes=[
-            pltpu.VMEM((fan, fan), jnp.bfloat16),
-            pltpu.VMEM((2, fan, 2 * width), jnp.bfloat16),
-            pltpu.VMEM((DEGREE + 1, fan, width), jnp.float32),
-            pltpu.SemaphoreType.DMA((CHUNKS,)),
+            pltpu.VMEM((size, size), jnp.bfloat16),
+            pltpu.VMEM((size, width), jnp.float32),
+            pltpu.VMEM((size, width), jnp.bfloat16),
+            pltpu.VMEM((2, width + 16, size), jnp.bfloat16),
+            pltpu.VMEM((DEGREE + 1, width, size), jnp.float32),
+            pltpu.VMEM((3 * width, width), jnp.float32),
         ],
         compiler_params=BIG,
         name="refresh",
-    )(first_row, joined, left_all, right_stat)
+    )(place, mine, theirs, left_mine, left_theirs, right_stat)
 
 
 def per_device(volume, weight, cotangent, left_stat, right_stat):
     fan, lanes = weight.shape
     leading, depth, height, wide = volume.shape
-    devices = lax.axis_size(EVERY)
     slabs = lax.axis_size("space")
-    left_all = lax.all_gather(left_stat.astype(jnp.bfloat16), "dp", axis=0, tiled=True)
+    chips = lax.axis_size(("space", "chip"))
+    swap = [(0, 1), (1, 0)]
+    core = lax.axis_index("core")
+    place = jnp.stack([core, lax.axis_index(("chip", "core"))]).astype(jnp.int32)
     onward = [(i, (i + 1) % slabs) for i in range(slabs)]
     back = [((i + 1) % slabs, i) for i in range(slabs)]
 
@@ -321,34 +372,40 @@
 
     before = lax.ppermute(with_plane(cotangent[:, -1:]), "space", onward)
     after = lax.ppermute(with_plane(cotangent[:, :1]), "space", back)
+    left_mine = lax.all_gather(packed_rows(left_stat), "chip", axis=0, tiled=True)
     channels = fan // 27
     flipped = weight.reshape(27, channels, lanes).transpose(0, 2, 1).reshape(27 * lanes, channels)
     flipped = jnp.concatenate([flipped, flipped], axis=1)
     padded_fan = (fan + lanes - 1) // lanes * lanes
     padded = jnp.pad(weight, ((0, padded_fan - fan), (0, 0)))
-    piece = 4 * ((fan + 4 * devices - 1) // (4 * devices))
-    cells = slabs * lax.axis_size("dp") * leading * depth * height * (wide // channels)
-    output, sent, pre_grad = convolved(
-        before, volume, after, cotangent, padded, 1.0 / math.sqrt(cells), piece * devices
-    )
-    terms = lax.all_to_all(sent.reshape(devices, piece, lanes), EVERY, 0, 0)
+    piece = 4 * ((fan + 8 * chips - 1) // (8 * chips))
+    cells = slabs * lax.axis_size(("chip", "core")) * leading * depth * height * (wide // channels)
+    output, keep, give, pre_grad = convolved(
+        place, before, volume, after, cotangent, padded, 1.0 / math.sqrt(cells), piece * chips
+    )
+    got = lax.ppermute(give, "core", swap)
+    sent, left_mine = added(keep, got, left_mine)
+    left_theirs = lax.ppermute(left_mine, "core", swap)
+    terms = lax.all_to_all(sent.reshape(chips, piece, lanes), ("space", "chip"), 0, 0)
     total = jnp.sum(terms.astype(jnp.float32), axis=0).astype(jnp.bfloat16)
-    joined = lax.all_to_all(jnp.broadcast_to(total[None], terms.shape), EVERY, 0, 0)
+    spread = jnp.broadcast_to(total[None], terms.shape)
+    mine = lax.all_to_all(spread, ("space", "chip"), 0, 0).reshape(chips * piece, lanes)
+    theirs = lax.ppermute(mine, "core", swap)
     input_grad = convolved_back(pre_grad, flipped, volume)
-    row_count = left_stat.shape[0]
-    first_row = (lax.axis_index("dp") * row_count).astype(jnp.int32).reshape(1)
     gradient, direction = refreshed(
-        first_row, joined.reshape(devices * piece, lanes), left_all, right_stat, fan, row_count
+        place, mine, theirs, left_mine, left_theirs, right_stat, fan, left_stat.shape[0]
     )
     return output, input_grad, gradient, direction
 
 
 def solution(mesh):
-    placed = (P("dp", "space", None, None), P(), P("dp", "space", None, None), P("dp", None), P())
+    cut = Mesh(mesh.devices.reshape(mesh.shape["space"], -1, 2), ("space", "chip", "core"))
+    parts = ("chip", "core")
+    slab = P(parts, "space", None, None)
     return jax.shard_map(
         per_device,
-        mesh=mesh,
-        in_specs=placed,
-        out_specs=(P("dp", "space", None, None), P("dp", "space", None, None), P(), P("dp", None)),
+        mesh=cut,
+        in_specs=(slab, P(), slab, P(parts, None), P()),
+        out_specs=(slab, slab, P(), P(parts, None)),
         check_vma=False,
     )

time: 145 us -> 178 us (1.23)
  waiting for transfers between devices: 31.4 us -> 62.3 us
  starting transfers between devices: 28 us -> 40 us
  blocking collectives: 38.6 us -> 31.4 us
  local copies, waits for them, and re-layouts: 1.45 us -> 6.88 us
  Pallas kernels: 25.3 us -> 19.9 us
    all_gather x1, waiting for transfers between devices: 9.72 us -> 39.7 us  [per_device(): lax.all_gather(packed_rows(left_stat), 'chip', axis=0, tiled=True)]
    ppermute x0 -> x3, starting transfers between devices: none -> 11.9 us  [the longest x1 5.32 us: per_device(): theirs = lax.ppermute(mine, 'core', swap)]
    ppermute x1, waiting for transfers between devices: 0.01 us -> 11.1 us  [per_device(): before = lax.ppermute(with_plane(cotangent[:, -1:]), 'space', onward)]
    ppermute x1, starting transfers between devices: 7.02 us -> 16.6 us  [per_device(): after = lax.ppermute(with_plane(cotangent[:, :1]), 'space', back)]
    ppermute x1, starting transfers between devices: 11.5 us -> 1.92 us  [per_device(): before = lax.ppermute(with_plane(cotangent[:, -1:]), 'space', onward)]
    all_to_all x1, waiting for transfers between devices: 19.9 us -> 10.4 us  [per_device(): lax.all_to_all(spread, ('space', 'chip'), 0, 0)]
    pallas_call x1, Pallas kernels: 23.1 us -> 14 us  [refreshed(): pl.pallas_call(refresh_kernel, out_shape=(jax.ShapeDtypeStruct((fan, widt...]
    all_to_all x1, blocking collectives: 38.6 us -> 31.4 us  [per_device(): lax.all_to_all(sent.reshape(chips, piece, lanes), ('space', 'chip'), 0, 0)]
  transfers between devices with their start and end apart: 4 -> 7, of which waited for: 3 -> 4; matrix products, arithmetic and copies ran while one was open for 2% -> 3% of each run, Pallas kernels for 2% -> 2%
where the time goes in v3:
time: 178 us; the launch traced here: 177 us
  waiting for transfers between devices  62.3 us (35%)
  starting transfers between devices  40 us (22%)
  blocking collectives  31.4 us (18%)
  Pallas kernels  19.9 us (11%)
  between operations  14.2 us (8%)
  local copies, waits for them, and re-layouts  6.88 us (4%)
  other arithmetic  2.41 us (1%)
    all_gather x1, waiting for transfers between devices, per_device(): lax.all_gather(packed_rows(left_stat), 'chip', axis=0, tiled=True)  39.7 us
    all_to_all x1, blocking collectives, per_device(): lax.all_to_all(sent.reshape(chips, piece, lanes), ('space', 'chip'), 0, 0)  31.4 us
    ppermute x1, starting transfers between devices, per_device(): after = lax.ppermute(with_plane(cotangent[:, :1]), 'space', back)  16.6 us
    pallas_call x1, Pallas kernels, refreshed(): pl.pallas_call(refresh_kernel, out_shape=(jax.ShapeDtypeStruct((fan, widt...  14 us
    ppermute x1, waiting for transfers between devices, per_device(): before = lax.ppermute(with_plane(cotangent[:, -1:]), 'space', onward)  11.1 us
    all_to_all x1, waiting for transfers between devices, per_device(): lax.all_to_all(spread, ('space', 'chip'), 0, 0)  10.4 us
    all_to_all x1, starting transfers between devices, per_device(): lax.all_to_all(spread, ('space', 'chip'), 0, 0)  9.61 us
    ppermute x1, starting transfers between devices, per_device(): theirs = lax.ppermute(mine, 'core', swap)  5.32 us
  transfers between devices with their start and end apart: 7, of which 4 were waited for; matrix products, arithmetic and copies ran while one was open for 3% of the time, Pallas kernels for 2%

profile of v3, /device:TPU:1, one launch (start us, length us, event | category | flops | bytes accessed | tf_op | source)
XLA Modules:
  0.0 177.0 jit_solution(6014999485397778799)
XLA Ops:
  7.2 0.0 all-gather.2.cloned.1.call-start
  7.2 0.0 copy-start.1
  7.2 1.4 copy-done.1
  8.6 0.0 copy-start.3
  8.6 0.0 copy-start.7
  8.6 0.0 copy-start.8
  8.6 1.2 pack.1
  9.9 0.0 all-gather.2.cloned.1.call-update
  9.9 0.0 copy-done.3
  9.9 0.0 copy-done.7
  9.9 16.6 %collective-permute-start.1 = (bf16[1,4,16,256]{3,2,1,0:T(8,128)(2,1)S(1)}, bf16[1,4,16,256]{3,2,1,0:T(8,128)(2,1)S(1)}, u32[]{:S(2)}, u32[]{:S(2)}) collective-permute-start(bf16[1,4,16,256]{3,2,1,0:T(8,128)(2,1)S(1)} %get-tuple-element.24), channel_id=1, source_target_pairs={{8,0},{16,8},{24,16},{32,24},{40,32},{48,40},{56,48},{64,56},{72,6... | collective-permute-start | bytes 98312 | tf_op jit(solution)/shard_map/ppermute | solution.py:374
  26.5 1.9 %collective-permute-start = (bf16[1,4,16,256]{3,2,1,0:T(8,128)(2,1)S(1)}, bf16[1,4,16,256]{3,2,1,0:T(8,128)(2,1)S(1)}, u32[]{:S(2)}, u32[]{:S(2)}) collective-permute-start(bf16[1,4,16,256]{3,2,1,0:T(8,128)(2,1)S(1)} %get-tuple-element.25), channel_id=1, source_target_pairs={{0,8},{8,16},{16,24},{24,32},{32,40},{40,48},{48,56},{56,64},{64,7... | collective-permute-start | bytes 98312 | tf_op jit(solution)/shard_map/ppermute | solution.py:373
  28.4 0.1 pad_add_fusion.place
  28.5 0.0 copy-done.8
  28.6 0.0 collective-permute-done.1.after
  28.6 11.1 %collective-permute-done.before = bf16[1,4,16,256]{3,2,1,0:T(8,128)(2,1)S(1)} collective-permute-done((bf16[1,4,16,256]{3,2,1,0:T(8,128)(2,1)S(1)}, bf16[1,4,16,256]{3,2,1,0:T(8,128)(2,1)S(1)}, u32[]{:S(2)}, u32[]{:S(2)}) %collective-permute-start) | collective-permute-done | bytes 32800 | tf_op jit(solution)/shard_map/ppermute | solution.py:373
  39.6 1.7 conv.1
  41.4 0.0 copy-start.2
  41.4 0.8 copy-done.2
  42.2 0.0 copy-start.5
  42.2 0.6 copy-done.5
  42.8 4.1 %collective-permute-start.2 = (bf16[1024,128]{1,0:T(8,128)(2,1)S(1)}, bf16[1024,128]{1,0:T(8,128)(2,1)S(1)}, u32[]{:S(2)}, u32[]{:S(2)}) collective-permute-start(bf16[1024,128]{1,0:T(8,128)(2,1)S(1)} %get-tuple-element.15), channel_id=1, source_target_pairs={{0,1},{1,0},{2,3},{3,2},{4,5},{5,4},{6,7},{7,6},{8,9},{9,8},{10,11... | collective-permute-start | bytes 786440 | tf_op jit(solution)/shard_map/ppermute | solution.py:386
  46.9 1.1 collective-permute-done.2.got
  48.1 0.0 copy-start.9
  48.1 39.7 %all-gather.2.cloned.1.call-done.passing = bf16[896,1792]{1,0:T(8,128)(2,1)} async-done(((bf16[224,1792]{1,0:T(8,128)(2,1)}), bf16[896,1792]{1,0:T(8,128)(2,1)}) %all-gather.2.cloned.1.call-update) | async-done | bytes 3211280 | tf_op jit(solution)/shard_map/all_gather | solution.py:375
  87.8 0.0 copy-done.9
  87.8 1.9 %add.9 = (bf16[1024,128]{1,0:T(8,128)(2,1)}, bf16[896,1792]{1,0:T(8,128)(2,1)}) custom-call(f32[1024,128]{1,0:T(8,128)} %copy-done.2, bf16[1024,128]{1,0:T(8,128)(2,1)} %copy-done.9, bf16[896,1792]{1,0:T(8,128)(2,1)} %all-gather.2.cloned.1.call-done.passing), custom_call_target="tpu_custom_call", output_to_operand_aliasing={{1}: (2, {})} | custom-call | tf_op jit(solution)/shard_map/add/pallas_call | solution.py:309
  89.6 2.5 %collective-permute-start.4 = (bf16[896,1792]{1,0:T(8,128)(2,1)}, bf16[896,1792]{1,0:T(8,128)(2,1)}, u32[]{:S(2)}, u32[]{:S(2)}) collective-permute-start(bf16[896,1792]{1,0:T(8,128)(2,1)} %get-tuple-element.17.left_mine), channel_id=1, source_target_pairs={{0,1},{1,0},{2,3},{3,2},{4,5},{5,4},{6,7},{7,6},{8,9},{9,8},{10,11... | collective-permute-start | bytes 9633800 | tf_op jit(solution)/shard_map/ppermute | solution.py:388
  92.1 31.4 %all_to_all.10 = bf16[256,4,128]{2,1,0:T(4,128)(2,1)S(1)} all-to-all(bf16[256,4,128]{2,1,0:T(4,128)(2,1)} %bitcast.12), channel_id=1, replica_groups=mesh['space'=64,'chip'=4,'core'=2] {'space','chip'}, dimensions={0} | all-to-all | bytes 524288 | tf_op jit(solution)/shard_map/all_to_all | solution.py:389
  123.5 0.3 reduce_sum.12
  123.7 0.8 broadcast_in_dim.2
  124.5 9.6 %all-to-all-start.1 = ((bf16[256,4,128]{2,1,0:T(4,128)(2,1)}), bf16[256,4,128]{2,1,0:T(4,128)(2,1)S(1)}, u32[]{:S(2)}, u32[]{:S(2)}) async-start(bf16[256,4,128]{2,1,0:T(4,128)(2,1)} %broadcast_in_dim.2), calls=%async_computation.1 | async-start | bytes 524288 | tf_op jit(solution)/shard_map/all_to_all | solution.py:392
  134.1 0.0 copy-start
  134.1 0.0 copy-start.4
  134.2 2.4 %copy.10 = bf16[27,64,128]{1,2,0:T(8,128)(2,1)} copy(bf16[27,64,128]{2,1,0:T(8,128)(2,1)} %bitcast.11) | data formatting | bytes 884736 | tf_op jit(solution)/shard_map/reshape | solution.py:377
  136.5 10.4 %all-to-all-done.1 = bf16[256,4,128]{2,1,0:T(4,128)(2,1)S(1)} async-done(((bf16[256,4,128]{2,1,0:T(4,128)(2,1)}), bf16[256,4,128]{2,1,0:T(4,128)(2,1)S(1)}, u32[]{:S(2)}, u32[]{:S(2)}) %all-to-all-start.1) | async-done | bytes 262176 | tf_op jit(solution)/shard_map/all_to_all | solution.py:392
  146.9 5.3 %collective-permute-start.3 = (bf16[1024,128]{1,0:T(8,128)(2,1)S(1)}, bf16[1024,128]{1,0:T(8,128)(2,1)S(1)}, u32[]{:S(2)}, u32[]{:S(2)}) collective-permute-start(bf16[1024,128]{1,0:T(8,128)(2,1)S(1)} %bitcast.8), channel_id=1, source_target_pairs={{0,1},{1,0},{2,3},{3,2},{4,5},{5,4},{6,7},{7,6},{8,9},{9,8},{10,11... | collective-permute-start | bytes 786440 | tf_op jit(solution)/shard_map/ppermute | solution.py:393
  152.2 2.0 %pad_maximum_fusion.flipped = bf16[3456,128]{1,0:T(8,128)(2,1)S(1)} fusion(bf16[3456,64]{1,0:T(8,128)(2,1)} %bitcast.10), kind=kLoop, calls=%fused_computation | loop fusion | flops 1769472 | bytes 1327104 | tf_op jit(solution)/shard_map/concatenate | solution.py:378
  154.3 0.0 copy-start.6
  154.3 0.8 copy-done.6
  155.1 1.0 conv_back.1
  156.1 0.0 collective-permute-done.3.theirs
  156.1 0.0 collective-permute-done.4.left_theirs
  156.1 0.0 copy-done
  156.1 0.0 copy-done.4
  156.2 14.0 %refresh.1 = (f32[1728,128]{1,0:T(8,128)}, f32[216,128]{1,0:T(8,128)}) custom-call(s32[2]{0:T(128)S(1)} %pad_add_fusion.place, bf16[1024,128]{1,0:T(8,128)(2,1)S(1)} %bitcast.9, bf16[1024,128]{1,0:T(8,128)(2,1)S(1)} %collective-permute-done.3.theirs, bf16[896,1792]{1,0:T(8,128)(2,1)S(1)} %copy-done, bf16[896,1792]{1,0:T(8,128)(2,1)} %collective-permute-done.4.left_theirs, ...), custom_call_target="tpu_custom_call" | custom-call | tf_op jit(solution)/shard_map/refresh/pallas_call | solution.py:338
  (3 shorter events, 0.0 us)
Async XLA Ops:
  7.2 80.6 %all-gather.2.cloned.1.call-start = ((), (), s32[]{:S(2)}) async-start(), calls=%async_computation.2 | async-start | bytes 4014080 | tf_op jit(solution)/shard_map/all_gather | solution.py:375
  7.2 1.4 copy-start.1
  8.6 1.3 copy-start.3
  8.6 1.3 copy-start.7
  8.6 19.9 %copy-start.8 = (bf16[1728,128]{1,0:T(8,128)(2,1)S(1)}, bf16[1728,128]{1,0:T(8,128)(2,1)}, u32[]{:S(2)}) copy-start(bf16[1728,128]{1,0:T(8,128)(2,1)} %param.6) | copy-start | bytes 1327108
  9.9 18.6 %collective-permute-start.1 = (bf16[1,4,16,256]{3,2,1,0:T(8,128)(2,1)S(1)}, bf16[1,4,16,256]{3,2,1,0:T(8,128)(2,1)S(1)}, u32[]{:S(2)}, u32[]{:S(2)}) collective-permute-start(bf16[1,4,16,256]{3,2,1,0:T(8,128)(2,1)S(1)} %get-tuple-element.24), channel_id=1, source_target_pairs={{8,0},{16,8},{24,16},{32,24},{40,32},{48,40},{56,48},{64,56},{72,6... | collective-permute-start | bytes 98312 | tf_op jit(solution)/shard_map/ppermute | solution.py:374
  26.5 13.1 %collective-permute-start = (bf16[1,4,16,256]{3,2,1,0:T(8,128)(2,1)S(1)}, bf16[1,4,16,256]{3,2,1,0:T(8,128)(2,1)S(1)}, u32[]{:S(2)}, u32[]{:S(2)}) collective-permute-start(bf16[1,4,16,256]{3,2,1,0:T(8,128)(2,1)S(1)} %get-tuple-element.25), channel_id=1, source_target_pairs={{0,8},{8,16},{16,24},{24,32},{32,40},{40,48},{48,56},{56,64},{64,7... | collective-permute-start | bytes 98312 | tf_op jit(solution)/shard_map/ppermute | solution.py:373
  41.4 0.8 copy-start.2
  42.2 0.6 copy-start.5
  42.8 5.3 %collective-permute-start.2 = (bf16[1024,128]{1,0:T(8,128)(2,1)S(1)}, bf16[1024,128]{1,0:T(8,128)(2,1)S(1)}, u32[]{:S(2)}, u32[]{:S(2)}) collective-permute-start(bf16[1024,128]{1,0:T(8,128)(2,1)S(1)} %get-tuple-element.15), channel_id=1, source_target_pairs={{0,1},{1,0},{2,3},{3,2},{4,5},{5,4},{6,7},{7,6},{8,9},{9,8},{10,11... | collective-permute-start | bytes 786440 | tf_op jit(solution)/shard_map/ppermute | solution.py:386
  48.1 39.7 %copy-start.9 = (bf16[1024,128]{1,0:T(8,128)(2,1)}, bf16[1024,128]{1,0:T(8,128)(2,1)S(1)}, u32[]{:S(2)}) copy-start(bf16[1024,128]{1,0:T(8,128)(2,1)S(1)} %collective-permute-done.2.got) | copy-start | bytes 786436
  89.6 66.5 %collective-permute-start.4 = (bf16[896,1792]{1,0:T(8,128)(2,1)}, bf16[896,1792]{1,0:T(8,128)(2,1)}, u32[]{:S(2)}, u32[]{:S(2)}) collective-permute-start(bf16[896,1792]{1,0:T(8,128)(2,1)} %get-tuple-element.17.left_mine), channel_id=1, source_target_pairs={{0,1},{1,0},{2,3},{3,2},{4,5},{5,4},{6,7},{7,6},{8,9},{9,8},{10,11... | collective-permute-start | bytes 9633800 | tf_op jit(solution)/shard_map/ppermute | solution.py:388
  124.5 22.4 %all-to-all-start.1 = ((bf16[256,4,128]{2,1,0:T(4,128)(2,1)}), bf16[256,4,128]{2,1,0:T(4,128)(2,1)S(1)}, u32[]{:S(2)}, u32[]{:S(2)}) async-start(bf16[256,4,128]{2,1,0:T(4,128)(2,1)} %broadcast_in_dim.2), calls=%async_computation.1 | async-start | bytes 524288 | tf_op jit(solution)/shard_map/all_to_all | solution.py:392
  134.1 22.0 %copy-start = (bf16[896,1792]{1,0:T(8,128)(2,1)S(1)}, bf16[896,1792]{1,0:T(8,128)(2,1)}, u32[]{:S(2)}) copy-start(bf16[896,1792]{1,0:T(8,128)(2,1)} %get-tuple-element.17.left_mine) | copy-start | bytes 9633796
  134.1 22.0 %copy-start.4 = (f32[128,128]{1,0:T(8,128)S(1)}, f32[128,128]{1,0:T(8,128)}, u32[]{:S(2)}) copy-start(f32[128,128]{1,0:T(8,128)} %right_stat.1) | copy-start | bytes 196612
  146.9 9.2 %collective-permute-start.3 = (bf16[1024,128]{1,0:T(8,128)(2,1)S(1)}, bf16[1024,128]{1,0:T(8,128)(2,1)S(1)}, u32[]{:S(2)}, u32[]{:S(2)}) collective-permute-start(bf16[1024,128]{1,0:T(8,128)(2,1)S(1)} %bitcast.8), channel_id=1, source_target_pairs={{0,1},{1,0},{2,3},{3,2},{4,5},{5,4},{6,7},{7,6},{8,9},{9,8},{10,11... | collective-permute-start | bytes 786440 | tf_op jit(solution)/shard_map/ppermute | solution.py:393
  154.3 0.8 copy-start.6
Sparse Core Ops, SparseCore 0:
  10.7 77.0 all-gather.1

commit v4 on v3

--- a/solution.py
+++ b/solution.py
@@ -14,7 +14,10 @@
 DECAY = 0.9
 VMEM = pl.BlockSpec(memory_space=pltpu.VMEM)
 SMEM = pl.BlockSpec(memory_space=pltpu.SMEM)
-BIG = pltpu.CompilerParams(vmem_limit_bytes=48 * 1024 * 1024)
+
+
+def room(mebibytes):
+    return pltpu.CompilerParams(vmem_limit_bytes=mebibytes * 1024 * 1024)
 
 
 def offset_list():
@@ -173,16 +176,46 @@
     return (low + sharp_dot(cube, high)) * lax.rsqrt(jnp.sqrt(largest))
 
 
-def pack_kernel(rows, packed):
+def pack_kernel(rows, *halves):
     count, fan = rows.shape
-    spare = packed.shape[0] - count
-    gap = jnp.zeros((count, spare), jnp.float32)
+    part = halves[0].shape[0]
+    spare = len(halves) * part - count
+    held = jnp.concatenate([rows[...], jnp.zeros((spare, fan), jnp.float32)], axis=0)
+    gap = jnp.zeros((held.shape[0], spare), jnp.float32)
     pieces = []
     for start in range(0, fan, count):
-        pieces.extend([rows[:, start : start + count], gap])
-    wide = jnp.concatenate(pieces, axis=1)
-    tall = jnp.concatenate([wide, jnp.zeros((spare, wide.shape[1]), jnp.float32)], axis=0)
-    packed[...] = tall.astype(jnp.bfloat16)
+        pieces.extend([held[:, start : start + count], gap])
+    packed = jnp.concatenate(pieces, axis=1).astype(jnp.bfloat16)
+    for k, half in enumerate(halves):
+        half[...] = packed[k * part : (k + 1) * part, :]
+
+
+def flip_kernel(weight, flipped):
+    lanes = weight.shape[1]
+    half = lanes // 2
+    low = lax.broadcasted_iota(jnp.int32, (1, lanes), 1) < half
+    for j in range(weight.shape[0] // lanes):
+        both = jnp.transpose(weight[j * lanes : (j + 1) * lanes, :].astype(jnp.float32))
+        turned = jnp.concatenate([both[:, half:], both[:, :half]], axis=1)
+        pair = (jnp.where(low, both, turned), jnp.where(low, turned, both))
+        for side in range(2):
+            first = (2 * j + side) * lanes
+            if first < flipped.shape[0]:
+                flipped[first : first + lanes, :] = pair[side].astype(jnp.bfloat16)
+
+
+def add_kernel(keep, got, sent):
+    sent[...] = (keep[...] + got[...].astype(jnp.float32)).astype(jnp.bfloat16)
+
+
+def spread_kernel(piece, terms, spread):
+    rows, lanes = terms.shape
+    total = jnp.sum(terms[...].astype(jnp.float32).reshape(rows // 8, 8, lanes), axis=0)
+    folded = total[:piece]
+    for first in range(piece, 8, piece):
+        folded = folded + total[first : first + piece]
+    again = jnp.concatenate([folded] * (8 // piece), axis=0)
+    spread[...] = jnp.broadcast_to(again[None], (rows // 8, 8, lanes)).reshape(rows, lanes).astype(jnp.bfloat16)
 
 
 def refresh_kernel(
@@ -206,12 +239,26 @@
     tall = spaced[...].astype(jnp.bfloat16)
     tall_ref[...] = tall
     flat = jnp.transpose(spaced[...]).astype(jnp.bfloat16)
+    right_full = DECAY * right_stat[...] + jnp.dot(flat, tall, preferred_element_type=jnp.float32)
+    root = right_root_of(right_full, coeffs)
+    root_high = root.astype(jnp.bfloat16)
+    root_low = (root - root_high.astype(jnp.float32)).astype(jnp.bfloat16)
+    parts = jnp.dot(
+        jnp.concatenate([root_high, root_low], axis=0), flat, preferred_element_type=jnp.float32
+    )
+    carried = parts[:width] + parts[width:]
+    powers[0] = carried
+    vectors = block.shape[1] - width
+    first_row = lax.broadcasted_iota(jnp.int32, (vectors, left.shape[0]), 0) == 0
+    block[0, :width, :] = carried.astype(jnp.bfloat16)
+    block[0, width:, :] = jnp.where(first_row, 1.0 / math.sqrt(fan), 0.0).astype(jnp.bfloat16)
     for source, side in ((left_mine, core), (left_theirs, 1 - core)):
 
-        def add_gradient(chip, _, source=source, side=side):
+        def add_gradient(turn, _, source=source, side=side):
+            chip = lax.rem(place[1] // 2 + blocks // 2 - turn, blocks // 2)
             rows = pl.ds(pl.multiple_of((2 * chip + side) * step, step), step)
             outer = jnp.dot(tall_ref[rows, :], flat, preferred_element_type=jnp.float32)
-            held = source[pl.ds(pl.multiple_of(chip * step, step), step), :].astype(jnp.float32)
+            held = source[pl.ds(pl.multiple_of(turn * step, step), step), :].astype(jnp.float32)
             left[rows, :] = (DECAY * held + outer).astype(jnp.bfloat16)
             return 0
 
@@ -221,19 +268,6 @@
         square = left[start : start + width, start : start + width]
         trace = trace + diagonal_sum(square.astype(jnp.float32))
     inverse = 1.0 / trace
-    right_full = DECAY * right_stat[...] + jnp.dot(flat, tall, preferred_element_type=jnp.float32)
-    root = right_root_of(right_full, coeffs)
-    root_high = root.astype(jnp.bfloat16)
-    root_low = (root - root_high.astype(jnp.float32)).astype(jnp.bfloat16)
-    parts = jnp.dot(
-        jnp.concatenate([root_high, root_low], axis=0), flat, preferred_element_type=jnp.float32
-    )
-    carried = parts[:width] + parts[width:]
-    powers[0] = carried
-    vectors = block.shape[1] - width
-    first_row = lax.broadcasted_iota(jnp.int32, (vectors, left.shape[0]), 0) == 0
-    block[0, :width, :] = carried.astype(jnp.bfloat16)
-    block[0, width:, :] = jnp.where(first_row, 1.0 / math.sqrt(fan), 0.0).astype(jnp.bfloat16)
     squares = {}
     for degree in range(1, DEGREE + 1):
         product = inverse * jnp.dot(
@@ -277,7 +311,7 @@
         in_specs=[SMEM] + [VMEM] * 5,
         out_specs=(VMEM,) * 4,
         scratch_shapes=[pltpu.VMEM((cells, weight.shape[0]), jnp.bfloat16)],
-        compiler_params=BIG,
+        compiler_params=room(12),
         name="conv",
     )(place, before, volume, after, cotangent, weight)
 
@@ -292,7 +326,7 @@
         in_specs=[VMEM] * 2,
         out_specs=VMEM,
         scratch_shapes=[pltpu.VMEM((own, flipped.shape[0]), jnp.bfloat16)],
-        compiler_params=BIG,
+        compiler_params=room(8),
         cost_estimate=pl.CostEstimate(
             flops=2 * own * flipped.size, bytes_accessed=2 * own * flipped.shape[0], transcendentals=0
         ),
@@ -300,23 +334,38 @@
     )(pre_grad, flipped)
 
 
-def add_kernel(keep, got, passing, sent, passed):
-    sent[...] = (keep[...] + got[...].astype(jnp.float32)).astype(jnp.bfloat16)
-
-
-def added(keep, got, passing):
-    far = pl.BlockSpec(memory_space=pl.ANY)
+def added(keep, got):
     return pl.pallas_call(
         add_kernel,
-        out_shape=(
-            jax.ShapeDtypeStruct(got.shape, jnp.bfloat16),
-            jax.ShapeDtypeStruct(passing.shape, passing.dtype),
-        ),
-        in_specs=[VMEM, VMEM, far],
-        out_specs=(VMEM, far),
-        input_output_aliases={2: 1},
+        out_shape=jax.ShapeDtypeStruct(got.shape, jnp.bfloat16),
+        in_specs=[VMEM, VMEM],
+        out_specs=VMEM,
+        compiler_params=room(4),
         name="add",
-    )(keep, got, passing)
+    )(keep, got)
+
+
+def summed(terms, piece):
+    return pl.pallas_call(
+        functools.partial(spread_kernel, piece),
+        out_shape=jax.ShapeDtypeStruct(terms.shape, jnp.bfloat16),
+        in_specs=[VMEM],
+        out_specs=VMEM,
+        compiler_params=room(4),
+        name="sum",
+    )(terms)
+
+
+def flipped_taps(weight, taps):
+    lanes = weight.shape[1]
+    return pl.pallas_call(
+        flip_kernel,
+        out_shape=jax.ShapeDtypeStruct((taps * lanes, lanes), jnp.bfloat16),
+        in_specs=[VMEM],
+        out_specs=VMEM,
+        compiler_params=room(8),
+        name="flip",
+    )(weight)
 
 
 def packed_rows(rows):
@@ -324,10 +373,10 @@
     step = (count + 31) // 32 * 32
     return pl.pallas_call(
         pack_kernel,
-        out_shape=jax.ShapeDtypeStruct((step, fan // count * step), jnp.bfloat16),
+        out_shape=(jax.ShapeDtypeStruct((step // 2, fan // count * step), jnp.bfloat16),) * 2,
         in_specs=[VMEM],
-        out_specs=VMEM,
-        compiler_params=BIG,
+        out_specs=(VMEM,) * 2,
+        compiler_params=room(16),
         name="pack",
     )(rows)
 
@@ -351,7 +400,7 @@
             pltpu.VMEM((DEGREE + 1, width, size), jnp.float32),
             pltpu.VMEM((3 * width, width), jnp.float32),
         ],
-        compiler_params=BIG,
+        compiler_params=room(32),
         name="refresh",
     )(place, mine, theirs, left_mine, left_theirs, right_stat)
 
@@ -359,39 +408,52 @@
 def per_device(volume, weight, cotangent, left_stat, right_stat):
     fan, lanes = weight.shape
     leading, depth, height, wide = volume.shape
-    slabs = lax.axis_size("space")
-    chips = lax.axis_size(("space", "chip"))
+    space = ("plane", "side")
+    slabs = lax.axis_size(space)
+    chips = lax.axis_size(space + ("chip",))
     swap = [(0, 1), (1, 0)]
     core = lax.axis_index("core")
-    place = jnp.stack([core, lax.axis_index(("chip", "core"))]).astype(jnp.int32)
+    place = jnp.stack([core, lax.axis_index(("chip", "core"))])
+    place = place.astype(jnp.int32)
     onward = [(i, (i + 1) % slabs) for i in range(slabs)]
     back = [((i + 1) % slabs, i) for i in range(slabs)]
 
     def with_plane(plane):
         return jnp.concatenate([volume, plane[..., :wide], plane[..., wide:]], axis=1)
 
-    before = lax.ppermute(with_plane(cotangent[:, -1:]), "space", onward)
-    after = lax.ppermute(with_plane(cotangent[:, :1]), "space", back)
-    left_mine = lax.all_gather(packed_rows(left_stat), "chip", axis=0, tiled=True)
-    channels = fan // 27
-    flipped = weight.reshape(27, channels, lanes).transpose(0, 2, 1).reshape(27 * lanes, channels)
-    flipped = jnp.concatenate([flipped, flipped], axis=1)
+    before = lax.ppermute(with_plane(cotangent[:, -1:]), space, onward)
+    after = lax.ppermute(with_plane(cotangent[:, :1]), space, back)
     padded_fan = (fan + lanes - 1) // lanes * lanes
     padded = jnp.pad(weight, ((0, padded_fan - fan), (0, 0)))
+    flipped = flipped_taps(padded, 27)
     piece = 4 * ((fan + 8 * chips - 1) // (8 * chips))
-    cells = slabs * lax.axis_size(("chip", "core")) * leading * depth * height * (wide // channels)
+    cells = slabs * lax.axis_size(("chip", "core")) * leading * depth * height * (wide // (fan // 27))
     output, keep, give, pre_grad = convolved(
         place, before, volume, after, cotangent, padded, 1.0 / math.sqrt(cells), piece * chips
     )
     got = lax.ppermute(give, "core", swap)
-    sent, left_mine = added(keep, got, left_mine)
+    sent = added(keep, got)
+    column = ("side", "chip")
+    levels = lax.axis_size(column)
+
+    def risen(rows, by):
+        return lax.ppermute(rows, column, [(i, (i + by) % levels) for i in range(levels)])
+
+    sent, own = lax.optimization_barrier((sent, packed_rows(left_stat)))
+    terms = lax.all_to_all(sent.reshape(chips, piece, lanes), space + ("chip",), 0, 0)
+    lower = [risen(half, 1) for half in own]
+    upper = [risen(half, -1) for half in own]
+    spread = summed(terms.reshape(chips * piece, lanes), piece)
+    mine = lax.all_to_all(spread.reshape(chips, piece, lanes), space + ("chip",), 0, 0)
+    lower[0], lower[1], upper[0], upper[1] = lax.optimization_barrier((*lower, *upper))
+    far = [risen(lower[0], 1), risen(upper[1], -1)]
+    input_grad = convolved_back(pre_grad, flipped, volume)
+    mine, input_grad, *lefts = lax.optimization_barrier(
+        (mine.reshape(chips * piece, lanes), input_grad, *own, *lower, *far, *upper)
+    )
+    theirs = lax.ppermute(mine, "core", swap)
+    left_mine = jnp.concatenate(lefts, axis=0)
     left_theirs = lax.ppermute(left_mine, "core", swap)
-    terms = lax.all_to_all(sent.reshape(chips, piece, lanes), ("space", "chip"), 0, 0)
-    total = jnp.sum(terms.astype(jnp.float32), axis=0).astype(jnp.bfloat16)
-    spread = jnp.broadcast_to(total[None], terms.shape)
-    mine = lax.all_to_all(spread, ("space", "chip"), 0, 0).reshape(chips * piece, lanes)
-    theirs = lax.ppermute(mine, "core", swap)
-    input_grad = convolved_back(pre_grad, flipped, volume)
     gradient, direction = refreshed(
         place, mine, theirs, left_mine, left_theirs, right_stat, fan, left_stat.shape[0]
     )
@@ -399,12 +461,13 @@
 
 
 def solution(mesh):
-    cut = Mesh(mesh.devices.reshape(mesh.shape["space"], -1, 2), ("space", "chip", "core"))
-    parts = ("chip", "core")
-    slab = P(parts, "space", None, None)
+    slabs = mesh.shape["space"]
+    cut = mesh.devices.reshape(slabs // 2, 2, -1, 2)
+    space, parts = ("plane", "side"), ("chip", "core")
+    slab = P(parts, space, None, None)
     return jax.shard_map(
         per_device,
-        mesh=cut,
+        mesh=Mesh(cut, space + parts),
         in_specs=(slab, P(), slab, P(parts, None), P()),
         out_specs=(slab, slab, P(), P(parts, None)),
         check_vma=False,

time: 178 us -> 122 us (0.69)
  waiting for transfers between devices: 62.3 us -> 15.6 us
  starting transfers between devices: 40 us -> 77.7 us
  blocking collectives: 31.4 us -> 0 us
  between operations: 14.2 us -> 0.89 us
    all_gather x1 -> x0, waiting for transfers between devices: 39.7 us -> none  [per_device(): lax.all_gather(packed_rows(left_stat), 'chip', axis=0, tiled=True)]
    all_to_all x1 -> x0, blocking collectives: 31.4 us -> none  [per_device(): lax.all_to_all(sent.reshape(chips, piece, lanes), ('space', 'chip'), 0, 0)]
    all_to_all x1 -> x2, starting transfers between devices: 9.61 us -> 32 us  [the longest x1 16.4 us: per_device(): lax.all_to_all(sent.reshape(chips, piece, lanes), space + ('chip',), 0, 0)]
    ppermute x2 -> x8, starting transfers between devices: 18.5 us -> 36.7 us  [the longest x6 18.3 us: risen(): lax.ppermute(rows, column, [(i, (i + by) % levels) for i in range(levels)])]
    all_to_all x1 -> x2, waiting for transfers between devices: 10.4 us -> 2.28 us  [the longest x1 2.28 us: per_device(): lax.all_to_all(sent.reshape(chips, piece, lanes), space + ('chip',), 0, 0)]
    ppermute x1, waiting for transfers between devices: 0.01 us -> 3.62 us  [per_device(): theirs = lax.ppermute(mine, 'core', swap)]
    ppermute x1, starting transfers between devices: 5.32 us -> 2.1 us  [per_device(): theirs = lax.ppermute(mine, 'core', swap)]
    reshape x1 -> x0, local copies, waits for them, and re-layouts: 2.39 us -> none  [per_device(): weight.reshape(27, channels, lanes).transpose(0, 2, 1)]
  transfers between devices with their start and end apart: 7 -> 13, of which waited for: 4 -> 4; matrix products, arithmetic and copies ran while one was open for 3% -> 1% of each run, Pallas kernels for 2% -> 2%
where the time goes in v4:
time: 122 us; the launch traced here: 121 us
  starting transfers between devices  77.7 us (64%)
  Pallas kernels  18.2 us (15%)
  waiting for transfers between devices  15.6 us (13%)
  local copies, waits for them, and re-layouts  7.48 us (6%)
    ppermute x6, starting transfers between devices, risen(): lax.ppermute(rows, column, [(i, (i + by) % levels) for i in range(levels)])  18.3 us
    all_to_all x1, starting transfers between devices, per_device(): lax.all_to_all(sent.reshape(chips, piece, lanes), space + ('chip',), 0, 0)  16.4 us
    all_to_all x1, starting transfers between devices, per_device(): lax.all_to_all(spread.reshape(chips, piece, lanes), space + ('chip',), 0, 0)  15.6 us
    pallas_call x1, Pallas kernels, refreshed(): pl.pallas_call(refresh_kernel, out_shape=(jax.ShapeDtypeStruct((fan, widt...  13 us
    ppermute x1, starting transfers between devices, per_device(): before = lax.ppermute(with_plane(cotangent[:, -1:]), space, onward)  11.5 us
    ppermute x6, waiting for transfers between devices, risen(): lax.ppermute(rows, column, [(i, (i + by) % levels) for i in range(levels)])  9.02 us
    ppermute x1, starting transfers between devices, per_device(): after = lax.ppermute(with_plane(cotangent[:, :1]), space, back)  7.02 us
    unnamed x19, local copies, waits for them, and re-layouts  5.65 us
  transfers between devices with their start and end apart: 13, of which 4 were waited for; matrix products, arithmetic and copies ran while one was open for 1% of the time, Pallas kernels for 2%

profile of v4, /device:TPU:1, one launch (start us, length us, event | category | flops | bytes accessed | tf_op | source)
XLA Modules:
  0.0 120.7 jit_solution(5936880330588249932)
XLA Ops:
  0.6 0.8 fusion.2
  1.4 0.7 fusion.1
  2.1 11.5 %collective-permute-start = (bf16[1,4,16,256]{3,2,1,0:T(8,128)(2,1)S(1)}, bf16[1,4,16,256]{3,2,1,0:T(8,128)(2,1)S(1)}, u32[]{:S(2)}, u32[]{:S(2)}) collective-permute-start(bf16[1,4,16,256]{3,2,1,0:T(8,128)(2,1)S(1)} %get-tuple-element.59), channel_id=1, source_target_pairs={{0,8},{8,16},{16,24},{24,32},{32,40},{40,48},{48,56},{56,64},{64,7... | collective-permute-start | bytes 98312 | tf_op jit(solution)/shard_map/ppermute | solution.py:424
  13.6 7.0 %collective-permute-start.1 = (bf16[1,4,16,256]{3,2,1,0:T(8,128)(2,1)S(1)}, bf16[1,4,16,256]{3,2,1,0:T(8,128)(2,1)S(1)}, u32[]{:S(2)}, u32[]{:S(2)}) collective-permute-start(bf16[1,4,16,256]{3,2,1,0:T(8,128)(2,1)S(1)} %get-tuple-element.58), channel_id=1, source_target_pairs={{8,0},{16,8},{24,16},{32,24},{40,32},{48,40},{56,48},{64,56},{72,6... | collective-permute-start | bytes 98312 | tf_op jit(solution)/shard_map/ppermute | solution.py:425
  20.6 0.1 pad_add_fusion.place
  20.7 1.0 pad.4.weight
  21.7 0.0 collective-permute-done.before
  21.7 0.7 collective-permute-done.1.after
  22.4 0.0 copy-start.1
  22.4 0.8 copy-done.1
  23.2 0.0 copy-start.3
  23.2 0.7 copy-done.3
  23.9 1.7 %conv.1 = (bf16[1,2,16,512]{3,2,1,0:T(8,128)(2,1)}, f32[1024,128]{1,0:T(8,128)S(1)}, bf16[1024,128]{1,0:T(8,128)(2,1)S(1)}, bf16[256,128]{1,0:T(8,128)(2,1)S(1)}) custom-call(s32[2]{0:T(128)S(1)} %pad_add_fusion.place, bf16[1,4,16,256]{3,2,1,0:T(8,128)(2,1)S(1)} %collective-permute-done.before, bf16[1,2,16,256]{3,2,1,0:T(8,128)(2,1)S(1)} %copy-done.3, ...), custom_call_target="tpu_custom_call" | custom-call | tf_op jit(solution)/shard_map/conv/pallas_call | solution.py:303
  25.6 4.0 %collective-permute-start.2 = (bf16[1024,128]{1,0:T(8,128)(2,1)S(1)}, bf16[1024,128]{1,0:T(8,128)(2,1)S(1)}, u32[]{:S(2)}, u32[]{:S(2)}) collective-permute-start(bf16[1024,128]{1,0:T(8,128)(2,1)S(1)} %get-tuple-element.31), channel_id=1, source_target_pairs={{0,1},{1,0},{2,3},{3,2},{4,5},{5,4},{6,7},{7,6},{8,9},{9,8},{10,11... | collective-permute-start | bytes 786440 | tf_op jit(solution)/shard_map/ppermute | solution.py:434
  29.7 0.0 copy-start
  29.7 1.4 %copy-done = f32[216,1728]{1,0:T(8,128)S(1)} copy-done((f32[216,1728]{1,0:T(8,128)S(1)}, f32[216,1728]{1,0:T(8,128)}, u32[]{:S(2)}) %copy-start) | copy-done | bytes 1493016
  31.1 0.4 pack.1
  31.4 0.0 collective-permute-done.2.got
  31.4 0.8 add.9
  32.2 16.4 %all-to-all-start = ((bf16[256,4,128]{2,1,0:T(4,128)(2,1)}), bf16[256,4,128]{2,1,0:T(4,128)(2,1)S(1)}, u32[]{:S(2)}, u32[]{:S(2)}) async-start(bf16[256,4,128]{2,1,0:T(4,128)(2,1)} %bitcast.2), calls=%async_computation | async-start | bytes 524288 | tf_op jit(solution)/shard_map/all_to_all | solution.py:443
  48.6 1.9 %collective-permute-start.3 = (bf16[112,1792]{1,0:T(8,128)(2,1)S(1)}, bf16[112,1792]{1,0:T(8,128)(2,1)S(1)}, u32[]{:S(2)}, u32[]{:S(2)}) collective-permute-start(bf16[112,1792]{1,0:T(8,128)(2,1)S(1)} %get-tuple-element.44), channel_id=1, source_target_pairs={{0,2},{2,4},{4,6},{6,8},{8,10},{10,12},{12,14},{14,0},{1,3},{3,5},... | collective-permute-start | bytes 1204232 | tf_op jit(solution)/shard_map/ppermute | solution.py:440
  50.5 2.8 %collective-permute-start.4 = (bf16[112,1792]{1,0:T(8,128)(2,1)S(1)}, bf16[112,1792]{1,0:T(8,128)(2,1)S(1)}, u32[]{:S(2)}, u32[]{:S(2)}) collective-permute-start(bf16[112,1792]{1,0:T(8,128)(2,1)S(1)} %get-tuple-element.45), channel_id=1, source_target_pairs={{0,2},{2,4},{4,6},{6,8},{8,10},{10,12},{12,14},{14,0},{1,3},{3,5},... | collective-permute-start | bytes 1204232 | tf_op jit(solution)/shard_map/ppermute | solution.py:440
  53.3 3.7 %collective-permute-start.5 = (bf16[112,1792]{1,0:T(8,128)(2,1)S(1)}, bf16[112,1792]{1,0:T(8,128)(2,1)S(1)}, u32[]{:S(2)}, u32[]{:S(2)}) collective-permute-start(bf16[112,1792]{1,0:T(8,128)(2,1)S(1)} %get-tuple-element.44), channel_id=1, source_target_pairs={{0,14},{2,0},{4,2},{6,4},{8,6},{10,8},{12,10},{14,12},{1,15},{3,1}... | collective-permute-start | bytes 1204232 | tf_op jit(solution)/shard_map/ppermute | solution.py:440
  57.0 3.4 %collective-permute-start.6 = (bf16[112,1792]{1,0:T(8,128)(2,1)S(1)}, bf16[112,1792]{1,0:T(8,128)(2,1)S(1)}, u32[]{:S(2)}, u32[]{:S(2)}) collective-permute-start(bf16[112,1792]{1,0:T(8,128)(2,1)S(1)} %get-tuple-element.45), channel_id=1, source_target_pairs={{0,14},{2,0},{4,2},{6,4},{8,6},{10,8},{12,10},{14,12},{1,15},{3,1}... | collective-permute-start | bytes 1204232 | tf_op jit(solution)/shard_map/ppermute | solution.py:440
  60.4 2.3 %all-to-all-done = bf16[256,4,128]{2,1,0:T(4,128)(2,1)S(1)} async-done(((bf16[256,4,128]{2,1,0:T(4,128)(2,1)}), bf16[256,4,128]{2,1,0:T(4,128)(2,1)S(1)}, u32[]{:S(2)}, u32[]{:S(2)}) %all-to-all-start) | async-done | bytes 262176 | tf_op jit(solution)/shard_map/all_to_all | solution.py:443
  62.7 0.9 sum.1
  63.5 15.6 %all-to-all-start.1 = ((bf16[256,4,128]{2,1,0:T(4,128)(2,1)}), bf16[256,4,128]{2,1,0:T(4,128)(2,1)S(1)}, u32[]{:S(2)}, u32[]{:S(2)}) async-start(bf16[256,4,128]{2,1,0:T(4,128)(2,1)} %bitcast.4), calls=%async_computation.1 | async-start | bytes 524288 | tf_op jit(solution)/shard_map/all_to_all | solution.py:447
  79.1 0.0 collective-permute-done.3
  79.1 0.0 collective-permute-done.4
  79.1 0.0 collective-permute-done.5
  79.1 0.0 collective-permute-done.6
  79.2 1.9 %collective-permute-start.7 = (bf16[112,1792]{1,0:T(8,128)(2,1)S(1)}, bf16[112,1792]{1,0:T(8,128)(2,1)S(1)}, u32[]{:S(2)}, u32[]{:S(2)}) collective-permute-start(bf16[112,1792]{1,0:T(8,128)(2,1)S(1)} %collective-permute-done.3), channel_id=1, source_target_pairs={{0,2},{2,4},{4,6},{6,8},{8,10},{10,12},{12,14},{14,0},{1,3},{3,5},... | collective-permute-start | bytes 1204232 | tf_op jit(solution)/shard_map/ppermute | solution.py:440
  81.1 4.6 %collective-permute-start.8 = (bf16[112,1792]{1,0:T(8,128)(2,1)S(1)}, bf16[112,1792]{1,0:T(8,128)(2,1)}, u32[]{:S(2)}, u32[]{:S(2)}) collective-permute-start(bf16[112,1792]{1,0:T(8,128)(2,1)S(1)} %collective-permute-done.6), channel_id=1, source_target_pairs={{0,14},{2,0},{4,2},{6,4},{8,6},{10,8},{12,10},{14,12},{1,15},{3,1}... | collective-permute-start | bytes 1204232 | tf_op jit(solution)/shard_map/ppermute | solution.py:440
  85.7 0.5 flip.1.flipped
  86.1 1.0 conv_back.1
  87.2 9.0 %collective-permute-done.7 = bf16[112,1792]{1,0:T(8,128)(2,1)S(1)} collective-permute-done((bf16[112,1792]{1,0:T(8,128)(2,1)S(1)}, bf16[112,1792]{1,0:T(8,128)(2,1)S(1)}, u32[]{:S(2)}, u32[]{:S(2)}) %collective-permute-start.7) | collective-permute-done | bytes 401440 | tf_op jit(solution)/shard_map/ppermute | solution.py:440
  96.2 0.7 copy-done.4
  96.9 0.0 collective-permute-done.8
  96.9 0.0 all-to-all-done.1
  96.9 0.0 copy-start.2
  97.1 0.8 copy-done.5
  97.9 1.0 constant_dynamic-update-slice_fusion.2
  99.0 2.9 %collective-permute-start.10 = (bf16[896,1792]{1,0:T(8,128)(2,1)S(1)}, bf16[896,1792]{1,0:T(8,128)(2,1)S(1)}, u32[]{:S(2)}, u32[]{:S(2)}) collective-permute-start(bf16[896,1792]{1,0:T(8,128)(2,1)S(1)} %constant_dynamic-update-slice_fusion.left_mine), channel_id=1, source_target_pairs={{0,1},{1,0},{2,3},{3,2},{4,5},{5,4},{6,7},{7,6},{8,9},{9,8},{10,11... | collective-permute-start | bytes 9633800 | tf_op jit(solution)/shard_map/ppermute | solution.py:456
  101.9 2.1 %collective-permute-start.9 = (bf16[1024,128]{1,0:T(8,128)(2,1)S(1)}, bf16[1024,128]{1,0:T(8,128)(2,1)S(1)}, u32[]{:S(2)}, u32[]{:S(2)}) collective-permute-start(bf16[1024,128]{1,0:T(8,128)(2,1)S(1)} %bitcast.6), channel_id=1, source_target_pairs={{0,1},{1,0},{2,3},{3,2},{4,5},{5,4},{6,7},{7,6},{8,9},{9,8},{10,11... | collective-permute-start | bytes 786440 | tf_op jit(solution)/shard_map/ppermute | solution.py:454
  104.0 3.6 %collective-permute-done.9.theirs = bf16[1024,128]{1,0:T(8,128)(2,1)S(1)} collective-permute-done((bf16[1024,128]{1,0:T(8,128)(2,1)S(1)}, bf16[1024,128]{1,0:T(8,128)(2,1)S(1)}, u32[]{:S(2)}, u32[]{:S(2)}) %collective-permute-start.9) | collective-permute-done | bytes 262176 | tf_op jit(solution)/shard_map/ppermute | solution.py:454
  107.7 0.0 collective-permute-done.10.left_theirs
  107.7 0.0 copy-done.2
  107.7 13.0 %refresh.1 = (f32[1728,128]{1,0:T(8,128)}, f32[216,128]{1,0:T(8,128)}) custom-call(s32[2]{0:T(128)S(1)} %pad_add_fusion.place, bf16[1024,128]{1,0:T(8,128)(2,1)S(1)} %bitcast.7, bf16[1024,128]{1,0:T(8,128)(2,1)S(1)} %collective-permute-done.9.theirs, bf16[896,1792]{1,0:T(8,128)(2,1)S(1)} %constant_dynamic-update-slice_fusion.left_mine, ...), custom_call_target="tpu_custom_call" | custom-call | tf_op jit(solution)/shard_map/refresh/pallas_call | solution.py:387
  (9 shorter events, 0.2 us)
Async XLA Ops:
  2.1 19.6 %collective-permute-start = (bf16[1,4,16,256]{3,2,1,0:T(8,128)(2,1)S(1)}, bf16[1,4,16,256]{3,2,1,0:T(8,128)(2,1)S(1)}, u32[]{:S(2)}, u32[]{:S(2)}) collective-permute-start(bf16[1,4,16,256]{3,2,1,0:T(8,128)(2,1)S(1)} %get-tuple-element.59), channel_id=1, source_target_pairs={{0,8},{8,16},{16,24},{24,32},{32,40},{40,48},{48,56},{56,64},{64,7... | collective-permute-start | bytes 98312 | tf_op jit(solution)/shard_map/ppermute | solution.py:424
  13.6 8.9 %collective-permute-start.1 = (bf16[1,4,16,256]{3,2,1,0:T(8,128)(2,1)S(1)}, bf16[1,4,16,256]{3,2,1,0:T(8,128)(2,1)S(1)}, u32[]{:S(2)}, u32[]{:S(2)}) collective-permute-start(bf16[1,4,16,256]{3,2,1,0:T(8,128)(2,1)S(1)} %get-tuple-element.58), channel_id=1, source_target_pairs={{8,0},{16,8},{24,16},{32,24},{40,32},{48,40},{56,48},{64,56},{72,6... | collective-permute-start | bytes 98312 | tf_op jit(solution)/shard_map/ppermute | solution.py:425
  22.4 0.8 copy-start.1
  23.2 0.7 copy-start.3
  25.6 5.8 %collective-permute-start.2 = (bf16[1024,128]{1,0:T(8,128)(2,1)S(1)}, bf16[1024,128]{1,0:T(8,128)(2,1)S(1)}, u32[]{:S(2)}, u32[]{:S(2)}) collective-permute-start(bf16[1024,128]{1,0:T(8,128)(2,1)S(1)} %get-tuple-element.31), channel_id=1, source_target_pairs={{0,1},{1,0},{2,3},{3,2},{4,5},{5,4},{6,7},{7,6},{8,9},{9,8},{10,11... | collective-permute-start | bytes 786440 | tf_op jit(solution)/shard_map/ppermute | solution.py:434
  29.7 1.4 %copy-start = (f32[216,1728]{1,0:T(8,128)S(1)}, f32[216,1728]{1,0:T(8,128)}, u32[]{:S(2)}) copy-start(f32[216,1728]{1,0:T(8,128)} %rows.1) | copy-start | bytes 4478980
  32.2 30.5 %all-to-all-start = ((bf16[256,4,128]{2,1,0:T(4,128)(2,1)}), bf16[256,4,128]{2,1,0:T(4,128)(2,1)S(1)}, u32[]{:S(2)}, u32[]{:S(2)}) async-start(bf16[256,4,128]{2,1,0:T(4,128)(2,1)} %bitcast.2), calls=%async_computation | async-start | bytes 524288 | tf_op jit(solution)/shard_map/all_to_all | solution.py:443
  48.6 30.5 %collective-permute-start.3 = (bf16[112,1792]{1,0:T(8,128)(2,1)S(1)}, bf16[112,1792]{1,0:T(8,128)(2,1)S(1)}, u32[]{:S(2)}, u32[]{:S(2)}) collective-permute-start(bf16[112,1792]{1,0:T(8,128)(2,1)S(1)} %get-tuple-element.44), channel_id=1, source_target_pairs={{0,2},{2,4},{4,6},{6,8},{8,10},{10,12},{12,14},{14,0},{1,3},{3,5},... | collective-permute-start | bytes 1204232 | tf_op jit(solution)/shard_map/ppermute | solution.py:440
  50.5 28.6 %collective-permute-start.4 = (bf16[112,1792]{1,0:T(8,128)(2,1)S(1)}, bf16[112,1792]{1,0:T(8,128)(2,1)S(1)}, u32[]{:S(2)}, u32[]{:S(2)}) collective-permute-start(bf16[112,1792]{1,0:T(8,128)(2,1)S(1)} %get-tuple-element.45), channel_id=1, source_target_pairs={{0,2},{2,4},{4,6},{6,8},{8,10},{10,12},{12,14},{14,0},{1,3},{3,5},... | collective-permute-start | bytes 1204232 | tf_op jit(solution)/shard_map/ppermute | solution.py:440
  53.3 25.8 %collective-permute-start.5 = (bf16[112,1792]{1,0:T(8,128)(2,1)S(1)}, bf16[112,1792]{1,0:T(8,128)(2,1)S(1)}, u32[]{:S(2)}, u32[]{:S(2)}) collective-permute-start(bf16[112,1792]{1,0:T(8,128)(2,1)S(1)} %get-tuple-element.44), channel_id=1, source_target_pairs={{0,14},{2,0},{4,2},{6,4},{8,6},{10,8},{12,10},{14,12},{1,15},{3,1}... | collective-permute-start | bytes 1204232 | tf_op jit(solution)/shard_map/ppermute | solution.py:440
  57.0 22.1 %collective-permute-start.6 = (bf16[112,1792]{1,0:T(8,128)(2,1)S(1)}, bf16[112,1792]{1,0:T(8,128)(2,1)S(1)}, u32[]{:S(2)}, u32[]{:S(2)}) collective-permute-start(bf16[112,1792]{1,0:T(8,128)(2,1)S(1)} %get-tuple-element.45), channel_id=1, source_target_pairs={{0,14},{2,0},{4,2},{6,4},{8,6},{10,8},{12,10},{14,12},{1,15},{3,1}... | collective-permute-start | bytes 1204232 | tf_op jit(solution)/shard_map/ppermute | solution.py:440
  63.5 33.4 %all-to-all-start.1 = ((bf16[256,4,128]{2,1,0:T(4,128)(2,1)}), bf16[256,4,128]{2,1,0:T(4,128)(2,1)S(1)}, u32[]{:S(2)}, u32[]{:S(2)}) async-start(bf16[256,4,128]{2,1,0:T(4,128)(2,1)} %bitcast.4), calls=%async_computation.1 | async-start | bytes 524288 | tf_op jit(solution)/shard_map/all_to_all | solution.py:447
  79.2 17.0 %collective-permute-start.7 = (bf16[112,1792]{1,0:T(8,128)(2,1)S(1)}, bf16[112,1792]{1,0:T(8,128)(2,1)S(1)}, u32[]{:S(2)}, u32[]{:S(2)}) collective-permute-start(bf16[112,1792]{1,0:T(8,128)(2,1)S(1)} %collective-permute-done.3), channel_id=1, source_target_pairs={{0,2},{2,4},{4,6},{6,8},{8,10},{10,12},{12,14},{14,0},{1,3},{3,5},... | collective-permute-start | bytes 1204232 | tf_op jit(solution)/shard_map/ppermute | solution.py:440
  81.1 15.8 %collective-permute-start.8 = (bf16[112,1792]{1,0:T(8,128)(2,1)S(1)}, bf16[112,1792]{1,0:T(8,128)(2,1)}, u32[]{:S(2)}, u32[]{:S(2)}) collective-permute-start(bf16[112,1792]{1,0:T(8,128)(2,1)S(1)} %collective-permute-done.6), channel_id=1, source_target_pairs={{0,14},{2,0},{4,2},{6,4},{8,6},{10,8},{12,10},{14,12},{1,15},{3,1}... | collective-permute-start | bytes 1204232 | tf_op jit(solution)/shard_map/ppermute | solution.py:440
  96.2 0.7 copy-start.4
  96.9 1.0 copy-start.5
  96.9 10.7 %copy-start.2 = (f32[128,128]{1,0:T(8,128)S(1)}, f32[128,128]{1,0:T(8,128)}, u32[]{:S(2)}) copy-start(f32[128,128]{1,0:T(8,128)} %right_stat.1) | copy-start | bytes 196612
  99.0 8.6 %collective-permute-start.10 = (bf16[896,1792]{1,0:T(8,128)(2,1)S(1)}, bf16[896,1792]{1,0:T(8,128)(2,1)S(1)}, u32[]{:S(2)}, u32[]{:S(2)}) collective-permute-start(bf16[896,1792]{1,0:T(8,128)(2,1)S(1)} %constant_dynamic-update-slice_fusion.left_mine), channel_id=1, source_target_pairs={{0,1},{1,0},{2,3},{3,2},{4,5},{5,4},{6,7},{7,6},{8,9},{9,8},{10,11... | collective-permute-start | bytes 9633800 | tf_op jit(solution)/shard_map/ppermute | solution.py:456
  101.9 5.7 %collective-permute-start.9 = (bf16[1024,128]{1,0:T(8,128)(2,1)S(1)}, bf16[1024,128]{1,0:T(8,128)(2,1)S(1)}, u32[]{:S(2)}, u32[]{:S(2)}) collective-permute-start(bf16[1024,128]{1,0:T(8,128)(2,1)S(1)} %bitcast.6), channel_id=1, source_target_pairs={{0,1},{1,0},{2,3},{3,2},{4,5},{5,4},{6,7},{7,6},{8,9},{9,8},{10,11... | collective-permute-start | bytes 786440 | tf_op jit(solution)/shard_map/ppermute | solution.py:454

commit v5 on v4

--- a/solution.py
+++ b/solution.py
@@ -43,17 +43,17 @@
 
 
 def conv_kernel(
-    scale, place, before, volume, after, cotangent, weight, out, keep, give, pre_grad, patches
+    scale, place, before, up, down, after, weight, out, keep, give, pre_grad, patches
 ):
-    height = volume.shape[2]
-    wide = volume.shape[3]
+    height = up.shape[2]
+    wide = up.shape[3]
     lanes = weight.shape[1]
     half = lanes // 2
     across = wide // half
-    depth = volume.shape[1]
+    depth = out.shape[1]
     held = depth + 2
     rows = held * height
-    cells = jnp.concatenate([before[0, :2], volume[0], after[0, :2]], axis=0).astype(jnp.float32)
+    cells = jnp.concatenate([before[0, :2], up[0, :2], after[0, :2]], axis=0).astype(jnp.float32)
     low = lax.broadcasted_iota(jnp.int32, (1, 1, lanes), 2) < half
     low_flat = lax.broadcasted_iota(jnp.int32, (1, lanes), 1) < half
     doubled = {}
@@ -86,9 +86,8 @@
         span = slice(x * lanes, (x + 1) * lanes)
         begin = (x % (across // 2)) * lanes
         side = 2 + x // (across // 2)
-        upstream.append(before[0, side, :, begin : begin + lanes])
-        upstream.extend(cotangent[0, p, :, span] for p in range(depth))
-        upstream.append(after[0, side, :, begin : begin + lanes])
+        for plane in (before, down, up, after):
+            upstream.append(plane[0, side, :, begin : begin + lanes])
         for p in range(depth):
             first = x * rows + (1 + p) * height
             out[0, p, :, span] = output[first : first + height]
@@ -176,6 +175,21 @@
     return (low + sharp_dot(cube, high)) * lax.rsqrt(jnp.sqrt(largest))
 
 
+def message_kernel(volume, cotangent, up, down):
+    depth, wide = volume.shape[1], volume.shape[3]
+    for message, plane in ((up, depth - 1), (down, 0)):
+        message[0, :depth] = volume[0]
+        for k in range(cotangent.shape[3] // wide):
+            message[0, depth + k] = cotangent[0, plane, :, k * wide : (k + 1) * wide]
+
+
+def stack_kernel(*refs):
+    pieces, stacked = refs[:-1], refs[-1]
+    part = pieces[0].shape[0]
+    for k, piece in enumerate(pieces):
+        stacked[k * part : (k + 1) * part, :] = piece[...]
+
+
 def pack_kernel(rows, *halves):
     count, fan = rows.shape
     part = halves[0].shape[0]
@@ -190,12 +204,15 @@
         half[...] = packed[k * part : (k + 1) * part, :]
 
 
-def flip_kernel(weight, flipped):
+def flip_kernel(weight, flipped, padded):
     lanes = weight.shape[1]
     half = lanes // 2
     low = lax.broadcasted_iota(jnp.int32, (1, lanes), 1) < half
-    for j in range(weight.shape[0] // lanes):
-        both = jnp.transpose(weight[j * lanes : (j + 1) * lanes, :].astype(jnp.float32))
+    spare = padded.shape[0] - weight.shape[0]
+    taps = jnp.concatenate([weight[...], jnp.zeros((spare, lanes), jnp.bfloat16)], axis=0)
+    padded[...] = taps
+    for j in range(taps.shape[0] // lanes):
+        both = jnp.transpose(taps[j * lanes : (j + 1) * lanes, :].astype(jnp.float32))
         turned = jnp.concatenate([both[:, half:], both[:, :half]], axis=1)
         pair = (jnp.where(low, both, turned), jnp.where(low, turned, both))
         for side in range(2):
@@ -296,14 +313,14 @@
     direction[...] = window[pl.ds(pl.multiple_of(first - base, 8), count), :] * ratio
 
 
-def convolved(place, before, volume, after, cotangent, weight, scale, part):
-    leading, depth, height, wide = volume.shape
+def convolved(place, before, up, down, after, weight, shape, scale, part):
+    leading, depth, height, wide = shape
     lanes = weight.shape[1]
-    cells = wide // (lanes // 2) * (depth + 2) * height
+    cells = wide // lanes * (depth + 2) * height
     return pl.pallas_call(
         functools.partial(conv_kernel, scale),
         out_shape=(
-            jax.ShapeDtypeStruct(cotangent.shape, jnp.bfloat16),
+            jax.ShapeDtypeStruct(shape, jnp.bfloat16),
             jax.ShapeDtypeStruct((part, lanes), jnp.float32),
             jax.ShapeDtypeStruct((part, lanes), jnp.bfloat16),
             jax.ShapeDtypeStruct((cells, lanes), jnp.bfloat16),
@@ -313,7 +330,7 @@
         scratch_shapes=[pltpu.VMEM((cells, weight.shape[0]), jnp.bfloat16)],
         compiler_params=room(12),
         name="conv",
-    )(place, before, volume, after, cotangent, weight)
+    )(place, before, up, down, after, weight)
 
 
 def convolved_back(pre_grad, flipped, volume):
@@ -357,15 +374,43 @@
 
 
 def flipped_taps(weight, taps):
-    lanes = weight.shape[1]
+    fan, lanes = weight.shape
     return pl.pallas_call(
         flip_kernel,
-        out_shape=jax.ShapeDtypeStruct((taps * lanes, lanes), jnp.bfloat16),
+        out_shape=(
+            jax.ShapeDtypeStruct((taps * lanes, lanes), jnp.bfloat16),
+            jax.ShapeDtypeStruct(((fan + lanes - 1) // lanes * lanes, lanes), jnp.bfloat16),
+        ),
         in_specs=[VMEM],
-        out_specs=VMEM,
+        out_specs=(VMEM,) * 2,
         compiler_params=room(8),
         name="flip",
     )(weight)
+
+
+def messages(volume, cotangent):
+    leading, depth, height, wide = volume.shape
+    shape = (leading, depth + cotangent.shape[3] // wide, height, wide)
+    return pl.pallas_call(
+        message_kernel,
+        out_shape=(jax.ShapeDtypeStruct(shape, jnp.bfloat16),) * 2,
+        in_specs=[VMEM] * 2,
+        out_specs=(VMEM,) * 2,
+        compiler_params=room(4),
+        name="messages",
+    )(volume, cotangent)
+
+
+def stacked_rows(pieces):
+    rows, size = pieces[0].shape
+    return pl.pallas_call(
+        stack_kernel,
+        out_shape=jax.ShapeDtypeStruct((rows * len(pieces), size), pieces[0].dtype),
+        in_specs=[VMEM] * len(pieces),
+        out_specs=VMEM,
+        compiler_params=room(4),
+        name="stack",
+    )(*pieces)
 
 
 def packed_rows(rows):
@@ -418,18 +463,14 @@
     onward = [(i, (i + 1) % slabs) for i in range(slabs)]
     back = [((i + 1) % slabs, i) for i in range(slabs)]
 
-    def with_plane(plane):
-        return jnp.concatenate([volume, plane[..., :wide], plane[..., wide:]], axis=1)
-
-    before = lax.ppermute(with_plane(cotangent[:, -1:]), space, onward)
-    after = lax.ppermute(with_plane(cotangent[:, :1]), space, back)
-    padded_fan = (fan + lanes - 1) // lanes * lanes
-    padded = jnp.pad(weight, ((0, padded_fan - fan), (0, 0)))
-    flipped = flipped_taps(padded, 27)
+    up, down = messages(volume, cotangent)
+    before = lax.ppermute(up, space, onward)
+    after = lax.ppermute(down, space, back)
+    flipped, padded = flipped_taps(weight, 27)
     piece = 4 * ((fan + 8 * chips - 1) // (8 * chips))
     cells = slabs * lax.axis_size(("chip", "core")) * leading * depth * height * (wide // (fan // 27))
     output, keep, give, pre_grad = convolved(
-        place, before, volume, after, cotangent, padded, 1.0 / math.sqrt(cells), piece * chips
+        place, before, up, down, after, padded, cotangent.shape, 1.0 / math.sqrt(cells), piece * chips
     )
     got = lax.ppermute(give, "core", swap)
     sent = added(keep, got)
@@ -448,11 +489,11 @@
     lower[0], lower[1], upper[0], upper[1] = lax.optimization_barrier((*lower, *upper))
     far = [risen(lower[0], 1), risen(upper[1], -1)]
     input_grad = convolved_back(pre_grad, flipped, volume)
-    mine, input_grad, *lefts = lax.optimization_barrier(
-        (mine.reshape(chips * piece, lanes), input_grad, *own, *lower, *far, *upper)
-    )
+    mine = mine.reshape(chips * piece, lanes)
+    _, *lefts = lax.optimization_barrier((mine, *own, *lower, *far, *upper))
+    mine, input_grad = lax.optimization_barrier((mine, input_grad))
     theirs = lax.ppermute(mine, "core", swap)
-    left_mine = jnp.concatenate(lefts, axis=0)
+    left_mine = stacked_rows(lefts)
     left_theirs = lax.ppermute(left_mine, "core", swap)
     gradient, direction = refreshed(
         place, mine, theirs, left_mine, left_theirs, right_stat, fan, left_stat.shape[0]

time: 122 us -> 121 us (level)
  starting transfers between devices: 77.7 us -> 76.2 us
    unnamed x19 -> x26, local copies, waits for them, and re-layouts: 5.65 us -> 8.02 us
    ppermute x6, waiting for transfers between devices: 9.02 us -> 10.5 us  [risen(): lax.ppermute(rows, column, [(i, (i + by) % levels) for i in range(levels)])]
  transfers between devices with their start and end apart: 13 -> 13, of which waited for: 4 -> 4; matrix products, arithmetic and copies ran while one was open for 1% -> 0% of each run, Pallas kernels for 2% -> 2%
where the time goes in v5:
time: 121 us; the launch traced here: 120 us
  starting transfers between devices  76.2 us (63%)
  Pallas kernels  18.4 us (15%)
  waiting for transfers between devices  16.2 us (13%)
  local copies, waits for them, and re-layouts  8.02 us (7%)
    ppermute x6, starting transfers between devices, risen(): lax.ppermute(rows, column, [(i, (i + by) % levels) for i in range(levels)])  17.7 us
    all_to_all x1, starting transfers between devices, per_device(): lax.all_to_all(sent.reshape(chips, piece, lanes), space + ('chip',), 0, 0)  16.4 us
    all_to_all x1, starting transfers between devices, per_device(): lax.all_to_all(spread.reshape(chips, piece, lanes), space + ('chip',), 0, 0)  14.7 us
    pallas_call x1, Pallas kernels, refreshed(): pl.pallas_call(refresh_kernel, out_shape=(jax.ShapeDtypeStruct((fan, widt...  13 us
    ppermute x1, starting transfers between devices, per_device(): before = lax.ppermute(up, space, onward)  11.5 us
    ppermute x6, waiting for transfers between devices, risen(): lax.ppermute(rows, column, [(i, (i + by) % levels) for i in range(levels)])  10.5 us
    unnamed x26, local copies, waits for them, and re-layouts  8.02 us
    ppermute x1, starting transfers between devices, per_device(): after = lax.ppermute(down, space, back)  7.02 us
  transfers between devices with their start and end apart: 13, of which 4 were waited for; matrix products, arithmetic and copies ran while one was open for 0% of the time, Pallas kernels for 2%

profile of v5, /device:TPU:1, one launch (start us, length us, event | category | flops | bytes accessed | tf_op | source)
XLA Modules:
  0.0 119.8 jit_solution(18411130493249515912)
XLA Ops:
  0.6 0.0 copy-start.9
  0.6 0.7 copy-done.9
  1.4 0.7 copy-done.10
  2.1 11.5 %collective-permute-start = (bf16[1,4,16,256]{3,2,1,0:T(8,128)(2,1)S(1)}, bf16[1,4,16,256]{3,2,1,0:T(8,128)(2,1)S(1)}, u32[]{:S(2)}, u32[]{:S(2)}) collective-permute-start(bf16[1,4,16,256]{3,2,1,0:T(8,128)(2,1)S(1)} %get-tuple-element.33.up), channel_id=1, source_target_pairs={{0,8},{8,16},{16,24},{24,32},{32,40},{40,48},{48,56},{56,64},{64,7... | collective-permute-start | bytes 98312 | tf_op jit(solution)/shard_map/ppermute | solution.py:467
  13.6 7.0 %collective-permute-start.1 = (bf16[1,4,16,256]{3,2,1,0:T(8,128)(2,1)S(1)}, bf16[1,4,16,256]{3,2,1,0:T(8,128)(2,1)S(1)}, u32[]{:S(2)}, u32[]{:S(2)}) collective-permute-start(bf16[1,4,16,256]{3,2,1,0:T(8,128)(2,1)S(1)} %get-tuple-element.34.down), channel_id=1, source_target_pairs={{8,0},{16,8},{24,16},{32,24},{40,32},{48,40},{56,48},{64,56},{72,6... | collective-permute-start | bytes 98312 | tf_op jit(solution)/shard_map/ppermute | solution.py:468
  20.6 0.1 pad_add_fusion.place
  20.7 1.0 copy-done.1
  21.7 0.5 flip.1
  22.2 0.0 collective-permute-done.before
  22.2 0.3 collective-permute-done.1.after
  22.4 1.7 %conv.1 = (bf16[1,2,16,512]{3,2,1,0:T(8,128)(2,1)}, f32[1024,128]{1,0:T(8,128)S(1)}, bf16[1024,128]{1,0:T(8,128)(2,1)S(1)}, bf16[256,128]{1,0:T(8,128)(2,1)S(1)}) custom-call(s32[2]{0:T(128)S(1)} %pad_add_fusion.place, bf16[1,4,16,256]{3,2,1,0:T(8,128)(2,1)S(1)} %collective-permute-done.before, bf16[1,4,16,256]{3,2,1,0:T(8,128)(2,1)S(1)} %get-tuple-element.33.up, ...), custom_call_target="tpu_custom_call" | custom-call | tf_op jit(solution)/shard_map/conv/pallas_call | solution.py:320
  24.2 0.6 copy-done.7
  24.8 0.0 copy-done.11
  24.8 4.0 %collective-permute-start.2 = (bf16[1024,128]{1,0:T(8,128)(2,1)S(1)}, bf16[1024,128]{1,0:T(8,128)(2,1)S(1)}, u32[]{:S(2)}, u32[]{:S(2)}) collective-permute-start(bf16[1024,128]{1,0:T(8,128)(2,1)S(1)} %get-tuple-element.38), channel_id=1, source_target_pairs={{0,1},{1,0},{2,3},{3,2},{4,5},{5,4},{6,7},{7,6},{8,9},{9,8},{10,11... | collective-permute-start | bytes 786440 | tf_op jit(solution)/shard_map/ppermute | solution.py:475
  28.8 0.0 copy-start
  28.8 1.4 %copy-done = f32[216,1728]{1,0:T(8,128)S(1)} copy-done((f32[216,1728]{1,0:T(8,128)S(1)}, f32[216,1728]{1,0:T(8,128)}, u32[]{:S(2)}) %copy-start) | copy-done | bytes 1493016
  30.2 0.4 pack.1
  30.6 0.0 collective-permute-done.2.got
  30.6 0.7 add.7
  31.4 16.4 %all-to-all-start = ((bf16[256,4,128]{2,1,0:T(4,128)(2,1)}), bf16[256,4,128]{2,1,0:T(4,128)(2,1)S(1)}, u32[]{:S(2)}, u32[]{:S(2)}) async-start(bf16[256,4,128]{2,1,0:T(4,128)(2,1)} %bitcast.2), calls=%async_computation | async-start | bytes 524288 | tf_op jit(solution)/shard_map/all_to_all | solution.py:484
  47.7 2.8 %collective-permute-start.6 = (bf16[112,1792]{1,0:T(8,128)(2,1)S(1)}, bf16[112,1792]{1,0:T(8,128)(2,1)S(1)}, u32[]{:S(2)}, u32[]{:S(2)}) collective-permute-start(bf16[112,1792]{1,0:T(8,128)(2,1)S(1)} %get-tuple-element.52.refs_0_), channel_id=1, source_target_pairs={{0,14},{2,0},{4,2},{6,4},{8,6},{10,8},{12,10},{14,12},{1,15},{3,1}... | collective-permute-start | bytes 1204232 | tf_op jit(solution)/shard_map/ppermute | solution.py:481
  50.5 2.5 %collective-permute-start.4 = (bf16[112,1792]{1,0:T(8,128)(2,1)S(1)}, bf16[112,1792]{1,0:T(8,128)(2,1)S(1)}, u32[]{:S(2)}, u32[]{:S(2)}) collective-permute-start(bf16[112,1792]{1,0:T(8,128)(2,1)S(1)} %get-tuple-element.52.refs_0_), channel_id=1, source_target_pairs={{0,2},{2,4},{4,6},{6,8},{8,10},{10,12},{12,14},{14,0},{1,3},{3,5},... | collective-permute-start | bytes 1204232 | tf_op jit(solution)/shard_map/ppermute | solution.py:481
  53.0 4.0 %collective-permute-start.7 = (bf16[112,1792]{1,0:T(8,128)(2,1)S(1)}, bf16[112,1792]{1,0:T(8,128)(2,1)S(1)}, u32[]{:S(2)}, u32[]{:S(2)}) collective-permute-start(bf16[112,1792]{1,0:T(8,128)(2,1)S(1)} %get-tuple-element.53.refs_1_), channel_id=1, source_target_pairs={{0,14},{2,0},{4,2},{6,4},{8,6},{10,8},{12,10},{14,12},{1,15},{3,1}... | collective-permute-start | bytes 1204232 | tf_op jit(solution)/shard_map/ppermute | solution.py:481
  57.1 1.9 %collective-permute-start.5 = (bf16[112,1792]{1,0:T(8,128)(2,1)S(1)}, bf16[112,1792]{1,0:T(8,128)(2,1)S(1)}, u32[]{:S(2)}, u32[]{:S(2)}) collective-permute-start(bf16[112,1792]{1,0:T(8,128)(2,1)S(1)} %get-tuple-element.53.refs_1_), channel_id=1, source_target_pairs={{0,2},{2,4},{4,6},{6,8},{8,10},{10,12},{12,14},{14,0},{1,3},{3,5},... | collective-permute-start | bytes 1204232 | tf_op jit(solution)/shard_map/ppermute | solution.py:481
  59.0 2.8 %all-to-all-done = bf16[256,4,128]{2,1,0:T(4,128)(2,1)S(1)} async-done(((bf16[256,4,128]{2,1,0:T(4,128)(2,1)}), bf16[256,4,128]{2,1,0:T(4,128)(2,1)S(1)}, u32[]{:S(2)}, u32[]{:S(2)}) %all-to-all-start) | async-done | bytes 262176 | tf_op jit(solution)/shard_map/all_to_all | solution.py:484
  61.8 0.8 sum.1
  62.6 14.7 %all-to-all-start.1 = ((bf16[256,4,128]{2,1,0:T(4,128)(2,1)}), bf16[256,4,128]{2,1,0:T(4,128)(2,1)S(1)}, u32[]{:S(2)}, u32[]{:S(2)}) async-start(bf16[256,4,128]{2,1,0:T(4,128)(2,1)} %bitcast.4), calls=%async_computation.1 | async-start | bytes 524288 | tf_op jit(solution)/shard_map/all_to_all | solution.py:488
  77.3 0.0 collective-permute-done.6.refs_6_
  77.3 0.0 collective-permute-done.4.refs_2_
  77.4 0.0 collective-permute-done.7.refs_7_
  77.4 0.0 collective-permute-done.5.refs_3_
  77.4 1.9 %collective-permute-start.8 = (bf16[112,1792]{1,0:T(8,128)(2,1)S(1)}, bf16[112,1792]{1,0:T(8,128)(2,1)S(1)}, u32[]{:S(2)}, u32[]{:S(2)}) collective-permute-start(bf16[112,1792]{1,0:T(8,128)(2,1)S(1)} %collective-permute-done.4.refs_2_), channel_id=1, source_target_pairs={{0,2},{2,4},{4,6},{6,8},{8,10},{10,12},{12,14},{14,0},{1,3},{3,5},... | collective-permute-start | bytes 1204232 | tf_op jit(solution)/shard_map/ppermute | solution.py:481
  79.3 4.6 %collective-permute-start.9 = (bf16[112,1792]{1,0:T(8,128)(2,1)S(1)}, bf16[112,1792]{1,0:T(8,128)(2,1)S(1)}, u32[]{:S(2)}, u32[]{:S(2)}) collective-permute-start(bf16[112,1792]{1,0:T(8,128)(2,1)S(1)} %collective-permute-done.7.refs_7_), channel_id=1, source_target_pairs={{0,14},{2,0},{4,2},{6,4},{8,6},{10,8},{12,10},{14,12},{1,15},{3,1}... | collective-permute-start | bytes 1204232 | tf_op jit(solution)/shard_map/ppermute | solution.py:481
  83.9 10.5 %collective-permute-done.8.refs_4_ = bf16[112,1792]{1,0:T(8,128)(2,1)S(1)} collective-permute-done((bf16[112,1792]{1,0:T(8,128)(2,1)S(1)}, bf16[112,1792]{1,0:T(8,128)(2,1)S(1)}, u32[]{:S(2)}, u32[]{:S(2)}) %collective-permute-start.8) | collective-permute-done | bytes 401440 | tf_op jit(solution)/shard_map/ppermute | solution.py:481
  94.4 0.7 copy-done.2
  95.2 0.0 collective-permute-done.9.refs_5_
  95.2 0.8 copy-done.4
  95.9 0.0 all-to-all-done.1
  95.9 1.0 copy-done.3
  96.9 1.0 copy-done.5
  97.9 0.2 stack.13.left_mine
  98.1 2.9 %collective-permute-start.10 = (bf16[896,1792]{1,0:T(8,128)(2,1)S(1)}, bf16[896,1792]{1,0:T(8,128)(2,1)S(1)}, u32[]{:S(2)}, u32[]{:S(2)}) collective-permute-start(bf16[896,1792]{1,0:T(8,128)(2,1)S(1)} %stack.13.left_mine), channel_id=1, source_target_pairs={{0,1},{1,0},{2,3},{3,2},{4,5},{5,4},{6,7},{7,6},{8,9},{9,8},{10,11... | collective-permute-start | bytes 9633800 | tf_op jit(solution)/shard_map/ppermute | solution.py:497
  101.0 0.0 copy-done.8
  101.0 1.0 conv_back.1
  102.0 2.1 %collective-permute-start.3 = (bf16[1024,128]{1,0:T(8,128)(2,1)S(1)}, bf16[1024,128]{1,0:T(8,128)(2,1)S(1)}, u32[]{:S(2)}, u32[]{:S(2)}) collective-permute-start(bf16[1024,128]{1,0:T(8,128)(2,1)S(1)} %bitcast.6), channel_id=1, source_target_pairs={{0,1},{1,0},{2,3},{3,2},{4,5},{5,4},{6,7},{7,6},{8,9},{9,8},{10,11... | collective-permute-start | bytes 786440 | tf_op jit(solution)/shard_map/ppermute | solution.py:495
  104.1 2.6 %collective-permute-done.3.theirs = bf16[1024,128]{1,0:T(8,128)(2,1)S(1)} collective-permute-done((bf16[1024,128]{1,0:T(8,128)(2,1)S(1)}, bf16[1024,128]{1,0:T(8,128)(2,1)S(1)}, u32[]{:S(2)}, u32[]{:S(2)}) %collective-permute-start.3) | collective-permute-done | bytes 262176 | tf_op jit(solution)/shard_map/ppermute | solution.py:495
  106.7 0.0 collective-permute-done.10.left_theirs
  106.7 13.0 %refresh.1 = (f32[1728,128]{1,0:T(8,128)}, f32[216,128]{1,0:T(8,128)}) custom-call(s32[2]{0:T(128)S(1)} %copy-done.12, bf16[1024,128]{1,0:T(8,128)(2,1)S(1)} %bitcast.7, bf16[1024,128]{1,0:T(8,128)(2,1)S(1)} %collective-permute-done.3.theirs, bf16[896,1792]{1,0:T(8,128)(2,1)S(1)} %stack.13.left_mine, ...), custom_call_target="tpu_custom_call" | custom-call | tf_op jit(solution)/shard_map/refresh/pallas_call | solution.py:432
  (14 shorter events, 0.0 us)
Async XLA Ops:
  0.6 0.8 copy-start.9
  1.4 0.7 copy-start.10
  2.1 20.1 %collective-permute-start = (bf16[1,4,16,256]{3,2,1,0:T(8,128)(2,1)S(1)}, bf16[1,4,16,256]{3,2,1,0:T(8,128)(2,1)S(1)}, u32[]{:S(2)}, u32[]{:S(2)}) collective-permute-start(bf16[1,4,16,256]{3,2,1,0:T(8,128)(2,1)S(1)} %get-tuple-element.33.up), channel_id=1, source_target_pairs={{0,8},{8,16},{16,24},{24,32},{32,40},{40,48},{48,56},{56,64},{64,7... | collective-permute-start | bytes 98312 | tf_op jit(solution)/shard_map/ppermute | solution.py:467
  13.6 8.9 %collective-permute-start.1 = (bf16[1,4,16,256]{3,2,1,0:T(8,128)(2,1)S(1)}, bf16[1,4,16,256]{3,2,1,0:T(8,128)(2,1)S(1)}, u32[]{:S(2)}, u32[]{:S(2)}) collective-permute-start(bf16[1,4,16,256]{3,2,1,0:T(8,128)(2,1)S(1)} %get-tuple-element.34.down), channel_id=1, source_target_pairs={{8,0},{16,8},{24,16},{32,24},{40,32},{48,40},{56,48},{64,56},{72,6... | collective-permute-start | bytes 98312 | tf_op jit(solution)/shard_map/ppermute | solution.py:468
  20.7 1.0 copy-start.1
  21.7 3.1 %copy-start.11 = (s32[2]{0:T(128)}, s32[2]{0:T(128)S(1)}, u32[]{:S(2)}) copy-start(s32[2]{0:T(128)S(1)} %pad_add_fusion.place) | copy-start | bytes 28
  24.2 0.6 copy-start.7
  24.8 5.8 %collective-permute-start.2 = (bf16[1024,128]{1,0:T(8,128)(2,1)S(1)}, bf16[1024,128]{1,0:T(8,128)(2,1)S(1)}, u32[]{:S(2)}, u32[]{:S(2)}) collective-permute-start(bf16[1024,128]{1,0:T(8,128)(2,1)S(1)} %get-tuple-element.38), channel_id=1, source_target_pairs={{0,1},{1,0},{2,3},{3,2},{4,5},{5,4},{6,7},{7,6},{8,9},{9,8},{10,11... | collective-permute-start | bytes 786440 | tf_op jit(solution)/shard_map/ppermute | solution.py:475
  28.8 1.4 %copy-start = (f32[216,1728]{1,0:T(8,128)S(1)}, f32[216,1728]{1,0:T(8,128)}, u32[]{:S(2)}) copy-start(f32[216,1728]{1,0:T(8,128)} %rows.1) | copy-start | bytes 4478980
  31.4 30.4 %all-to-all-start = ((bf16[256,4,128]{2,1,0:T(4,128)(2,1)}), bf16[256,4,128]{2,1,0:T(4,128)(2,1)S(1)}, u32[]{:S(2)}, u32[]{:S(2)}) async-start(bf16[256,4,128]{2,1,0:T(4,128)(2,1)} %bitcast.2), calls=%async_computation | async-start | bytes 524288 | tf_op jit(solution)/shard_map/all_to_all | solution.py:484
  47.7 29.6 %collective-permute-start.6 = (bf16[112,1792]{1,0:T(8,128)(2,1)S(1)}, bf16[112,1792]{1,0:T(8,128)(2,1)S(1)}, u32[]{:S(2)}, u32[]{:S(2)}) collective-permute-start(bf16[112,1792]{1,0:T(8,128)(2,1)S(1)} %get-tuple-element.52.refs_0_), channel_id=1, source_target_pairs={{0,14},{2,0},{4,2},{6,4},{8,6},{10,8},{12,10},{14,12},{1,15},{3,1}... | collective-permute-start | bytes 1204232 | tf_op jit(solution)/shard_map/ppermute | solution.py:481
  50.5 26.8 %collective-permute-start.4 = (bf16[112,1792]{1,0:T(8,128)(2,1)S(1)}, bf16[112,1792]{1,0:T(8,128)(2,1)S(1)}, u32[]{:S(2)}, u32[]{:S(2)}) collective-permute-start(bf16[112,1792]{1,0:T(8,128)(2,1)S(1)} %get-tuple-element.52.refs_0_), channel_id=1, source_target_pairs={{0,2},{2,4},{4,6},{6,8},{8,10},{10,12},{12,14},{14,0},{1,3},{3,5},... | collective-permute-start | bytes 1204232 | tf_op jit(solution)/shard_map/ppermute | solution.py:481
  53.0 24.3 %collective-permute-start.7 = (bf16[112,1792]{1,0:T(8,128)(2,1)S(1)}, bf16[112,1792]{1,0:T(8,128)(2,1)S(1)}, u32[]{:S(2)}, u32[]{:S(2)}) collective-permute-start(bf16[112,1792]{1,0:T(8,128)(2,1)S(1)} %get-tuple-element.53.refs_1_), channel_id=1, source_target_pairs={{0,14},{2,0},{4,2},{6,4},{8,6},{10,8},{12,10},{14,12},{1,15},{3,1}... | collective-permute-start | bytes 1204232 | tf_op jit(solution)/shard_map/ppermute | solution.py:481
  57.1 20.3 %collective-permute-start.5 = (bf16[112,1792]{1,0:T(8,128)(2,1)S(1)}, bf16[112,1792]{1,0:T(8,128)(2,1)S(1)}, u32[]{:S(2)}, u32[]{:S(2)}) collective-permute-start(bf16[112,1792]{1,0:T(8,128)(2,1)S(1)} %get-tuple-element.53.refs_1_), channel_id=1, source_target_pairs={{0,2},{2,4},{4,6},{6,8},{8,10},{10,12},{12,14},{14,0},{1,3},{3,5},... | collective-permute-start | bytes 1204232 | tf_op jit(solution)/shard_map/ppermute | solution.py:481
  62.6 33.3 %all-to-all-start.1 = ((bf16[256,4,128]{2,1,0:T(4,128)(2,1)}), bf16[256,4,128]{2,1,0:T(4,128)(2,1)S(1)}, u32[]{:S(2)}, u32[]{:S(2)}) async-start(bf16[256,4,128]{2,1,0:T(4,128)(2,1)} %bitcast.4), calls=%async_computation.1 | async-start | bytes 524288 | tf_op jit(solution)/shard_map/all_to_all | solution.py:488
  77.4 17.0 %collective-permute-start.8 = (bf16[112,1792]{1,0:T(8,128)(2,1)S(1)}, bf16[112,1792]{1,0:T(8,128)(2,1)S(1)}, u32[]{:S(2)}, u32[]{:S(2)}) collective-permute-start(bf16[112,1792]{1,0:T(8,128)(2,1)S(1)} %collective-permute-done.4.refs_2_), channel_id=1, source_target_pairs={{0,2},{2,4},{4,6},{6,8},{8,10},{10,12},{12,14},{14,0},{1,3},{3,5},... | collective-permute-start | bytes 1204232 | tf_op jit(solution)/shard_map/ppermute | solution.py:481
  79.3 15.9 %collective-permute-start.9 = (bf16[112,1792]{1,0:T(8,128)(2,1)S(1)}, bf16[112,1792]{1,0:T(8,128)(2,1)S(1)}, u32[]{:S(2)}, u32[]{:S(2)}) collective-permute-start(bf16[112,1792]{1,0:T(8,128)(2,1)S(1)} %collective-permute-done.7.refs_7_), channel_id=1, source_target_pairs={{0,14},{2,0},{4,2},{6,4},{8,6},{10,8},{12,10},{14,12},{1,15},{3,1}... | collective-permute-start | bytes 1204232 | tf_op jit(solution)/shard_map/ppermute | solution.py:481
  94.4 0.7 copy-start.2
  95.2 0.8 copy-start.4
  95.9 1.0 copy-start.3
  96.9 1.0 copy-start.5
  97.9 3.1 %copy-start.8 = (bf16[256,128]{1,0:T(8,128)(2,1)S(1)}, bf16[256,128]{1,0:T(8,128)(2,1)}, u32[]{:S(2)}) copy-start(bf16[256,128]{1,0:T(8,128)(2,1)} %copy-done.7) | copy-start | bytes 196612
  97.9 8.8 %copy-start.6 = (f32[128,128]{1,0:T(8,128)S(1)}, f32[128,128]{1,0:T(8,128)}, u32[]{:S(2)}) copy-start(f32[128,128]{1,0:T(8,128)} %right_stat.1) | copy-start | bytes 196612
  97.9 8.8 %copy-start.12 = (s32[2]{0:T(128)S(1)}, s32[2]{0:T(128)}, u32[]{:S(2)}) copy-start(s32[2]{0:T(128)} %copy-done.11) | copy-start | bytes 28
  98.1 8.6 %collective-permute-start.10 = (bf16[896,1792]{1,0:T(8,128)(2,1)S(1)}, bf16[896,1792]{1,0:T(8,128)(2,1)S(1)}, u32[]{:S(2)}, u32[]{:S(2)}) collective-permute-start(bf16[896,1792]{1,0:T(8,128)(2,1)S(1)} %stack.13.left_mine), channel_id=1, source_target_pairs={{0,1},{1,0},{2,3},{3,2},{4,5},{5,4},{6,7},{7,6},{8,9},{9,8},{10,11... | collective-permute-start | bytes 9633800 | tf_op jit(solution)/shard_map/ppermute | solution.py:497
  102.0 4.7 %collective-permute-start.3 = (bf16[1024,128]{1,0:T(8,128)(2,1)S(1)}, bf16[1024,128]{1,0:T(8,128)(2,1)S(1)}, u32[]{:S(2)}, u32[]{:S(2)}) collective-permute-start(bf16[1024,128]{1,0:T(8,128)(2,1)S(1)} %bitcast.6), channel_id=1, source_target_pairs={{0,1},{1,0},{2,3},{3,2},{4,5},{5,4},{6,7},{7,6},{8,9},{9,8},{10,11... | collective-permute-start | bytes 786440 | tf_op jit(solution)/shard_map/ppermute | solution.py:495

commit v6 on v5

--- a/solution.py
+++ b/solution.py
@@ -43,7 +43,8 @@
 
 
 def conv_kernel(
-    scale, place, before, up, down, after, weight, out, keep, give, pre_grad, patches
+    scale, place, before, up, down, after, weight, flipped,
+    out, keep, give, input_grad, patches, pre_grad, back_patches,
 ):
     height = up.shape[2]
     wide = up.shape[3]
@@ -108,6 +109,7 @@
     leading = place[0] == 0
     keep[...] = jnp.where(leading, head, tail)
     give[...] = jnp.where(leading, tail, head).astype(jnp.bfloat16)
+    back_kernel(pre_grad, flipped, input_grad, back_patches)
 
 
 def back_kernel(pre_grad, flipped, out, patches):
@@ -313,42 +315,29 @@
     direction[...] = window[pl.ds(pl.multiple_of(first - base, 8), count), :] * ratio
 
 
-def convolved(place, before, up, down, after, weight, shape, scale, part):
+def convolved(place, before, up, down, after, weight, flipped, shape, scale, part):
     leading, depth, height, wide = shape
     lanes = weight.shape[1]
-    cells = wide // lanes * (depth + 2) * height
+    across = wide // lanes
+    cells, own = across * (depth + 2) * height, across * depth * height
     return pl.pallas_call(
         functools.partial(conv_kernel, scale),
         out_shape=(
             jax.ShapeDtypeStruct(shape, jnp.bfloat16),
             jax.ShapeDtypeStruct((part, lanes), jnp.float32),
             jax.ShapeDtypeStruct((part, lanes), jnp.bfloat16),
-            jax.ShapeDtypeStruct((cells, lanes), jnp.bfloat16),
+            jax.ShapeDtypeStruct((leading, depth, height, wide // 2), jnp.bfloat16),
         ),
-        in_specs=[SMEM] + [VMEM] * 5,
+        in_specs=[SMEM] + [VMEM] * 6,
         out_specs=(VMEM,) * 4,
-        scratch_shapes=[pltpu.VMEM((cells, weight.shape[0]), jnp.bfloat16)],
+        scratch_shapes=[
+            pltpu.VMEM((cells, weight.shape[0]), jnp.bfloat16),
+            pltpu.VMEM((cells, lanes), jnp.bfloat16),
+            pltpu.VMEM((own, flipped.shape[0]), jnp.bfloat16),
+        ],
         compiler_params=room(12),
         name="conv",
-    )(place, before, up, down, after, weight)
-
-
-def convolved_back(pre_grad, flipped, volume):
-    leading, depth, height, wide = volume.shape
-    lanes = pre_grad.shape[1]
-    own = wide // (lanes // 2) * depth * height
-    return pl.pallas_call(
-        back_kernel,
-        out_shape=jax.ShapeDtypeStruct(volume.shape, jnp.bfloat16),
-        in_specs=[VMEM] * 2,
-        out_specs=VMEM,
-        scratch_shapes=[pltpu.VMEM((own, flipped.shape[0]), jnp.bfloat16)],
-        compiler_params=room(8),
-        cost_estimate=pl.CostEstimate(
-            flops=2 * own * flipped.size, bytes_accessed=2 * own * flipped.shape[0], transcendentals=0
-        ),
-        name="conv_back",
-    )(pre_grad, flipped)
+    )(place, before, up, down, after, weight, flipped)
 
 
 def added(keep, got):
@@ -469,8 +458,8 @@
     flipped, padded = flipped_taps(weight, 27)
     piece = 4 * ((fan + 8 * chips - 1) // (8 * chips))
     cells = slabs * lax.axis_size(("chip", "core")) * leading * depth * height * (wide // (fan // 27))
-    output, keep, give, pre_grad = convolved(
-        place, before, up, down, after, padded, cotangent.shape, 1.0 / math.sqrt(cells), piece * chips
+    output, keep, give, input_grad = convolved(
+        place, before, up, down, after, padded, flipped, cotangent.shape, 1.0 / math.sqrt(cells), piece * chips
     )
     got = lax.ppermute(give, "core", swap)
     sent = added(keep, got)
@@ -488,10 +477,8 @@
     mine = lax.all_to_all(spread.reshape(chips, piece, lanes), space + ("chip",), 0, 0)
     lower[0], lower[1], upper[0], upper[1] = lax.optimization_barrier((*lower, *upper))
     far = [risen(lower[0], 1), risen(upper[1], -1)]
-    input_grad = convolved_back(pre_grad, flipped, volume)
     mine = mine.reshape(chips * piece, lanes)
     _, *lefts = lax.optimization_barrier((mine, *own, *lower, *far, *upper))
-    mine, input_grad = lax.optimization_barrier((mine, input_grad))
     theirs = lax.ppermute(mine, "core", swap)
     left_mine = stacked_rows(lefts)
     left_theirs = lax.ppermute(left_mine, "core", swap)

time: 121 us -> 117 us (0.967)
  local copies, waits for them, and re-layouts: 8.02 us -> 3.88 us
    unnamed x26 -> x10, local copies, waits for them, and re-layouts: 8.02 us -> 3.88 us
  transfers between devices with their start and end apart: 13 -> 13, of which waited for: 4 -> 4; matrix products, arithmetic and copies ran while one was open for 0% -> 0% of each run, Pallas kernels for 2% -> 1%
where the time goes in v6:
time: 117 us; the launch traced here: 116 us
  starting transfers between devices  76.2 us (65%)
  Pallas kernels  18 us (15%)
  waiting for transfers between devices  17.2 us (15%)
  local copies, waits for them, and re-layouts  3.88 us (3%)
    ppermute x6, starting transfers between devices, risen(): lax.ppermute(rows, column, [(i, (i + by) % levels) for i in range(levels)])  17.7 us
    all_to_all x1, starting transfers between devices, per_device(): lax.all_to_all(sent.reshape(chips, piece, lanes), space + ('chip',), 0, 0)  16.4 us
    all_to_all x1, starting transfers between devices, per_device(): lax.all_to_all(spread.reshape(chips, piece, lanes), space + ('chip',), 0, 0)  14.7 us
    pallas_call x1, Pallas kernels, refreshed(): pl.pallas_call(refresh_kernel, out_shape=(jax.ShapeDtypeStruct((fan, widt...  13 us
    ppermute x1, starting transfers between devices, per_device(): before = lax.ppermute(up, space, onward)  11.5 us
    ppermute x6, waiting for transfers between devices, risen(): lax.ppermute(rows, column, [(i, (i + by) % levels) for i in range(levels)])  10.5 us
    ppermute x1, starting transfers between devices, per_device(): after = lax.ppermute(down, space, back)  7.02 us
    ppermute x1, starting transfers between devices, per_device(): got = lax.ppermute(give, 'core', swap)  4.02 us
  transfers between devices with their start and end apart: 13, of which 4 were waited for; matrix products, arithmetic and copies ran while one was open for 0% of the time, Pallas kernels for 1%

profile of v6, /device:TPU:1, one launch (start us, length us, event | category | flops | bytes accessed | tf_op | source)
XLA Modules:
  0.0 116.2 jit_solution(10431687556065417288)
XLA Ops:
  0.6 0.0 copy-start.3
  0.6 0.7 copy-done.3
  1.4 0.0 copy-start.4
  1.4 0.7 copy-done.4
  2.1 11.5 %collective-permute-start = (bf16[1,4,16,256]{3,2,1,0:T(8,128)(2,1)S(1)}, bf16[1,4,16,256]{3,2,1,0:T(8,128)(2,1)S(1)}, u32[]{:S(2)}, u32[]{:S(2)}) collective-permute-start(bf16[1,4,16,256]{3,2,1,0:T(8,128)(2,1)S(1)} %get-tuple-element.31.up), channel_id=1, source_target_pairs={{0,8},{8,16},{16,24},{24,32},{32,40},{40,48},{48,56},{56,64},{64,7... | collective-permute-start | bytes 98312 | tf_op jit(solution)/shard_map/ppermute | solution.py:456
  13.6 7.0 %collective-permute-start.1 = (bf16[1,4,16,256]{3,2,1,0:T(8,128)(2,1)S(1)}, bf16[1,4,16,256]{3,2,1,0:T(8,128)(2,1)S(1)}, u32[]{:S(2)}, u32[]{:S(2)}) collective-permute-start(bf16[1,4,16,256]{3,2,1,0:T(8,128)(2,1)S(1)} %get-tuple-element.32.down), channel_id=1, source_target_pairs={{8,0},{16,8},{24,16},{32,24},{40,32},{48,40},{56,48},{64,56},{72,6... | collective-permute-start | bytes 98312 | tf_op jit(solution)/shard_map/ppermute | solution.py:457
  20.6 0.1 pad_add_fusion.place
  20.7 0.0 copy-start.1
  20.7 1.0 copy-done.1
  21.7 0.5 flip.1
  22.2 0.0 collective-permute-done.before
  22.2 0.3 collective-permute-done.1.after
  22.4 2.3 %conv.1 = (bf16[1,2,16,512]{3,2,1,0:T(8,128)(2,1)}, f32[1024,128]{1,0:T(8,128)S(1)}, bf16[1024,128]{1,0:T(8,128)(2,1)S(1)}, bf16[1,2,16,256]{3,2,1,0:T(8,128)(2,1)}) custom-call(s32[2]{0:T(128)S(1)} %pad_add_fusion.place, bf16[1,4,16,256]{3,2,1,0:T(8,128)(2,1)S(1)} %collective-permute-done.before, bf16[1,4,16,256]{3,2,1,0:T(8,128)(2,1)S(1)} %get-tuple-element.31.up, ...), custom_call_target="tpu_custom_call" | custom-call | tf_op jit(solution)/shard_map/conv/pallas_call | solution.py:323
  24.8 4.0 %collective-permute-start.2 = (bf16[1024,128]{1,0:T(8,128)(2,1)S(1)}, bf16[1024,128]{1,0:T(8,128)(2,1)S(1)}, u32[]{:S(2)}, u32[]{:S(2)}) collective-permute-start(bf16[1024,128]{1,0:T(8,128)(2,1)S(1)} %get-tuple-element.38), channel_id=1, source_target_pairs={{0,1},{1,0},{2,3},{3,2},{4,5},{5,4},{6,7},{7,6},{8,9},{9,8},{10,11... | collective-permute-start | bytes 786440 | tf_op jit(solution)/shard_map/ppermute | solution.py:464
  28.8 0.0 copy-start
  28.8 1.4 %copy-done = f32[216,1728]{1,0:T(8,128)S(1)} copy-done((f32[216,1728]{1,0:T(8,128)S(1)}, f32[216,1728]{1,0:T(8,128)}, u32[]{:S(2)}) %copy-start) | copy-done | bytes 1493016
  30.2 0.4 pack.1
  30.5 0.0 collective-permute-done.2.got
  30.5 0.7 add.7
  31.3 16.4 %all-to-all-start = ((bf16[256,4,128]{2,1,0:T(4,128)(2,1)}), bf16[256,4,128]{2,1,0:T(4,128)(2,1)S(1)}, u32[]{:S(2)}, u32[]{:S(2)}) async-start(bf16[256,4,128]{2,1,0:T(4,128)(2,1)} %bitcast.2), calls=%async_computation | async-start | bytes 524288 | tf_op jit(solution)/shard_map/all_to_all | solution.py:473
  47.7 2.8 %collective-permute-start.6 = (bf16[112,1792]{1,0:T(8,128)(2,1)S(1)}, bf16[112,1792]{1,0:T(8,128)(2,1)S(1)}, u32[]{:S(2)}, u32[]{:S(2)}) collective-permute-start(bf16[112,1792]{1,0:T(8,128)(2,1)S(1)} %get-tuple-element.48.refs_0_), channel_id=1, source_target_pairs={{0,14},{2,0},{4,2},{6,4},{8,6},{10,8},{12,10},{14,12},{1,15},{3,1}... | collective-permute-start | bytes 1204232 | tf_op jit(solution)/shard_map/ppermute | solution.py:470
  50.5 2.5 %collective-permute-start.4 = (bf16[112,1792]{1,0:T(8,128)(2,1)S(1)}, bf16[112,1792]{1,0:T(8,128)(2,1)S(1)}, u32[]{:S(2)}, u32[]{:S(2)}) collective-permute-start(bf16[112,1792]{1,0:T(8,128)(2,1)S(1)} %get-tuple-element.48.refs_0_), channel_id=1, source_target_pairs={{0,2},{2,4},{4,6},{6,8},{8,10},{10,12},{12,14},{14,0},{1,3},{3,5},... | collective-permute-start | bytes 1204232 | tf_op jit(solution)/shard_map/ppermute | solution.py:470
  53.0 4.0 %collective-permute-start.7 = (bf16[112,1792]{1,0:T(8,128)(2,1)S(1)}, bf16[112,1792]{1,0:T(8,128)(2,1)S(1)}, u32[]{:S(2)}, u32[]{:S(2)}) collective-permute-start(bf16[112,1792]{1,0:T(8,128)(2,1)S(1)} %get-tuple-element.49.refs_1_), channel_id=1, source_target_pairs={{0,14},{2,0},{4,2},{6,4},{8,6},{10,8},{12,10},{14,12},{1,15},{3,1}... | collective-permute-start | bytes 1204232 | tf_op jit(solution)/shard_map/ppermute | solution.py:470
  57.0 1.9 %collective-permute-start.5 = (bf16[112,1792]{1,0:T(8,128)(2,1)S(1)}, bf16[112,1792]{1,0:T(8,128)(2,1)S(1)}, u32[]{:S(2)}, u32[]{:S(2)}) collective-permute-start(bf16[112,1792]{1,0:T(8,128)(2,1)S(1)} %get-tuple-element.49.refs_1_), channel_id=1, source_target_pairs={{0,2},{2,4},{4,6},{6,8},{8,10},{10,12},{12,14},{14,0},{1,3},{3,5},... | collective-permute-start | bytes 1204232 | tf_op jit(solution)/shard_map/ppermute | solution.py:470
  58.9 2.8 %all-to-all-done = bf16[256,4,128]{2,1,0:T(4,128)(2,1)S(1)} async-done(((bf16[256,4,128]{2,1,0:T(4,128)(2,1)}), bf16[256,4,128]{2,1,0:T(4,128)(2,1)S(1)}, u32[]{:S(2)}, u32[]{:S(2)}) %all-to-all-start) | async-done | bytes 262176 | tf_op jit(solution)/shard_map/all_to_all | solution.py:473
  61.7 0.9 sum.1
  62.6 14.7 %all-to-all-start.1 = ((bf16[256,4,128]{2,1,0:T(4,128)(2,1)}), bf16[256,4,128]{2,1,0:T(4,128)(2,1)S(1)}, u32[]{:S(2)}, u32[]{:S(2)}) async-start(bf16[256,4,128]{2,1,0:T(4,128)(2,1)} %bitcast.4), calls=%async_computation.1 | async-start | bytes 524288 | tf_op jit(solution)/shard_map/all_to_all | solution.py:477
  77.3 0.0 collective-permute-done.6.refs_6_
  77.3 0.0 collective-permute-done.4.refs_2_
  77.3 0.0 collective-permute-done.7.refs_7_
  77.3 0.0 collective-permute-done.5.refs_3_
  77.3 1.9 %collective-permute-start.8 = (bf16[112,1792]{1,0:T(8,128)(2,1)S(1)}, bf16[112,1792]{1,0:T(8,128)(2,1)S(1)}, u32[]{:S(2)}, u32[]{:S(2)}) collective-permute-start(bf16[112,1792]{1,0:T(8,128)(2,1)S(1)} %collective-permute-done.4.refs_2_), channel_id=1, source_target_pairs={{0,2},{2,4},{4,6},{6,8},{8,10},{10,12},{12,14},{14,0},{1,3},{3,5},... | collective-permute-start | bytes 1204232 | tf_op jit(solution)/shard_map/ppermute | solution.py:470
  79.3 4.6 %collective-permute-start.9 = (bf16[112,1792]{1,0:T(8,128)(2,1)S(1)}, bf16[112,1792]{1,0:T(8,128)(2,1)S(1)}, u32[]{:S(2)}, u32[]{:S(2)}) collective-permute-start(bf16[112,1792]{1,0:T(8,128)(2,1)S(1)} %collective-permute-done.7.refs_7_), channel_id=1, source_target_pairs={{0,14},{2,0},{4,2},{6,4},{8,6},{10,8},{12,10},{14,12},{1,15},{3,1}... | collective-permute-start | bytes 1204232 | tf_op jit(solution)/shard_map/ppermute | solution.py:470
  83.8 10.5 %collective-permute-done.8.refs_4_ = bf16[112,1792]{1,0:T(8,128)(2,1)S(1)} collective-permute-done((bf16[112,1792]{1,0:T(8,128)(2,1)S(1)}, bf16[112,1792]{1,0:T(8,128)(2,1)S(1)}, u32[]{:S(2)}, u32[]{:S(2)}) %collective-permute-start.8) | collective-permute-done | bytes 401440 | tf_op jit(solution)/shard_map/ppermute | solution.py:470
  94.4 0.0 collective-permute-done.9.refs_5_
  94.4 0.0 all-to-all-done.1
  94.4 0.0 copy-start.2
  94.4 0.2 stack.13.left_mine
  94.6 2.9 %collective-permute-start.10 = (bf16[896,1792]{1,0:T(8,128)(2,1)S(1)}, bf16[896,1792]{1,0:T(8,128)(2,1)S(1)}, u32[]{:S(2)}, u32[]{:S(2)}) collective-permute-start(bf16[896,1792]{1,0:T(8,128)(2,1)S(1)} %stack.13.left_mine), channel_id=1, source_target_pairs={{0,1},{1,0},{2,3},{3,2},{4,5},{5,4},{6,7},{7,6},{8,9},{9,8},{10,11... | collective-permute-start | bytes 9633800 | tf_op jit(solution)/shard_map/ppermute | solution.py:484
  97.5 2.1 %collective-permute-start.3 = (bf16[1024,128]{1,0:T(8,128)(2,1)S(1)}, bf16[1024,128]{1,0:T(8,128)(2,1)S(1)}, u32[]{:S(2)}, u32[]{:S(2)}) collective-permute-start(bf16[1024,128]{1,0:T(8,128)(2,1)S(1)} %bitcast.6), channel_id=1, source_target_pairs={{0,1},{1,0},{2,3},{3,2},{4,5},{5,4},{6,7},{7,6},{8,9},{9,8},{10,11... | collective-permute-start | bytes 786440 | tf_op jit(solution)/shard_map/ppermute | solution.py:482
  99.6 3.6 %collective-permute-done.3.theirs = bf16[1024,128]{1,0:T(8,128)(2,1)S(1)} collective-permute-done((bf16[1024,128]{1,0:T(8,128)(2,1)S(1)}, bf16[1024,128]{1,0:T(8,128)(2,1)S(1)}, u32[]{:S(2)}, u32[]{:S(2)}) %collective-permute-start.3) | collective-permute-done | bytes 262176 | tf_op jit(solution)/shard_map/ppermute | solution.py:482
  103.2 0.0 collective-permute-done.10.left_theirs
  103.2 0.0 copy-done.2
  103.2 13.0 %refresh.1 = (f32[1728,128]{1,0:T(8,128)}, f32[216,128]{1,0:T(8,128)}) custom-call(s32[2]{0:T(128)S(1)} %pad_add_fusion.place, bf16[1024,128]{1,0:T(8,128)(2,1)S(1)} %bitcast.7, bf16[1024,128]{1,0:T(8,128)(2,1)S(1)} %collective-permute-done.3.theirs, bf16[896,1792]{1,0:T(8,128)(2,1)S(1)} %stack.13.left_mine, ...), custom_call_target="tpu_custom_call" | custom-call | tf_op jit(solution)/shard_map/refresh/pallas_call | solution.py:421
  (1 shorter events, 0.0 us)
Async XLA Ops:
  0.6 0.8 copy-start.3
  1.4 0.7 copy-start.4
  2.1 20.1 %collective-permute-start = (bf16[1,4,16,256]{3,2,1,0:T(8,128)(2,1)S(1)}, bf16[1,4,16,256]{3,2,1,0:T(8,128)(2,1)S(1)}, u32[]{:S(2)}, u32[]{:S(2)}) collective-permute-start(bf16[1,4,16,256]{3,2,1,0:T(8,128)(2,1)S(1)} %get-tuple-element.31.up), channel_id=1, source_target_pairs={{0,8},{8,16},{16,24},{24,32},{32,40},{40,48},{48,56},{56,64},{64,7... | collective-permute-start | bytes 98312 | tf_op jit(solution)/shard_map/ppermute | solution.py:456
  13.6 8.9 %collective-permute-start.1 = (bf16[1,4,16,256]{3,2,1,0:T(8,128)(2,1)S(1)}, bf16[1,4,16,256]{3,2,1,0:T(8,128)(2,1)S(1)}, u32[]{:S(2)}, u32[]{:S(2)}) collective-permute-start(bf16[1,4,16,256]{3,2,1,0:T(8,128)(2,1)S(1)} %get-tuple-element.32.down), channel_id=1, source_target_pairs={{8,0},{16,8},{24,16},{32,24},{40,32},{48,40},{56,48},{64,56},{72,6... | collective-permute-start | bytes 98312 | tf_op jit(solution)/shard_map/ppermute | solution.py:457
  20.7 1.0 copy-start.1
  24.8 5.8 %collective-permute-start.2 = (bf16[1024,128]{1,0:T(8,128)(2,1)S(1)}, bf16[1024,128]{1,0:T(8,128)(2,1)S(1)}, u32[]{:S(2)}, u32[]{:S(2)}) collective-permute-start(bf16[1024,128]{1,0:T(8,128)(2,1)S(1)} %get-tuple-element.38), channel_id=1, source_target_pairs={{0,1},{1,0},{2,3},{3,2},{4,5},{5,4},{6,7},{7,6},{8,9},{9,8},{10,11... | collective-permute-start | bytes 786440 | tf_op jit(solution)/shard_map/ppermute | solution.py:464
  28.8 1.4 %copy-start = (f32[216,1728]{1,0:T(8,128)S(1)}, f32[216,1728]{1,0:T(8,128)}, u32[]{:S(2)}) copy-start(f32[216,1728]{1,0:T(8,128)} %rows.1) | copy-start | bytes 4478980
  31.3 30.4 %all-to-all-start = ((bf16[256,4,128]{2,1,0:T(4,128)(2,1)}), bf16[256,4,128]{2,1,0:T(4,128)(2,1)S(1)}, u32[]{:S(2)}, u32[]{:S(2)}) async-start(bf16[256,4,128]{2,1,0:T(4,128)(2,1)} %bitcast.2), calls=%async_computation | async-start | bytes 524288 | tf_op jit(solution)/shard_map/all_to_all | solution.py:473
  47.7 29.6 %collective-permute-start.6 = (bf16[112,1792]{1,0:T(8,128)(2,1)S(1)}, bf16[112,1792]{1,0:T(8,128)(2,1)S(1)}, u32[]{:S(2)}, u32[]{:S(2)}) collective-permute-start(bf16[112,1792]{1,0:T(8,128)(2,1)S(1)} %get-tuple-element.48.refs_0_), channel_id=1, source_target_pairs={{0,14},{2,0},{4,2},{6,4},{8,6},{10,8},{12,10},{14,12},{1,15},{3,1}... | collective-permute-start | bytes 1204232 | tf_op jit(solution)/shard_map/ppermute | solution.py:470
  50.5 26.8 %collective-permute-start.4 = (bf16[112,1792]{1,0:T(8,128)(2,1)S(1)}, bf16[112,1792]{1,0:T(8,128)(2,1)S(1)}, u32[]{:S(2)}, u32[]{:S(2)}) collective-permute-start(bf16[112,1792]{1,0:T(8,128)(2,1)S(1)} %get-tuple-element.48.refs_0_), channel_id=1, source_target_pairs={{0,2},{2,4},{4,6},{6,8},{8,10},{10,12},{12,14},{14,0},{1,3},{3,5},... | collective-permute-start | bytes 1204232 | tf_op jit(solution)/shard_map/ppermute | solution.py:470
  53.0 24.4 %collective-permute-start.7 = (bf16[112,1792]{1,0:T(8,128)(2,1)S(1)}, bf16[112,1792]{1,0:T(8,128)(2,1)S(1)}, u32[]{:S(2)}, u32[]{:S(2)}) collective-permute-start(bf16[112,1792]{1,0:T(8,128)(2,1)S(1)} %get-tuple-element.49.refs_1_), channel_id=1, source_target_pairs={{0,14},{2,0},{4,2},{6,4},{8,6},{10,8},{12,10},{14,12},{1,15},{3,1}... | collective-permute-start | bytes 1204232 | tf_op jit(solution)/shard_map/ppermute | solution.py:470
  57.0 20.3 %collective-permute-start.5 = (bf16[112,1792]{1,0:T(8,128)(2,1)S(1)}, bf16[112,1792]{1,0:T(8,128)(2,1)S(1)}, u32[]{:S(2)}, u32[]{:S(2)}) collective-permute-start(bf16[112,1792]{1,0:T(8,128)(2,1)S(1)} %get-tuple-element.49.refs_1_), channel_id=1, source_target_pairs={{0,2},{2,4},{4,6},{6,8},{8,10},{10,12},{12,14},{14,0},{1,3},{3,5},... | collective-permute-start | bytes 1204232 | tf_op jit(solution)/shard_map/ppermute | solution.py:470
  62.6 31.8 %all-to-all-start.1 = ((bf16[256,4,128]{2,1,0:T(4,128)(2,1)}), bf16[256,4,128]{2,1,0:T(4,128)(2,1)S(1)}, u32[]{:S(2)}, u32[]{:S(2)}) async-start(bf16[256,4,128]{2,1,0:T(4,128)(2,1)} %bitcast.4), calls=%async_computation.1 | async-start | bytes 524288 | tf_op jit(solution)/shard_map/all_to_all | solution.py:477
  77.3 17.0 %collective-permute-start.8 = (bf16[112,1792]{1,0:T(8,128)(2,1)S(1)}, bf16[112,1792]{1,0:T(8,128)(2,1)S(1)}, u32[]{:S(2)}, u32[]{:S(2)}) collective-permute-start(bf16[112,1792]{1,0:T(8,128)(2,1)S(1)} %collective-permute-done.4.refs_2_), channel_id=1, source_target_pairs={{0,2},{2,4},{4,6},{6,8},{8,10},{10,12},{12,14},{14,0},{1,3},{3,5},... | collective-permute-start | bytes 1204232 | tf_op jit(solution)/shard_map/ppermute | solution.py:470
  79.3 15.1 %collective-permute-start.9 = (bf16[112,1792]{1,0:T(8,128)(2,1)S(1)}, bf16[112,1792]{1,0:T(8,128)(2,1)S(1)}, u32[]{:S(2)}, u32[]{:S(2)}) collective-permute-start(bf16[112,1792]{1,0:T(8,128)(2,1)S(1)} %collective-permute-done.7.refs_7_), channel_id=1, source_target_pairs={{0,14},{2,0},{4,2},{6,4},{8,6},{10,8},{12,10},{14,12},{1,15},{3,1}... | collective-permute-start | bytes 1204232 | tf_op jit(solution)/shard_map/ppermute | solution.py:470
  94.4 8.8 %copy-start.2 = (f32[128,128]{1,0:T(8,128)S(1)}, f32[128,128]{1,0:T(8,128)}, u32[]{:S(2)}) copy-start(f32[128,128]{1,0:T(8,128)} %right_stat.1) | copy-start | bytes 196612
  94.6 8.6 %collective-permute-start.10 = (bf16[896,1792]{1,0:T(8,128)(2,1)S(1)}, bf16[896,1792]{1,0:T(8,128)(2,1)S(1)}, u32[]{:S(2)}, u32[]{:S(2)}) collective-permute-start(bf16[896,1792]{1,0:T(8,128)(2,1)S(1)} %stack.13.left_mine), channel_id=1, source_target_pairs={{0,1},{1,0},{2,3},{3,2},{4,5},{5,4},{6,7},{7,6},{8,9},{9,8},{10,11... | collective-permute-start | bytes 9633800 | tf_op jit(solution)/shard_map/ppermute | solution.py:484
  97.5 5.7 %collective-permute-start.3 = (bf16[1024,128]{1,0:T(8,128)(2,1)S(1)}, bf16[1024,128]{1,0:T(8,128)(2,1)S(1)}, u32[]{:S(2)}, u32[]{:S(2)}) collective-permute-start(bf16[1024,128]{1,0:T(8,128)(2,1)S(1)} %bitcast.6), channel_id=1, source_target_pairs={{0,1},{1,0},{2,3},{3,2},{4,5},{5,4},{6,7},{7,6},{8,9},{9,8},{10,11... | collective-permute-start | bytes 786440 | tf_op jit(solution)/shard_map/ppermute | solution.py:482
